TPU v7x, 32 devices: a whole 2x2x4 slice. The times are simulated.
32 devices in a mesh: seq: 2 (over x), shard: 16 (over z, y, core).
Axes of the slice: x: 2, y: 2, z: 4, core: 2. Of those that a mesh axis runs over, the one named last changes fastest.
Arguments:
- features: bfloat16 [32, 768, 512], P('shard', 'seq'), may hold values from -6 to 6
- time_mask: int32 [32, 768], P('shard', 'seq'), may hold values from 0 to 1, as said below
- negatives: int32 [32, 768, 100], P('shard', 'seq'), may hold values from 0 to 767, as said below
- target_codes: int32 [32, 768, 2], P('shard', 'seq'), may hold values from 0 to 319
- feature_weight: float32 [512, 768], P('shard'), may hold values from -0.25 to 0.25
- feature_first: float32 [512, 768], P('shard')
- feature_second: float32 [512, 768], P('shard')
- conv_weight: float32 [6144, 768], P('shard'), may hold values from -0.15625 to 0.15625
- conv_first: float32 [6144, 768], P('shard')
- conv_second: float32 [6144, 768], P('shard')
- attention_weight: float32 [8, 768, 768], P(None, 'shard')
- attention_first: float32 [8, 768, 768], P(None, 'shard')
- attention_second: float32 [8, 768, 768], P(None, 'shard')
- left_basis_t: float32 [8, 768, 768], P(None, 'shard'), may hold values from -1 to 1, as said below
- right_orthogonal_basis: float32 [8, 768, 768], replicated, may hold values from -1 to 1
- expand_weight: float32 [2, 768, 3072], P(None, 'shard'), may hold values from -0.21875 to 0.21875
- expand_first: float32 [2, 768, 3072], P(None, 'shard')
- expand_second: float32 [2, 768, 3072], P(None, 'shard')
- shrink_weight: float32 [2, 3072, 768], P(None, 'shard'), may hold values from -0.109375 to 0.109375
- shrink_first: float32 [2, 3072, 768], P(None, 'shard')
- shrink_second: float32 [2, 3072, 768], P(None, 'shard')
- final_weight: float32 [768, 256], P('shard'), may hold values from -0.21875 to 0.21875
- final_first: float32 [768, 256], P('shard')
- final_second: float32 [768, 256], P('shard')
- target_weight: float32 [256, 256], P('shard'), may hold values from -0.375 to 0.375
- target_first: float32 [256, 256], P('shard')
- target_second: float32 [256, 256], P('shard')
- codebook_weight: float32 [256, 320], P('shard'), may hold values from -6 to 6
- codebook_first: float32 [256, 320], P('shard')
- codebook_second: float32 [256, 320], P('shard')
- vector_params: float32 [23808], P('shard')
- vector_first: float32 [23808], P('shard')
- vector_second: float32 [23808], P('shard')
Outputs:
- loss_total: float32 [2], replicated
- new_feature_weight: float32 [512, 768], P('shard')
- new_feature_first: float32 [512, 768], P('shard')
- new_feature_second: float32 [512, 768], P('shard')
- new_conv_weight: float32 [6144, 768], P('shard')
- new_conv_first: float32 [6144, 768], P('shard')
- new_conv_second: float32 [6144, 768], P('shard')
- new_attention_weight: float32 [8, 768, 768], P(None, 'shard')
- new_attention_first: float32 [8, 768, 768], P(None, 'shard')
- new_attention_second: float32 [8, 768, 768], P(None, 'shard')
- new_expand_weight: float32 [2, 768, 3072], P(None, 'shard')
- new_expand_first: float32 [2, 768, 3072], P(None, 'shard')
- new_expand_second: float32 [2, 768, 3072], P(None, 'shard')
- new_shrink_weight: float32 [2, 3072, 768], P(None, 'shard')
- new_shrink_first: float32 [2, 3072, 768], P(None, 'shard')
- new_shrink_second: float32 [2, 3072, 768], P(None, 'shard')
- new_final_weight: float32 [768, 256], P('shard')
- new_final_first: float32 [768, 256], P('shard')
- new_final_second: float32 [768, 256], P('shard')
- new_target_weight: float32 [256, 256], P('shard')
- new_target_first: float32 [256, 256], P('shard')
- new_target_second: float32 [256, 256], P('shard')
- new_codebook_weight: float32 [256, 320], P('shard')
- new_codebook_first: float32 [256, 320], P('shard')
- new_codebook_second: float32 [256, 320], P('shard')
- new_vector_params: float32 [23808], P('shard')
- new_vector_first: float32 [23808], P('shard')
- new_vector_second: float32 [23808], P('shard')
Inputs may be any that keep to these rules, and one draw needn't show every extreme that they name: `time_mask`: masked frames come in runs of 10 that start at random; runs start more often late in a clip and in later clips. `negatives`: frame indices within the same clip, never the frame itself. `left_basis_t`: each matrix is orthogonal.
All inputs are finite; a program needn't handle non-finite values.
Results may differ from a plain program's by a relative error of at most 0.018.
Values may be sent and summed in bfloat16 or wider, within the bound.
A program may use at most 512 MiB of HBM per device.

v0:
```python
import jax
import jax.numpy as jnp
from jax import lax
from jax.sharding import PartitionSpec as P

D = 768
HEADS = 12
HDIM = 64
FF = 3072
CIN = 512
KW = 128
GROUPS = 16
PROJ = 256
CODES = 320
QGROUPS = 2
NEG = 100
LAYERS = 2
STEP = 10


beta_one = 0.9
beta_two = 0.95
beta_rotated = 0.5
adam_epsilon = 1e-08
decay_rate = 0.01
rate_matrix = 0.02
rate_target = 0.08
rate_codebook = 0.6
rate_vector = 0.3
rate_rotated = 0.08
contrastive_sharpness = 0.1
norm_epsilon = 1e-05
unit_epsilon = 1e-06
maximum_score = lax.Precision.HIGHEST


def padded_2(block, sides, width):
    for axis, dim in sides:
        count = lax.axis_size(axis)
        forward = [(i, i + 1) for i in range(count - 1)]
        backward = [(target, source) for source, target in forward]
        low = lax.ppermute(
            lax.slice_in_dim(block, block.shape[dim] - width, None, axis=dim), axis, forward
        )
        high = lax.ppermute(lax.slice_in_dim(block, 0, width, axis=dim), axis, backward)
        block = jnp.concatenate([low, block, high], axis=dim)
    return block


def lowered(values):
    return values.astype(jnp.bfloat16)


def bdot(left_side, right_side):
    return jnp.dot(left_side, right_side, preferred_element_type=jnp.float32)


def fdot(left_side, right_side):
    return jnp.dot(
        left_side, right_side, precision=maximum_score, preferred_element_type=jnp.float32
    )


def column_sum(values):
    return jnp.sum(values.astype(jnp.float32), 0)


def gelu_exact(values):
    return jax.nn.gelu(values, approximate=False)


def layer_norm(values, gain_row, bias_row):
    centred = values - jnp.mean(values, -1, keepdims=True)
    spread = jnp.mean(centred * centred, -1, keepdims=True)
    return centred * lax.rsqrt(spread + norm_epsilon) * gain_row + bias_row


def unit_rows(values):
    return values * lax.rsqrt(jnp.sum(values * values, -1, keepdims=True) + unit_epsilon)


def vector_pieces(vector):
    widths = [CIN, CIN, D, D, D, D, D] + [D, D, D, D, D, FF, D, D, D] * LAYERS + [PROJ, PROJ]
    pieces = []
    offset = 0
    for width in widths:
        pieces.append(vector[offset : offset + width])
        offset = offset + width
    return pieces


def conv_windows(padded_clip, frame_count, flipped):
    if flipped:
        window_index = jnp.arange(frame_count)[:, None] + KW - jnp.arange(KW)[None, :]
    else:
        window_index = jnp.arange(frame_count)[:, None] + jnp.arange(KW)[None, :]
    return padded_clip[window_index].reshape(frame_count, KW, GROUPS, D // GROUPS)


def frames_to_items(values, clip_count, frame_count):
    stack_count = values.shape[0]
    shaped = values.reshape(stack_count, clip_count, frame_count, HEADS, HDIM).transpose(
        0, 1, 3, 2, 4
    )
    return shaped.reshape(stack_count, clip_count * HEADS, frame_count, HDIM)


def items_to_frames(values, clip_count, frame_count):
    stack_count = values.shape[0]
    shaped = values.reshape(stack_count, clip_count, HEADS, frame_count, HDIM).transpose(
        0, 1, 3, 2, 4
    )
    return shaped.reshape(stack_count, clip_count * frame_count, D)


def attend_items(block):
    moved = jnp.moveaxis(block[:, 0], 1, 0)

    def one_item(stacked):
        scores = bdot(stacked[0], stacked[1].T) * HDIM ** (-0.5)
        largest = jnp.max(scores, -1, keepdims=True)
        power_value = jnp.exp(scores - largest)
        running_totals = jnp.sum(power_value, -1, keepdims=True)
        output = bdot(lowered(power_value / running_totals), stacked[2])
        return (lowered(output), (largest + jnp.log(running_totals))[:, 0])

    output, logsum = lax.map(one_item, moved)
    return (output, logsum, moved)


def attend_back(inputs):
    stacked, logsum, grad_output = inputs
    scale_factor = HDIM ** (-0.5)
    scores = bdot(stacked[0], stacked[1].T) * scale_factor
    probs = jnp.exp(scores - logsum[:, None])
    grad_values = bdot(lowered(probs).T, grad_output)
    grad_probs = bdot(grad_output, stacked[2].T)
    grad_scores = lowered(probs * (grad_probs - jnp.sum(probs * grad_probs, -1, keepdims=True)))
    grad_query = bdot(grad_scores, stacked[1]) * scale_factor
    grad_keys = bdot(grad_scores.T, stacked[0]) * scale_factor
    return lowered(jnp.stack([grad_query, grad_keys, grad_values]))


def layer_forward(hidden, attn_w, expand_w, shrink_w, pieces, clip_count, frame_count):
    q_bias, v_bias, o_bias, gain_one, bias_one, expand_bias, shrink_bias, gain_two, bias_two = (
        pieces
    )
    seq_count = lax.axis_size("seq")
    entry = lowered(hidden)
    query = bdot(entry, attn_w[0]) + q_bias
    key_rows = bdot(entry, attn_w[1])
    value_rows = bdot(entry, attn_w[2]) + v_bias
    heads_in = frames_to_items(
        lowered(jnp.stack([query, key_rows, value_rows])), clip_count, frame_count
    )
    heads_in = heads_in.reshape(3, seq_count, clip_count * HEADS // seq_count, frame_count, HDIM)
    output, logsum, kept = attend_items(
        lax.all_to_all(heads_in, "seq", split_axis=1, concat_axis=3, tiled=True)
    )
    returned = lax.all_to_all(output, "seq", split_axis=1, concat_axis=0, tiled=True)
    mixed = items_to_frames(returned[None], clip_count, frame_count)[0]
    branch = bdot(mixed, attn_w[3]) + o_bias
    middle, middle_pull = jax.vjp(layer_norm, hidden + branch, gain_one, bias_one)
    middle_low = lowered(middle)
    inner = bdot(middle_low, expand_w) + expand_bias
    activated, gelu_pull = jax.vjp(gelu_exact, inner)
    active_low = lowered(activated)
    outer = bdot(active_low, shrink_w) + shrink_bias
    result, final_pull = jax.vjp(layer_norm, middle + outer, gain_two, bias_two)
    return (
        result,
        (entry, kept, logsum, mixed, middle_pull, middle_low, gelu_pull, active_low, final_pull),
    )


def layer_backward(grad_out, cache, attn_w, expand_w, shrink_w, clip_count, frame_count):
    entry, kept, logsum, mixed, middle_pull, middle_low, gelu_pull, active_low, final_pull = cache
    grad_sum_two, grad_gain_two, grad_bias_two = final_pull(grad_out)
    grad_outer = lowered(grad_sum_two)
    grad_shrink = bdot(active_low.T, grad_outer)
    (grad_inner,) = gelu_pull(bdot(grad_outer, shrink_w.T))
    grad_inner = lowered(grad_inner)
    grad_expand = bdot(middle_low.T, grad_inner)
    grad_middle = grad_sum_two + bdot(grad_inner, expand_w.T)
    grad_sum_one, grad_gain_one, grad_bias_one = middle_pull(grad_middle)
    grad_branch = lowered(grad_sum_one)
    grad_out_proj = bdot(mixed.T, grad_branch)
    grad_mixed = lowered(bdot(grad_branch, attn_w[3].T))
    grad_items = frames_to_items(grad_mixed[None], clip_count, frame_count)[0]
    arrived = lax.all_to_all(grad_items, "seq", split_axis=0, concat_axis=1, tiled=True)
    item_grads = lax.map(attend_back, (kept, logsum, arrived))
    returned = lax.all_to_all(
        jnp.moveaxis(item_grads, 1, 0), "seq", split_axis=2, concat_axis=1, tiled=True
    )
    grad_rows = items_to_frames(returned, clip_count, frame_count)
    grad_entry = (
        bdot(grad_rows[0], attn_w[0].T)
        + bdot(grad_rows[1], attn_w[1].T)
        + bdot(grad_rows[2], attn_w[2].T)
    )
    grad_attn = jnp.stack(
        [
            bdot(entry.T, grad_rows[0]),
            bdot(entry.T, grad_rows[1]),
            bdot(entry.T, grad_rows[2]),
            grad_out_proj,
        ]
    )
    grad_pieces = [
        column_sum(grad_rows[0]),
        column_sum(grad_rows[2]),
        column_sum(grad_branch),
        grad_gain_one,
        grad_bias_one,
        column_sum(grad_inner),
        column_sum(grad_outer),
        grad_gain_two,
        grad_bias_two,
    ]
    return (grad_sum_one + grad_entry, grad_attn, grad_expand, grad_shrink, grad_pieces)


def target_vectors(codes, code_w, target_w, target_bias):
    width = PROJ // QGROUPS
    chosen = []
    for group in range(QGROUPS):
        onehot = (codes[:, group][:, None] == jnp.arange(CODES)[None, :]).astype(jnp.bfloat16)
        chosen.append(bdot(onehot, code_w[group * width : (group + 1) * width].T))
    code_rows = jnp.concatenate(chosen, 1)
    raw_targets = fdot(code_rows, target_w.astype(jnp.float32)) + target_bias
    targets, target_pull = jax.vjp(unit_rows, raw_targets)
    return (targets, target_pull, code_rows)


def code_grads(codes, code_rows, grad_raw, target_w):
    width = PROJ // QGROUPS
    grad_target_w = fdot(code_rows.T, grad_raw)
    grad_code_rows = fdot(grad_raw, target_w.astype(jnp.float32).T)
    blocks = []
    for group in range(QGROUPS):
        onehot = (codes[:, group][:, None] == jnp.arange(CODES)[None, :]).astype(jnp.float32)
        blocks.append(fdot(grad_code_rows[:, group * width : (group + 1) * width].T, onehot))
    return (grad_target_w, jnp.concatenate(blocks, 0), column_sum(grad_raw))


def adam_update(weight, grad, first, second, rate, decay):
    first = beta_one * first + (1 - beta_one) * grad
    second = beta_two * second + (1 - beta_two) * grad * grad
    share_fraction = (
        first / (1 - beta_one**STEP) / (jnp.sqrt(second / (1 - beta_two**STEP)) + adam_epsilon)
    )
    return (weight - rate * (share_fraction + decay * weight), first, second)


def on_device(
    features,
    time_mask,
    negatives,
    target_codes,
    feature_weight,
    feature_first,
    feature_second,
    conv_weight,
    conv_first,
    conv_second,
    attention_weight,
    attention_first,
    attention_second,
    left_basis_t,
    right_orthogonal_basis,
    expand_weight,
    expand_first,
    expand_second,
    shrink_weight,
    shrink_first,
    shrink_second,
    final_weight,
    final_first,
    final_second,
    target_weight,
    target_first,
    target_second,
    codebook_weight,
    codebook_first,
    codebook_second,
    vector_params,
    vector_first,
    vector_second,
):
    clip_count, frame_count = (features.shape[0], features.shape[1])
    row_count = clip_count * frame_count
    seq_count = lax.axis_size("seq")
    shard_count = lax.axis_size("shard")
    clip_frames = frame_count * seq_count
    gathered = (
        lax.all_gather(lowered(feature_weight), "shard", axis=0, tiled=True),
        lax.all_gather(lowered(conv_weight), "shard", axis=0, tiled=True),
        lax.all_gather(lowered(attention_weight), "shard", axis=1, tiled=True),
        lax.all_gather(lowered(expand_weight), "shard", axis=1, tiled=True),
        lax.all_gather(lowered(shrink_weight), "shard", axis=1, tiled=True),
        lax.all_gather(lowered(final_weight), "shard", axis=0, tiled=True),
        lax.all_gather(lowered(target_weight), "shard", axis=0, tiled=True),
        lax.all_gather(lowered(codebook_weight), "shard", axis=0, tiled=True),
        lax.all_gather(lowered(vector_params), "shard", axis=0, tiled=True),
    )
    feat_w, conv_w, attn_w, expand_w, shrink_w, final_w, target_w, code_w, vector_low = gathered
    pieces = vector_pieces(vector_low.astype(jnp.float32))
    mask_on = (time_mask > 0).reshape(row_count, 1)
    feats = features.reshape(row_count, CIN).astype(jnp.float32)
    normed, norm_pull = jax.vjp(layer_norm, feats, pieces[0], pieces[1])
    normed_low = lowered(normed)
    projected = bdot(normed_low, feat_w) + pieces[2]
    masked = jnp.where(mask_on, pieces[3][None, :], projected)
    padded = padded_2(lowered(masked).reshape(clip_count, frame_count, D), (("seq", 1),), KW // 2)
    kernel = conv_w.reshape(KW, D // GROUPS, GROUPS, D // GROUPS)

    def conv_clip(padded_clip):
        window = conv_windows(padded_clip, frame_count, False)
        return jnp.einsum("tkgc,kcgo->tgo", window, kernel, preferred_element_type=jnp.float32)

    conv_out = lax.map(conv_clip, padded).reshape(row_count, D) + pieces[4]
    hidden, front_pull = jax.vjp(
        lambda base, conv_in, gain_row, bias_row: layer_norm(
            base + gelu_exact(conv_in), gain_row, bias_row
        ),
        masked,
        conv_out,
        pieces[5],
        pieces[6],
    )
    caches = []
    for layer in range(LAYERS):
        hidden, cache = layer_forward(
            hidden,
            attn_w[4 * layer : 4 * layer + 4],
            expand_w[layer],
            shrink_w[layer],
            pieces[7 + 9 * layer : 16 + 9 * layer],
            clip_count,
            frame_count,
        )
        caches.append(cache)
    top_low = lowered(hidden)
    context, context_pull = jax.vjp(unit_rows, bdot(top_low, final_w) + pieces[-2])
    context_low = lowered(context).reshape(clip_count, frame_count, PROJ)
    code_ids = target_codes.reshape(row_count, QGROUPS)
    targets, target_pull, code_rows = target_vectors(code_ids, code_w, target_w, pieces[-1])
    all_targets = lax.all_gather(
        lowered(targets).reshape(clip_count, frame_count, PROJ), "seq", axis=1, tiled=True
    )
    angular_agreement = jnp.einsum(
        "cfp,clp->cfl", context_low, all_targets, preferred_element_type=jnp.float32
    )
    positions = lax.axis_index("seq") * frame_count + jnp.arange(frame_count)
    own_place = jnp.broadcast_to(positions[None, :, None], (clip_count, frame_count, 1))
    contrast_choice_embeddings = jnp.concatenate([own_place, negatives], 2)
    score_logits = (
        jnp.take_along_axis(angular_agreement, contrast_choice_embeddings, axis=2)
        / contrastive_sharpness
    )
    largest = jnp.max(score_logits, -1, keepdims=True)
    power_value = jnp.exp(score_logits - largest)
    running_totals = jnp.sum(power_value, -1, keepdims=True)
    mask_as_floats = time_mask.astype(jnp.float32)
    row_loss = largest[..., 0] + jnp.log(running_totals[..., 0]) - score_logits[..., 0]
    loss_sum = jnp.sum(mask_as_floats * row_loss)
    mask_count = jnp.sum(mask_as_floats)
    derivative_multiplier = 1.0 / (clip_count * shard_count * clip_frames)
    leading_position = (jnp.arange(NEG + 1) == 0).astype(jnp.float32)
    grad_logits = (
        mask_as_floats[..., None]
        * (power_value / running_totals - leading_position)
        * (derivative_multiplier / contrastive_sharpness)
    )

    def scatter_row(indices, values):
        return jnp.zeros((clip_frames,), jnp.float32).at[indices].add(values)

    grad_similar = lowered(jax.vmap(jax.vmap(scatter_row))(contrast_choice_embeddings, grad_logits))
    grad_context = jnp.einsum(
        "cfl,clp->cfp", grad_similar, all_targets, preferred_element_type=jnp.float32
    )
    grad_targets = jnp.einsum(
        "cfl,cfp->clp", grad_similar, context_low, preferred_element_type=jnp.float32
    )
    grad_targets = lax.psum_scatter(
        grad_targets.astype(jnp.bfloat16), "seq", scatter_dimension=1, tiled=True
    ).astype(jnp.float32)
    (grad_raw,) = target_pull(grad_targets.reshape(-1, PROJ))
    grad_target_w, grad_codebook, grad_target_bias = code_grads(
        code_ids, code_rows, grad_raw, target_w
    )
    (grad_context_raw,) = context_pull(grad_context.reshape(row_count, PROJ))
    grad_context_low = lowered(grad_context_raw)
    grad_final_w = bdot(top_low.T, grad_context_low)
    grad_final_bias = column_sum(grad_context_low)
    grad_hidden = bdot(grad_context_low, final_w.T)
    attn_grads = [None] * LAYERS
    expand_grads = [None] * LAYERS
    shrink_grads = [None] * LAYERS
    layer_pieces = [None] * LAYERS
    for layer in reversed(range(LAYERS)):
        (
            grad_hidden,
            attn_grads[layer],
            expand_grads[layer],
            shrink_grads[layer],
            layer_pieces[layer],
        ) = layer_backward(
            grad_hidden,
            caches[layer],
            attn_w[4 * layer : 4 * layer + 4],
            expand_w[layer],
            shrink_w[layer],
            clip_count,
            frame_count,
        )
    grad_masked, grad_conv, grad_gain_enc, grad_bias_enc = front_pull(grad_hidden)
    grad_conv_low = lowered(grad_conv).reshape(clip_count, frame_count, D)
    grad_padded = padded_2(grad_conv_low, (("seq", 1),), KW // 2)

    def conv_back(carry, inputs):
        padded_clip, grad_clip, grad_pad_clip = inputs
        window = conv_windows(padded_clip, frame_count, False)
        grad_window = conv_windows(grad_pad_clip, frame_count, True)
        grad_input = jnp.einsum(
            "tkgo,kcgo->tgc", grad_window, kernel, preferred_element_type=jnp.float32
        )
        grad_grouped = grad_clip.reshape(frame_count, GROUPS, D // GROUPS)
        carry = carry + jnp.einsum(
            "tkgc,tgo->kcgo", window, grad_grouped, preferred_element_type=jnp.float32
        )
        return (carry, grad_input.reshape(frame_count, D))

    kernel_zero = jnp.zeros((KW, D // GROUPS, GROUPS, D // GROUPS), jnp.float32)
    grad_kernel, grad_sent = lax.scan(conv_back, kernel_zero, (padded, grad_conv_low, grad_padded))
    grad_masked = grad_masked + grad_sent.reshape(row_count, D)
    grad_embedding = jnp.sum(jnp.where(mask_on, grad_masked, 0.0), 0)
    grad_projected = lowered(jnp.where(mask_on, 0.0, grad_masked))
    grad_feat_w = bdot(normed_low.T, grad_projected)
    _, grad_gain_feat, grad_bias_feat = norm_pull(bdot(grad_projected, feat_w.T))
    vector_grads = [
        grad_gain_feat,
        grad_bias_feat,
        column_sum(grad_projected),
        grad_embedding,
        column_sum(grad_conv_low.reshape(row_count, D)),
        grad_gain_enc,
        grad_bias_enc,
    ]
    for layer in range(LAYERS):
        vector_grads = vector_grads + layer_pieces[layer]
    vector_grads = vector_grads + [grad_final_bias, grad_target_bias]
    loss_tile = jnp.tile(jnp.stack([loss_sum, mask_count]), shard_count)
    owned = (
        lax.psum_scatter(
            grad_feat_w.astype(jnp.bfloat16), "shard", scatter_dimension=0, tiled=True
        ).astype(jnp.float32),
        lax.psum_scatter(
            grad_kernel.reshape(KW * (D // GROUPS), D).astype(jnp.bfloat16),
            "shard",
            scatter_dimension=0,
            tiled=True,
        ).astype(jnp.float32),
        lax.psum_scatter(
            jnp.concatenate(attn_grads, 0).astype(jnp.bfloat16),
            "shard",
            scatter_dimension=1,
            tiled=True,
        ).astype(jnp.float32),
        lax.psum_scatter(
            jnp.stack(expand_grads).astype(jnp.bfloat16), "shard", scatter_dimension=1, tiled=True
        ).astype(jnp.float32),
        lax.psum_scatter(
            jnp.stack(shrink_grads).astype(jnp.bfloat16), "shard", scatter_dimension=1, tiled=True
        ).astype(jnp.float32),
        lax.psum_scatter(
            grad_final_w.astype(jnp.bfloat16), "shard", scatter_dimension=0, tiled=True
        ).astype(jnp.float32),
        lax.psum_scatter(
            grad_target_w.astype(jnp.bfloat16), "shard", scatter_dimension=0, tiled=True
        ).astype(jnp.float32),
        lax.psum_scatter(
            grad_codebook.astype(jnp.bfloat16), "shard", scatter_dimension=0, tiled=True
        ).astype(jnp.float32),
        lax.psum_scatter(
            jnp.concatenate(vector_grads).astype(jnp.bfloat16),
            "shard",
            scatter_dimension=0,
            tiled=True,
        ).astype(jnp.float32),
        lax.psum_scatter(
            loss_tile.astype(jnp.bfloat16), "shard", scatter_dimension=0, tiled=True
        ).astype(jnp.float32),
    )
    (
        sum_feat,
        sum_conv,
        sum_attn,
        sum_expand,
        sum_shrink,
        sum_final,
        sum_target,
        sum_code,
        sum_vector,
        sum_loss,
    ) = owned
    summed = (
        lax.psum(sum_feat.astype(jnp.bfloat16), "seq").astype(jnp.float32),
        lax.psum(sum_conv.astype(jnp.bfloat16), "seq").astype(jnp.float32),
        lax.psum(sum_attn.astype(jnp.bfloat16), "seq").astype(jnp.float32),
        lax.psum(sum_expand.astype(jnp.bfloat16), "seq").astype(jnp.float32),
        lax.psum(sum_shrink.astype(jnp.bfloat16), "seq").astype(jnp.float32),
        lax.psum(sum_final.astype(jnp.bfloat16), "seq").astype(jnp.float32),
        lax.psum(sum_target.astype(jnp.bfloat16), "seq").astype(jnp.float32),
        lax.psum(sum_code.astype(jnp.bfloat16), "seq").astype(jnp.float32),
        lax.psum(sum_vector.astype(jnp.bfloat16), "seq").astype(jnp.float32),
        lax.psum(sum_loss.astype(jnp.bfloat16), "seq").astype(jnp.float32),
    )
    (
        sum_feat,
        sum_conv,
        sum_attn,
        sum_expand,
        sum_shrink,
        sum_final,
        sum_target,
        sum_code,
        sum_vector,
        sum_loss,
    ) = summed
    attn_whole = lax.all_gather(sum_attn.astype(jnp.bfloat16), "shard", axis=1, tiled=True).astype(
        sum_attn.dtype
    )
    rotated_gradient = jnp.einsum("mrd,mde->mre", left_basis_t, attn_whole, precision=maximum_score)
    rotated_gradient = jnp.einsum(
        "zih,zhy->ziy", rotated_gradient, right_orthogonal_basis, precision=maximum_score
    )
    rot_first = beta_rotated * attention_first + (1 - beta_rotated) * rotated_gradient
    rot_second = (
        beta_rotated * attention_second + (1 - beta_rotated) * rotated_gradient * rotated_gradient
    )
    share_fraction = (
        rot_first
        / (1 - beta_rotated**STEP)
        / (jnp.sqrt(rot_second / (1 - beta_rotated**STEP)) + adam_epsilon)
    )
    halved_pullback = jnp.einsum(
        "vpu,vcu->vpc", share_fraction, right_orthogonal_basis, precision=maximum_score
    )
    update = lax.psum_scatter(
        jnp.einsum("mrs,mre->sme", left_basis_t, halved_pullback, precision=maximum_score).astype(
            jnp.bfloat16
        ),
        "shard",
        scatter_dimension=0,
        tiled=True,
    ).astype(jnp.float32)
    new_attention = attention_weight - rate_rotated * jnp.transpose(update, (1, 0, 2))
    feature_new = adam_update(
        feature_weight, sum_feat, feature_first, feature_second, rate_matrix, decay_rate
    )
    conv_new = adam_update(conv_weight, sum_conv, conv_first, conv_second, rate_matrix, decay_rate)
    expand_new = adam_update(
        expand_weight, sum_expand, expand_first, expand_second, rate_matrix, decay_rate
    )
    shrink_new = adam_update(
        shrink_weight, sum_shrink, shrink_first, shrink_second, rate_matrix, decay_rate
    )
    final_new = adam_update(
        final_weight, sum_final, final_first, final_second, rate_matrix, decay_rate
    )
    target_new = adam_update(
        target_weight, sum_target, target_first, target_second, rate_target, decay_rate
    )
    codebook_new = adam_update(
        codebook_weight, sum_code, codebook_first, codebook_second, rate_codebook, decay_rate
    )
    vector_new = adam_update(
        vector_params, sum_vector, vector_first, vector_second, rate_vector, 0.0
    )
    return (
        sum_loss,
        feature_new[0],
        feature_new[1],
        feature_new[2],
        conv_new[0],
        conv_new[1],
        conv_new[2],
        new_attention,
        rot_first,
        rot_second,
        expand_new[0],
        expand_new[1],
        expand_new[2],
        shrink_new[0],
        shrink_new[1],
        shrink_new[2],
        final_new[0],
        final_new[1],
        final_new[2],
        target_new[0],
        target_new[1],
        target_new[2],
        codebook_new[0],
        codebook_new[1],
        codebook_new[2],
        vector_new[0],
        vector_new[1],
        vector_new[2],
    )


def solution(mesh):
    return jax.shard_map(
        on_device,
        mesh=mesh,
        in_specs=(
            P("shard", "seq", None),
            P("shard", "seq"),
            P("shard", "seq", None),
            P("shard", "seq", None),
            P("shard", None),
            P("shard", None),
            P("shard", None),
            P("shard", None),
            P("shard", None),
            P("shard", None),
            P(None, "shard", None),
            P(None, "shard", None),
            P(None, "shard", None),
            P(None, "shard", None),
            P(),
            P(None, "shard", None),
            P(None, "shard", None),
            P(None, "shard", None),
            P(None, "shard", None),
            P(None, "shard", None),
            P(None, "shard", None),
            P("shard", None),
            P("shard", None),
            P("shard", None),
            P("shard", None),
            P("shard", None),
            P("shard", None),
            P("shard", None),
            P("shard", None),
            P("shard", None),
            P("shard"),
            P("shard"),
            P("shard"),
        ),
        out_specs=(
            P(),
            P("shard", None),
            P("shard", None),
            P("shard", None),
            P("shard", None),
            P("shard", None),
            P("shard", None),
            P(None, "shard", None),
            P(None, "shard", None),
            P(None, "shard", None),
            P(None, "shard", None),
            P(None, "shard", None),
            P(None, "shard", None),
            P(None, "shard", None),
            P(None, "shard", None),
            P(None, "shard", None),
            P("shard", None),
            P("shard", None),
            P("shard", None),
            P("shard", None),
            P("shard", None),
            P("shard", None),
            P("shard", None),
            P("shard", None),
            P("shard", None),
            P("shard"),
            P("shard"),
            P("shard"),
        ),
        check_vma=False,
    )
```

profile of v0, /device:TPU:0, one launch (start us, length us, event | category | flops | bytes accessed | tf_op | source)
XLA Modules:
  0.0 5953.2 jit_solution(16318397926848952933)
XLA Ops:
  13.0 65.1 %all-reduce = bf16[23808]{0:T(1024)(128)(2,1)S(1)} all-reduce(bf16[23808]{0:T(1024)(128)(2,1)S(1)} %dynamic-update-slice), channel_id=1, replica_groups=mesh['seq'=2,'shard'=16] {'shard'}, use_global_device_ids=true, to_apply=%add | all-reduce | flops 23808 | bytes 95232
  78.5 23.0 all_gather.34
  116.9 35.4 reshape.775
  152.3 30.4 copy.302
  182.7 830.2 %while.67 = (s32[]{:T(128)}, f32[2,384,16,48]{1,0,3,2:T(2,128)}, bf16[2,512,768]{2,1,0:T(8,128)(2,1)}, bf16[128,48,16,48]{0,3,1,2:T(8,128)(2,1)}, s32[]{:T(128)}, /*index=5*/s32[]{:T(128)}) while((s32[]{:T(128)}, f32[2,384,16,48]{1,0,3,2:T(2,128)}, bf16[2,512,768]{2,1,0:T(8,128)(2,1)}, bf16[128,48,16,48]{0,3,1,2:T(8,128)(2,1)}, s32[]{:T(128)}, ...), condition=%wide.region_3.4_spmd, body=%wide.region_2.3_spmd.sunk | while | flops 3624124416 | bytes 545783872 | solution.py:321
  183.9 202.6 %gather_fusion = bf16[49152,768]{1,0:T(8,128)(2,1)} fusion(bf16[512,768]{1,0:T(8,128)(2,1)S(1)} %dynamic-slice_bitcast_fusion.41, s32[49152]{0:T(1024)S(1)} %fusion.362), kind=kCustom, calls=%fused_computation.clone.1 | custom fusion | bytes 151191552 | tf_op jit(solution)/shard_map/while/body/eval_jaxpr/gather | solution.py:97
  386.5 96.8 %copy.432 = bf16[49152,768]{0,1:T(8,128)(2,1)} copy(bf16[49152,768]{1,0:T(8,128)(2,1)} %gather_fusion) | data formatting | bytes 150994944 | tf_op jit(solution)/shard_map/while/body/eval_jaxpr/gather | solution.py:97
  483.2 49.5 copy.433
  532.8 33.5 convolution_bitcast_fusion.2
  567.5 30.3 dynamic_update_slice.43
  599.0 202.6 %gather_fusion = bf16[49152,768]{1,0:T(8,128)(2,1)} fusion(bf16[512,768]{1,0:T(8,128)(2,1)S(1)} %dynamic-slice_bitcast_fusion.41, s32[49152]{0:T(1024)S(1)} %fusion.362), kind=kCustom, calls=%fused_computation.clone.1 | custom fusion | bytes 151191552 | tf_op jit(solution)/shard_map/while/body/eval_jaxpr/gather | solution.py:97
  801.6 96.8 %copy.432 = bf16[49152,768]{0,1:T(8,128)(2,1)} copy(bf16[49152,768]{1,0:T(8,128)(2,1)} %gather_fusion) | data formatting | bytes 150994944 | tf_op jit(solution)/shard_map/while/body/eval_jaxpr/gather | solution.py:97
  898.4 49.5 copy.433
  947.9 33.5 convolution_bitcast_fusion.2
  982.6 30.3 dynamic_update_slice.43
  1057.6 20.6 all_gather.40
  1079.5 16.7 all-to-all-done
  1122.2 66.1 %while.68 = (s32[]{:T(128)}, bf16[12,768,64]{1,2,0:T(8,128)(2,1)}, f32[12,768]{1,0:T(8,128)}, bf16[12,3,768,64]{3,2,1,0:T(8,128)(2,1)}, s32[]{:T(128)}, /*index=5*/s32[]{:T(128)}, s32[]{}, s32[]{}) while((s32[]{:T(128)}, bf16[12,768,64]{1,2,0:T(8,128)(2,1)}, f32[12,768]{1,0:T(8,128)}, bf16[12,3,768,64]{3,2,1,0:T(8,128)(2,1)}, s32[]{:T(128)}, ...), condition=%wide.region_9.10_spmd, body=%wide.region_6.9_spmd.sunk | while | flops 156351744 | bytes 7805049 | solution.py:127
  1201.1 19.9 all_gather.41
  1245.1 28.3 multiply_convert_fusion.3
  1312.1 35.3 all-to-all-done.2
  1373.7 66.0 %while.69 = (s32[]{:T(128)}, bf16[12,768,64]{1,2,0:T(8,128)(2,1)}, f32[12,768]{1,0:T(8,128)}, bf16[12,3,768,64]{3,2,1,0:T(8,128)(2,1)}, s32[]{:T(128)}, /*index=5*/s32[]{:T(128)}, s32[]{}, s32[]{}) while((s32[]{:T(128)}, bf16[12,768,64]{1,2,0:T(8,128)(2,1)}, f32[12,768]{1,0:T(8,128)}, bf16[12,3,768,64]{3,2,1,0:T(8,128)(2,1)}, s32[]{:T(128)}, ...), condition=%wide.region_17.18_spmd, body=%wide.region_14.17_spmd.sunk | while | flops 156351744 | bytes 7805049 | solution.py:127
  1452.6 20.7 all_gather.39
  1507.8 28.0 multiply_convert_fusion.2
  1544.6 905.2 %gather_fusion.3 = f32[77568]{0:T(1024)} fusion(f32[2,384,768]{2,1,0:T(8,128)S(1)} %fusion.239, s32[77568]{0:T(1024)} %reshape.819), kind=kCustom, calls=%fused_computation.3 | custom fusion | bytes 1551360 | tf_op jit(solution)/shard_map/jit(take_along_axis)/gather | solution.py:358
  2456.3 475.0 %scatter_custom_fusion = f32[589824]{0:T(1024)S(1)} fusion(s32[77568]{0:T(1024)} %reshape.825, f32[77568]{0:T(1024)} %reshape.827, f32[]{:T(128)} %constant.128.clone.1), kind=kCustom, calls=%fused_computation.309 | custom fusion | flops 77568 | bytes 2359808
  2996.4 111.2 %while.70 = (s32[]{:T(128)}, bf16[12,3,768,64]{2,3,1,0:T(8,128)(2,1)}, bf16[12,3,768,64]{3,2,1,0:T(8,128)(2,1)}, f32[12,768]{1,0:T(8,128)}, bf16[12,768,64]{2,1,...) while((s32[]{:T(128)}, bf16[12,3,768,64]{2,3,1,0:T(8,128)(2,1)}, ...), condition=%wide.region_38.39_spmd, body=%wide.region_36.38_spmd.sunk | while | flops 383335680 | bytes 19975300 | solution.py:191
  3158.3 31.0 all-to-all-done.5
  3202.3 23.6 copy.333
  3273.8 16.4 fusion.236
  3341.1 111.9 %while.71 = (s32[]{:T(128)}, bf16[12,3,768,64]{2,3,1,0:T(8,128)(2,1)}, bf16[12,3,768,64]{3,2,1,0:T(8,128)(2,1)}, f32[12,768]{1,0:T(8,128)}, bf16[12,768,64]{2,1,...) while((s32[]{:T(128)}, bf16[12,3,768,64]{2,3,1,0:T(8,128)(2,1)}, ...), condition=%wide.region_45.46_spmd, body=%wide.region_43.45_spmd.sunk | while | flops 383335680 | bytes 19975300 | solution.py:191
  3453.1 15.3 copy.339
  3496.0 35.8 copy.342
  3546.6 23.6 copy.340
  3616.9 1544.3 %while.72 = (s32[]{:T(128)}, f32[128,48,16,48]{0,3,1,2:T(8,128)}, f32[2,384,768]{2,1,0:T(8,128)}, bf16[2,384,768]{2,1,0:T(8,128)(2,1)}, bf16[2,512,768]{2,1,0:T(...) while((s32[]{:T(128)}, f32[128,48,16,48]{0,3,1,2:T(8,128)}, ...), condition=%wide.region_49.50_spmd.clone, body=%wide.region_48.49_spmd.clone.sunk | while | flops 7257686528 | bytes 1124798080 | solution.py:436
  3619.3 202.5 %gather_fusion.1 = bf16[49152,768]{1,0:T(8,128)(2,1)} fusion(bf16[512,768]{1,0:T(8,128)(2,1)S(1)} %get-tuple-element.977, s32[49152]{0:T(1024)S(1)} %fusion.389), kind=kCustom, calls=%fused_computation.1.clone.clone.1 | custom fusion | bytes 151191552 | tf_op jit(solution)/shard_map/while/body/eval_jaxpr/gather | solution.py:97
  3821.9 96.8 %copy.436 = bf16[49152,768]{0,1:T(8,128)(2,1)} copy(bf16[49152,768]{1,0:T(8,128)(2,1)} %gather_fusion.1) | data formatting | bytes 150994944 | tf_op jit(solution)/shard_map/while/body/eval_jaxpr/gather | solution.py:97
  3918.6 49.9 copy.437
  3968.9 33.4 bitcast_add_fusion.3
  4002.4 202.6 %gather_fusion.2 = bf16[49152,768]{1,0:T(8,128)(2,1)} fusion(bf16[512,768]{1,0:T(8,128)(2,1)S(1)} %copy-done.1, s32[49152]{0:T(1024)S(1)} %fusion.390), kind=kCustom, calls=%fused_computation.2.clone.clone.1 | custom fusion | bytes 151191552 | tf_op jit(solution)/shard_map/while/body/eval_jaxpr/gather | solution.py:97
  4205.0 96.8 %copy.438 = bf16[49152,768]{0,1:T(8,128)(2,1)} copy(bf16[49152,768]{1,0:T(8,128)(2,1)} %gather_fusion.2) | data formatting | bytes 150994944 | tf_op jit(solution)/shard_map/while/body/eval_jaxpr/gather | solution.py:97
  4301.8 49.5 copy.439
  4351.3 33.6 fusion.391
  4388.8 202.5 %gather_fusion.1 = bf16[49152,768]{1,0:T(8,128)(2,1)} fusion(bf16[512,768]{1,0:T(8,128)(2,1)S(1)} %get-tuple-element.977, s32[49152]{0:T(1024)S(1)} %fusion.389), kind=kCustom, calls=%fused_computation.1.clone.clone.1 | custom fusion | bytes 151191552 | tf_op jit(solution)/shard_map/while/body/eval_jaxpr/gather | solution.py:97
  4591.3 96.8 %copy.436 = bf16[49152,768]{0,1:T(8,128)(2,1)} copy(bf16[49152,768]{1,0:T(8,128)(2,1)} %gather_fusion.1) | data formatting | bytes 150994944 | tf_op jit(solution)/shard_map/while/body/eval_jaxpr/gather | solution.py:97
  4688.1 49.9 copy.437
  4738.3 38.8 bitcast_add_fusion.3
  4777.3 202.6 %gather_fusion.2 = bf16[49152,768]{1,0:T(8,128)(2,1)} fusion(bf16[512,768]{1,0:T(8,128)(2,1)S(1)} %copy-done.1, s32[49152]{0:T(1024)S(1)} %fusion.390), kind=kCustom, calls=%fused_computation.2.clone.clone.1 | custom fusion | bytes 151191552 | tf_op jit(solution)/shard_map/while/body/eval_jaxpr/gather | solution.py:97
  4979.8 96.8 %copy.438 = bf16[49152,768]{0,1:T(8,128)(2,1)} copy(bf16[49152,768]{1,0:T(8,128)(2,1)} %gather_fusion.2) | data formatting | bytes 150994944 | tf_op jit(solution)/shard_map/while/body/eval_jaxpr/gather | solution.py:97
  5076.6 49.5 copy.439
  5126.1 33.6 fusion.391
  5171.1 33.8 copy.344
  5204.9 34.8 convert_element_type.343
  5242.8 109.4 %reduce-scatter.15.cloned.1.call-done = bf16[384,768]{1,0:T(8,128)(2,1)} async-done(((bf16[6144,768]{1,0:T(8,128)(2,1)}), bf16[384,768]{1,0:T(8,128)(2,1)}) %reduce-scatter.15.cloned.1.call-update) | async-done | bytes 589840 | tf_op jit(solution)/shard_map/reduce_scatter | solution.py:459
  5355.4 16.8 reduce-scatter.27.cloned.1.call-done
  5391.5 52.4 all-reduce.11.cloned.1.call-done
  5498.9 61.9 %all-reduce.3 = (bf16[32]{0:T(256)(128)(2,1)S(1)}, bf16[23808]{0:T(1024)(128)(2,1)S(1)}) all-reduce(bf16[32]{0:T(256)(128)(2,1)} %convert_element_type.325, bf16[23808]{0:T(1024)(128)(2,1)} %constant_dynamic-update-slice_fusion.1), channel_id=2, replica_groups=mesh['seq'=2,'shard'=16] {'shard'}, use_global_device_ids=true, to_apply=%region_28.29.clone | all-reduce | flops 23840 | bytes 95360
  5562.2 57.2 reduce-scatter.31.cloned.1.call-done
  5619.3 60.0 %reduce-scatter.13.cloned.1.call-done = bf16[32,768]{1,0:T(8,128)(2,1)} async-done(((bf16[512,768]{1,0:T(8,128)(2,1)}), bf16[32,768]{1,0:T(8,128)(2,1)}) %reduce-scatter.13.cloned.1.call-update) | async-done | bytes 49168 | tf_op jit(solution)/shard_map/reduce_scatter | solution.py:456
  5679.4 82.6 %all-gather.14.cloned.1.call-done = bf16[8,768,768]{2,1,0:T(8,128)(2,1)} async-done(((bf16[8,48,768]{2,1,0:T(8,128)(2,1)}), bf16[8,768,768]{2,1,0:T(8,128)(2,1)}) %all-gather.14.cloned.1.call-update) | async-done | bytes 9437200 | tf_op jit(solution)/shard_map/all_gather | solution.py:532
  5769.5 15.6 multiply_add_fusion.5
  5785.2 18.1 fusion.135
  5803.3 17.1 convert_bitcast_fusion
  5853.0 90.3 %reduce-scatter.19.cloned.1.call-done = bf16[48,8,768]{2,1,0:T(8,128)(2,1)} async-done(((bf16[768,8,768]{2,1,0:T(8,128)(2,1)}), bf16[48,8,768]{2,1,0:T(8,128)(2,1)}) %reduce-scatter.19.cloned.1.call-update) | async-done | bytes 589840 | tf_op jit(solution)/shard_map/reduce_scatter | solution.py:551
  (1175 shorter events, 1072.2 us)
Async XLA Ops:
  7.2 5754.8 %copy-start = (f32[8,48,768]{2,1,0:T(8,128)S(1)}, f32[8,48,768]{2,1,0:T(8,128)}, u32[]{:S(2)}) copy-start(f32[8,48,768]{2,1,0:T(8,128)} %param.58) | copy-start | bytes 3538948
  7.3 109.6 %all-gather.6.cloned.1.call-start = ((), (), s32[]{:S(2)}) async-start(), calls=%async_computation.18 | async-start | bytes 10027008 | tf_op jit(solution)/shard_map/all_gather | solution.py:297
  9.6 1019.3 %all-gather.8.cloned.1.call-start = ((), (), s32[]{:S(2)}) async-start(), calls=%async_computation.19 | async-start | bytes 10027008 | tf_op jit(solution)/shard_map/all_gather | solution.py:298
  10.6 1234.5 %all-gather.10.cloned.1.call-start = ((), (), s32[]{:S(2)}) async-start(), calls=%async_computation.20 | async-start | bytes 10027008 | tf_op jit(solution)/shard_map/all_gather | solution.py:299
  10.9 92.8 %copy-start.176 = (f32[768]{0:T(1024)}, f32[768]{0:T(1024)S(1)}, u32[]{:S(2)}) copy-start(f32[768]{0:T(1024)S(1)} %div.270) | copy-start | bytes 9220
  11.3 92.4 %copy-start.177 = (f32[768]{0:T(1024)}, f32[768]{0:T(1024)S(1)}, u32[]{:S(2)}) copy-start(f32[768]{0:T(1024)S(1)} %rsqrt.82) | copy-start | bytes 9220
  11.4 92.4 %copy-start.162 = (pred[768]{0:T(1024)(128)(4,1)}, pred[768]{0:T(1024)(128)(4,1)S(1)}, u32[]{:S(2)}) copy-start(pred[768]{0:T(1024)(128)(4,1)S(1)} %broadcast_in_dim.89) | copy-start | bytes 2308
  78.1 31.0 copy-start.103
  78.1 25.6 copy-start.133
  78.1 25.6 copy-start.135
  103.8 7.7 collective-permute-start
  106.9 8.8 collective-permute-start.1
  1027.1 212.2 %copy-start.106 = (f32[768]{0:T(1024)}, f32[768]{0:T(1024)S(1)}, u32[]{:S(2)}) copy-start(f32[768]{0:T(1024)S(1)} %broadcast_multiply_fusion.4) | copy-start | bytes 9220
  1050.5 45.7 all-to-all-start
  1056.0 217.4 %all-gather.12.cloned.1.call-start = ((), (), s32[]{:S(2)}) async-start(), calls=%async_computation.21 | async-start | bytes 10027008 | tf_op jit(solution)/shard_map/all_gather | solution.py:300
  1197.3 29.9 copy-start.45
  1197.3 31.5 all-to-all-start.1
  1242.7 30.8 copy-start.139
  1245.1 28.4 copy-start.178
  1245.1 28.3 copy-start.25
  1281.1 222.0 %copy-start.108 = (f32[768]{0:T(1024)}, f32[768]{0:T(1024)S(1)}, u32[]{:S(2)}) copy-start(f32[768]{0:T(1024)S(1)} %broadcast_multiply_fusion.2) | copy-start | bytes 9220
  1300.5 46.8 all-to-all-start.2
  1308.8 46.0 copy-start.145
  1448.8 25.4 copy-start.160
  1448.8 43.5 all-to-all-start.3
  1452.6 27.2 copy-start.20
  1452.6 27.2 copy-start.137
  1503.1 32.7 slice-start.11
  1506.4 29.4 copy-start.27
  1506.4 29.4 copy-start.141
  1507.8 28.1 copy-start.180
  1507.8 28.1 copy-start.203
  1507.8 28.1 slice-start.12
  1507.8 28.1 slice-start.13
  2973.5 18.2 all-to-all-start.4
  3144.8 44.5 all-to-all-start.5
  3150.2 2092.5 %reduce-scatter.23.cloned.1.call-start = ((), (), s32[]{:S(2)}) async-start(), calls=%async_computation.28 | async-start | bytes 10027008 | tf_op jit(solution)/shard_map/reduce_scatter | solution.py:474
  3313.8 21.4 all-to-all-start.6
  3318.3 1924.5 %reduce-scatter.21.cloned.1.call-start = ((), (), s32[]{:S(2)}) async-start(), calls=%async_computation.27 | async-start | bytes 10027008 | tf_op jit(solution)/shard_map/reduce_scatter | solution.py:471
  3490.5 43.1 all-to-all-start.7
  3495.9 1746.9 %reduce-scatter.17.cloned.1.call-start = ((), (), s32[]{:S(2)}) async-start(), calls=%async_computation.24 | async-start | bytes 10027008 | tf_op jit(solution)/shard_map/reduce_scatter | solution.py:465
  3594.1 21.6 collective-permute-start.2
  3596.3 19.4 collective-permute-start.3
  3615.4 1736.8 %reduce-scatter.15.cloned.1.call-start = ((), (), s32[]{:S(2)}) async-start(), calls=%async_computation.23 | async-start | bytes 10027008 | tf_op jit(solution)/shard_map/reduce_scatter | solution.py:459
  3918.6 49.9 copy-start.13
  3968.9 33.6 copy-start.1
  4688.1 49.9 copy-start.13
  4738.3 38.9 copy-start.1
  5239.8 112.5 %copy-start.58 = (bf16[768,256]{1,0:T(8,128)(2,1)S(1)}, bf16[768,256]{1,0:T(8,128)(2,1)}, u32[]{:S(2)}) copy-start(bf16[768,256]{1,0:T(8,128)(2,1)} %copy-done.57) | copy-start | bytes 1179652
  5239.8 132.4 %reduce-scatter.27.cloned.1.call-start = ((), (), s32[]{:S(2)}) async-start(), calls=%async_computation.30 | async-start | bytes 1179648 | tf_op jit(solution)/shard_map/reduce_scatter | solution.py:386
  5242.7 201.2 %all-reduce.11.cloned.1.call-start = ((), (), s32[]{:S(2)}) async-start(), calls=%async_computation.34 | async-start | bytes 4718592 | tf_op jit(solution)/shard_map/psum | solution.py:510
  5352.3 209.8 %reduce-scatter.25.cloned.1.call-start = ((), (), s32[]{:S(2)}) async-start(), calls=%async_computation.29 | async-start | bytes 417792 | tf_op jit(solution)/shard_map/reduce_scatter | solution.py:477
  5355.0 207.2 %reduce-scatter.29.cloned.1.call-start = ((), (), s32[]{:S(2)}) async-start(), calls=%async_computation.31 | async-start | bytes 139264 | tf_op jit(solution)/shard_map/reduce_scatter | solution.py:480
  5380.1 239.2 %reduce-scatter.31.cloned.1.call-start = ((), (), s32[]{:S(2)}) async-start(), calls=%async_computation.32 | async-start | bytes 208896 | tf_op jit(solution)/shard_map/reduce_scatter | solution.py:483
  5385.9 293.5 %reduce-scatter.13.cloned.1.call-start = ((), (), s32[]{:S(2)}) async-start(), calls=%async_computation.22 | async-start | bytes 835584 | tf_op jit(solution)/shard_map/reduce_scatter | solution.py:456
  5389.7 56.1 copy-start.130
  5389.7 56.1 copy-start.158
  5389.7 56.1 copy-start.161
  5391.4 370.5 %all-gather.14.cloned.1.call-start = ((), (), s32[]{:S(2)}) async-start(), calls=%async_computation.25 | async-start | bytes 10027008 | tf_op jit(solution)/shard_map/all_gather | solution.py:532
  5444.0 389.6 %all-reduce.9.cloned.1.call-start = ((), (), s32[]{:S(2)}) async-start(), calls=%async_computation.33 | async-start | bytes 197632 | tf_op jit(solution)/shard_map/psum | solution.py:518
  5461.3 31.4 copy-start.192
  5461.3 32.8 copy-start.191
  5679.4 263.9 %reduce-scatter.19.cloned.1.call-start = ((), (), s32[]{:S(2)}) async-start(), calls=%async_computation.26 | async-start | bytes 10027008 | tf_op jit(solution)/shard_map/reduce_scatter | solution.py:551
  5850.6 92.7 %copy-start.42 = (f32[8,48,768]{2,1,0:T(8,128)S(1)}, f32[8,48,768]{2,1,0:T(8,128)}, u32[]{:S(2)}) copy-start(f32[8,48,768]{2,1,0:T(8,128)} %param.55) | copy-start | bytes 3538948
  (198 other events, 1176.6 us)
Sparse Core Ops, SparseCore 0:
  10.9 88.3 all-gather.5
  102.2 81.0 all-gather.7
  186.2 79.5 all-gather.9
  1059.4 80.1 all-gather.11
  3263.5 109.3 reduce-scatter.22
  3377.4 111.1 reduce-scatter.20
  3615.5 112.2 reduce-scatter.16
  5239.9 112.2 reduce-scatter.14
  5355.1 17.1 reduce-scatter.26
  5374.7 69.1 all-reduce.10
  5448.0 55.6 reduce-scatter.24
  5508.0 54.0 reduce-scatter.28
  5566.6 52.6 reduce-scatter.30
  5623.7 55.5 reduce-scatter.12
  5681.5 80.4 all-gather.13
  5765.6 19.3 all-reduce.8
  5833.7 109.5 reduce-scatter.18
where the time goes:
time: 5990 us; the launch traced here: 5950 us
  local copies, waits for them, and re-layouts  3690 us (62%)
  matrix products  760 us (13%)
  other arithmetic  632 us (11%)
  waiting for transfers between devices  574 us (10%)
  blocking collectives  224 us (4%)
    gather x12, local copies, waits for them, and re-layouts, conv_windows(): padded_clip[window_index].reshape(frame_count, KW, GROUPS, D // GROUPS)  1800 us
    gather x6, local copies, waits for them, and re-layouts, on_device(): jnp.take_along_axis(angular_agreement, contrast_choice_embeddings, axis=2)  909 us
    dot_general x212, matrix products, bdot(): return jnp.dot(left_side, right_side, preferred_element_type=jnp.float32)  485 us
    unnamed x11, other arithmetic  477 us
    while x14, local copies, waits for them, and re-layouts  298 us
    unnamed x514, local copies, waits for them, and re-layouts  204 us
    unnamed x2, blocking collectives  127 us
  transfers between devices with their start and end apart: 29, of which 15 were waited for; matrix products, arithmetic and copies ran while one was open for 54% of the time, Pallas kernels for 0%

commit v1 on v0

v1 whole, which is shorter than its diff:
```python
import functools

import jax
import jax.numpy as jnp
from jax import lax
from jax.experimental import pallas as pl
from jax.experimental.pallas import tpu as pltpu
from jax.sharding import PartitionSpec as P

D = 768
HEADS = 12
HDIM = 64
FF = 3072
CIN = 512
PROJ = 256
CODES = 320
QGROUPS = 2
LAYERS = 2
STEP = 10
SMALL_LANES = 1536


beta_one = 0.9
beta_two = 0.95
beta_rotated = 0.5
adam_epsilon = 1e-08
decay_rate = 0.01
rate_matrix = 0.02
rate_target = 0.08
rate_codebook = 0.6
rate_vector = 0.3
rate_rotated = 0.08
contrastive_sharpness = 0.1
norm_epsilon = 1e-05
unit_epsilon = 1e-06

KW = 128
GROUPS = 16
GC = D // GROUPS
LANE = 64
PACK = 4
PADW = GROUPS * LANE
HALF = KW // PACK
STEPS = HALF + 1
VMEM = 56 * 1024 * 1024
NT = (((1,), (1,)), ((), ()))
NN = (((1,), (0,)), ((), ()))


def mm(a, b, dims=NN):
    return lax.dot_general(a, b, dims, preferred_element_type=jnp.float32)


def spread_matrix(rows, out_cols, block, wide):
    i = lax.broadcasted_iota(jnp.int32, (rows, out_cols), 0)
    j = lax.broadcasted_iota(jnp.int32, (rows, out_cols), 1)
    return ((i // block) * wide + i % block == j).astype(jnp.bfloat16)


def pack_pair(x_ref, even_ref, odd_ref, rows):
    low = lax.broadcasted_iota(jnp.int32, (rows * 16, 128), 1) < LANE
    x = x_ref[...].reshape(rows, PACK, 16, 128)
    for half in range(2):
        first = x[:, 2 * half].reshape(rows * 16, 128).astype(jnp.float32)
        second = x[:, 2 * half + 1].reshape(rows * 16, 128).astype(jnp.float32)
        even_ref[:, half * 128:half * 128 + 128] = jnp.where(low, first, pltpu.roll(second, LANE, 1)).astype(jnp.bfloat16)
        odd_ref[:, half * 128:half * 128 + 128] = jnp.where(low, pltpu.roll(first, LANE, 1), second).astype(jnp.bfloat16)


def unpack_pair(even, odd, out_ref, rows):
    low = lax.broadcasted_iota(jnp.int32, (rows * 16, 128), 1) < LANE
    parts = []
    for half in range(2):
        e = even[:, half * 128:half * 128 + 128]
        o = odd[:, half * 128:half * 128 + 128]
        parts.append(jnp.where(low, e, pltpu.roll(o, LANE, 1)).reshape(rows, 1, 16, 128))
        parts.append(jnp.where(low, pltpu.roll(e, LANE, 1), o).reshape(rows, 1, 16, 128))
    out_ref[...] = jnp.concatenate(parts, axis=1).reshape(PACK * rows, 16, 128)


def widen_taps(w_ref, wide_ref, shards):
    per = KW // shards
    sel = spread_matrix(per * GC, per * LANE, GC, LANE)
    block = mm(w_ref[...].reshape(shards * 2 * GC, per * GC), sel).astype(jnp.bfloat16)
    for group in range(2):
        wide_ref[group, GC:, :] = jnp.zeros((LANE - GC, STEPS * 256), jnp.bfloat16)
        wide_ref[group, 0:GC, KW * LANE:] = jnp.zeros((GC, STEPS * 256 - KW * LANE), jnp.bfloat16)
        for s in range(shards):
            start = (2 * s + group) * GC
            wide_ref[group, 0:GC, s * per * LANE:(s + 1) * per * LANE] = block[start:start + GC]


def build_taps(wide_ref, taps_ref, group):
    wide = wide_ref[group]
    shifted = pltpu.roll(wide.astype(jnp.float32), LANE, 1).astype(jnp.bfloat16)
    total = STEPS * 256
    taps_ref[0:64, :] = wide
    taps_ref[64:128, :] = shifted
    taps_ref[128:192, 0:128] = jnp.zeros((64, 128), jnp.bfloat16)
    taps_ref[128:192, 128:total] = wide[:, 0:total - 128]
    taps_ref[192:256, 0:128] = jnp.zeros((64, 128), jnp.bfloat16)
    taps_ref[192:256, 128:total] = shifted[:, 0:total - 128]


def conv_forward_kernel(rows, shards, x_ref, w_ref, y_ref, even_ref, odd_ref, taps_ref, wide_ref):
    m = rows * 16
    pack_pair(x_ref, even_ref, odd_ref, rows + HALF)
    widen_taps(w_ref, wide_ref, shards)
    results = []
    for group, packed in enumerate((even_ref, odd_ref)):
        build_taps(wide_ref, taps_ref, group)
        left = jnp.concatenate([packed[q * 16:q * 16 + m, :] for q in range(STEPS)], axis=1)
        results.append(mm(left, taps_ref[...], NT))
    unpack_pair(results[0], results[1], y_ref, rows)


def conv_forward(x, w, rows, shards):
    frames = PACK * (rows + HALF)
    return pl.pallas_call(
        functools.partial(conv_forward_kernel, rows, shards),
        grid=(GROUPS // 2,),
        in_specs=[
            pl.BlockSpec((frames, 16, 128), lambda g: (0, 0, g)),
            pl.BlockSpec((shards, 2 * GC, w.shape[2]), lambda g: (0, g, 0)),
        ],
        out_specs=pl.BlockSpec((PACK * rows, 16, 128), lambda g: (0, 0, g)),
        out_shape=jax.ShapeDtypeStruct((PACK * rows, 16, PADW), jnp.float32),
        scratch_shapes=[pltpu.VMEM(((rows + HALF) * 16, 256), jnp.bfloat16)] * 2 + [
            pltpu.VMEM((256, STEPS * 256), jnp.bfloat16),
            pltpu.VMEM((2, LANE, STEPS * 256), jnp.bfloat16),
        ],
        compiler_params=pltpu.CompilerParams(vmem_limit_bytes=VMEM, dimension_semantics=("arbitrary",)),
        name="conv_forward",
    )(x, w)


def conv_backward_kernel(rows, shards, x_ref, d_ref, w_ref, dx_ref, dw_ref,
                         xe_ref, xo_ref, de_ref, do_ref, taps_ref, wide_ref, prod_ref, grad_ref):
    m = rows * 16
    per = KW // shards
    pack_pair(x_ref, xe_ref, xo_ref, rows + HALF)
    pack_pair(d_ref, de_ref, do_ref, rows + HALF)
    widen_taps(w_ref, wide_ref, shards)
    results = []
    for group, (x_packed, d_packed) in enumerate(((xe_ref, de_ref), (xo_ref, do_ref))):
        build_taps(wide_ref, taps_ref, group)
        d_turned = d_packed[HALF // 2 * 16:HALF // 2 * 16 + m, :].astype(jnp.float32).T.astype(jnp.bfloat16)
        acc = jnp.zeros((m, 256), jnp.float32)
        for q in range(STEPS):
            left = d_packed[(HALF - q) * 16:(HALF - q) * 16 + m, :]
            acc = acc + mm(left, taps_ref[:, q * 256:q * 256 + 256])
            prod_ref[:, q * 256:q * 256 + 256] = mm(d_turned, x_packed[q * 16:q * 16 + m, :])
        results.append(acc)
        width = KW * LANE
        straight = prod_ref[0:GC, 0:width] + prod_ref[128:128 + GC, 128:128 + width]
        turned = prod_ref[64:64 + GC, :] + pltpu.roll(prod_ref[192:192 + GC, :], STEPS * 256 - 128, 1)
        grad = straight + pltpu.roll(turned, STEPS * 256 - 64, 1)[:, 0:width]
        grad = grad.astype(jnp.bfloat16)
        for s in range(shards):
            start = (2 * s + group) * GC
            grad_ref[start:start + GC, :] = grad[:, s * per * LANE:(s + 1) * per * LANE]
    sel = spread_matrix(per * GC, per * LANE, GC, LANE)
    dw_ref[...] = mm(grad_ref[...], sel, NT).astype(jnp.bfloat16).reshape(shards, 2 * GC, per * GC)
    unpack_pair(results[0], results[1], dx_ref, rows)


def conv_backward(x, d, w, rows, shards):
    frames = PACK * (rows + HALF)
    return pl.pallas_call(
        functools.partial(conv_backward_kernel, rows, shards),
        grid=(GROUPS // 2,),
        in_specs=[
            pl.BlockSpec((frames, 16, 128), lambda g: (0, 0, g)),
            pl.BlockSpec((frames, 16, 128), lambda g: (0, 0, g)),
            pl.BlockSpec((shards, 2 * GC, w.shape[2]), lambda g: (0, g, 0)),
        ],
        out_specs=[
            pl.BlockSpec((PACK * rows, 16, 128), lambda g: (0, 0, g)),
            pl.BlockSpec((shards, 2 * GC, w.shape[2]), lambda g: (0, g, 0)),
        ],
        out_shape=[
            jax.ShapeDtypeStruct((PACK * rows, 16, PADW), jnp.float32),
            jax.ShapeDtypeStruct(w.shape, jnp.bfloat16),
        ],
        scratch_shapes=[pltpu.VMEM(((rows + HALF) * 16, 256), jnp.bfloat16)] * 4 + [
            pltpu.VMEM((256, STEPS * 256), jnp.bfloat16),
            pltpu.VMEM((2, LANE, STEPS * 256), jnp.bfloat16),
            pltpu.VMEM((256, STEPS * 256), jnp.float32),
            pltpu.VMEM((shards * 2 * GC, KW // shards * LANE), jnp.bfloat16),
        ],
        compiler_params=pltpu.CompilerParams(vmem_limit_bytes=VMEM, dimension_semantics=("arbitrary",)),
        name="conv_backward",
    )(x, d, w)


def to_strips(padded, frame_count):
    clips = padded.shape[0]
    strips = 16 // clips
    length = frame_count // strips
    sel = spread_matrix(D, PADW, GC, LANE)
    wide = mm(padded.reshape(-1, D), sel).astype(jnp.bfloat16).reshape(clips, -1, PADW)
    parts = jnp.stack([wide[:, s * length:s * length + length + KW] for s in range(strips)], 1)
    return parts.reshape(16, length + KW, PADW).transpose(1, 0, 2)


def from_strips(y, clips):
    rows = y.transpose(1, 0, 2).reshape(-1, PADW)
    high = lax.reduce_precision(rows, 8, 7)
    rest = (rows - high).astype(jnp.bfloat16)
    high = high.astype(jnp.bfloat16)
    sel = spread_matrix(D, PADW, GC, LANE)
    return mm(high, sel, NT) + mm(rest, sel, NT)


SCALE = HDIM ** (-0.5)


def turned(block):
    return block.astype(jnp.float32).T.astype(jnp.bfloat16)


def attend_kernel(blocks, q_ref, *refs):
    keys = [refs[2 * j] for j in range(blocks)]
    values = [refs[2 * j + 1] for j in range(blocks)]
    mixed_ref, stat_ref = refs[2 * blocks:]
    frames = q_ref.shape[0]
    low = lax.broadcasted_iota(jnp.int32, (frames, 128), 1) < HDIM
    scaled = q_ref[...] * jnp.bfloat16(SCALE)
    none = jnp.zeros_like(scaled)
    turned_keys = [turned(k[...]) for k in keys]
    parts = []
    stats = []
    for head in range(2):
        query = jnp.where(low, scaled, none) if head == 0 else jnp.where(low, none, scaled)
        scores = [mm(query, k) for k in turned_keys]
        largest = functools.reduce(jnp.maximum, [jnp.max(s, 1, keepdims=True) for s in scores])
        powers = [jnp.exp(s - largest) for s in scores]
        total = functools.reduce(jnp.add, [jnp.sum(p, 1, keepdims=True) for p in powers])
        out = functools.reduce(jnp.add, [mm(p.astype(jnp.bfloat16), v[...]) for p, v in zip(powers, values)])
        parts.append(out * (1.0 / total))
        stats.append(jnp.broadcast_to(largest + jnp.log(total), (frames, 128)))
    mixed_ref[...] = jnp.where(low, parts[0], parts[1]).astype(jnp.bfloat16)
    rows = jnp.where(low, stats[0], stats[1]).T
    stat_ref[0, 0, 0:1, :] = rows[0:1, :]
    stat_ref[0, 0, 1:2, :] = rows[HDIM:HDIM + 1, :]


def attend(query, keys, values, clips):
    blocks = len(keys)
    rows = query.shape[0]
    frames = rows // clips
    spec = pl.BlockSpec((frames, 128), lambda c, h: (c, h))
    operands = [query]
    for k, v in zip(keys, values):
        operands += [k, v]
    return pl.pallas_call(
        functools.partial(attend_kernel, blocks),
        grid=(clips, HEADS // 2),
        in_specs=[spec] * len(operands),
        out_specs=[spec, pl.BlockSpec((1, 1, 2, frames), lambda c, h: (c, h, 0, 0))],
        out_shape=[
            jax.ShapeDtypeStruct((rows, D), jnp.bfloat16),
            jax.ShapeDtypeStruct((clips, HEADS // 2, 2, frames), jnp.float32),
        ],
        compiler_params=pltpu.CompilerParams(vmem_limit_bytes=VMEM, dimension_semantics=("arbitrary", "arbitrary")),
        name="attend",
    )(*operands)


def attend_back_kernel(blocks, q_ref, d_ref, stat_ref, *refs):
    keys = [refs[2 * j] for j in range(blocks)]
    values = [refs[2 * j + 1] for j in range(blocks)]
    dq_ref = refs[2 * blocks]
    dk = [refs[2 * blocks + 1 + 2 * j] for j in range(blocks)]
    dv = [refs[2 * blocks + 2 + 2 * j] for j in range(blocks)]
    frames = q_ref.shape[0]
    low = lax.broadcasted_iota(jnp.int32, (frames, 128), 1) < HDIM
    scaled = q_ref[...] * jnp.bfloat16(SCALE)
    grad = d_ref[...]
    none = jnp.zeros_like(scaled)
    q_turned = turned(scaled)
    d_turned = turned(grad)
    gap = jnp.zeros((HDIM, frames), jnp.bfloat16)
    k_turned = [turned(k[...]) for k in keys]
    dq_rows = []
    dk_sum = [None] * blocks
    dv_sum = [None] * blocks
    for head in range(2):
        pick = slice(head * HDIM, head * HDIM + HDIM)
        if head == 0:
            query, grad_head = jnp.where(low, scaled, none), jnp.where(low, grad, none)
            q_side = jnp.concatenate([q_turned[pick], gap], 0)
            d_side = jnp.concatenate([d_turned[pick], gap], 0)
        else:
            query, grad_head = jnp.where(low, none, scaled), jnp.where(low, none, grad)
            q_side = jnp.concatenate([gap, q_turned[pick]], 0)
            d_side = jnp.concatenate([gap, d_turned[pick]], 0)
        stat = stat_ref[0, 0, head:head + 1, :]
        probs = [jnp.exp(mm(k[...], q_side) - stat) for k in keys]
        weighted = [p * mm(v[...], d_side) for p, v in zip(probs, values)]
        delta = functools.reduce(jnp.add, [jnp.sum(w, 0, keepdims=True) for w in weighted])
        dq = None
        for j in range(blocks):
            ds = (weighted[j] - probs[j] * delta).astype(jnp.bfloat16)
            grad_v = mm(probs[j].astype(jnp.bfloat16), grad_head)
            grad_k = mm(ds, query)
            part = mm(k_turned[j][pick], ds)
            dq = part if dq is None else dq + part
            dv_sum[j] = grad_v if dv_sum[j] is None else dv_sum[j] + grad_v
            dk_sum[j] = grad_k if dk_sum[j] is None else dk_sum[j] + grad_k
        dq_rows.append(dq)
    dq_ref[...] = (jnp.concatenate(dq_rows, 0) * SCALE).T.astype(jnp.bfloat16)
    for j in range(blocks):
        dk[j][...] = dk_sum[j].astype(jnp.bfloat16)
        dv[j][...] = dv_sum[j].astype(jnp.bfloat16)


def attend_back(query, grad, stat, keys, values, clips):
    blocks = len(keys)
    rows = query.shape[0]
    frames = rows // clips
    spec = pl.BlockSpec((frames, 128), lambda c, h: (c, h))
    operands = []
    for k, v in zip(keys, values):
        operands += [k, v]
    shape = jax.ShapeDtypeStruct((rows, D), jnp.bfloat16)
    return pl.pallas_call(
        functools.partial(attend_back_kernel, blocks),
        grid=(clips, HEADS // 2),
        in_specs=[spec, spec, pl.BlockSpec((1, 1, 2, frames), lambda c, h: (c, h, 0, 0))] + [spec] * len(operands),
        out_specs=[spec] * (1 + 2 * blocks),
        out_shape=[shape] * (1 + 2 * blocks),
        compiler_params=pltpu.CompilerParams(vmem_limit_bytes=VMEM, dimension_semantics=("arbitrary", "arbitrary")),
        name="attend_back",
    )(query, grad, stat, *operands)


def count_kernel(draws, n_ref, out_ref):
    length, frames = out_ref.shape[1:]
    place = lax.broadcasted_iota(jnp.int32, (length // 8, 8, frames), 0) * 8 + lax.broadcasted_iota(
        jnp.int32, (length // 8, 8, frames), 1)
    total = jnp.zeros((length // 8, 8, frames), jnp.float32)
    for n in range(draws):
        row = n_ref[0, n:n + 1, :]
        total = total + jnp.where(place == row[None], 1.0, 0.0)
    out_ref[0] = total.reshape(length, frames).astype(jnp.bfloat16)


def count_draws(negatives, length):
    clips, draws, frames = negatives.shape
    tile = 128 if frames % 128 == 0 else frames
    return pl.pallas_call(
        functools.partial(count_kernel, draws),
        grid=(clips, frames // tile),
        in_specs=[pl.BlockSpec((1, draws, tile), lambda c, f: (c, 0, f))],
        out_specs=pl.BlockSpec((1, length, tile), lambda c, f: (c, 0, f)),
        out_shape=jax.ShapeDtypeStruct((clips, length, frames), jnp.bfloat16),
        compiler_params=pltpu.CompilerParams(vmem_limit_bytes=VMEM, dimension_semantics=("arbitrary", "arbitrary")),
        name="count_draws",
    )(negatives)


def swap_moves(count, step):
    return [(i, (i - step) % count) for i in range(count)]


def gather_ring(block):
    count = lax.axis_size("seq")
    return [block] + [lax.ppermute(block, "seq", swap_moves(count, step)) for step in range(1, count)]


def return_ring(blocks):
    count = lax.axis_size("seq")
    return [lax.ppermute(block, "seq", swap_moves(count, -step)) for step, block in enumerate(blocks) if step > 0]


def seq_sum(values):
    if lax.axis_size("seq") > 2:
        return lax.psum(values, "seq").astype(jnp.float32)
    other = lax.ppermute(values, "seq", [(0, 1), (1, 0)])
    return values.astype(jnp.float32) + other.astype(jnp.float32)


def lowered(values):
    return values.astype(jnp.bfloat16)


def bdot(left_side, right_side):
    return jnp.dot(left_side, right_side, preferred_element_type=jnp.float32)


def turned_dot(left_side, right_side):
    return lax.dot_general(left_side, right_side, NT, preferred_element_type=jnp.float32)


def rows_dot(left_side, right_side):
    return lax.dot_general(left_side, right_side, (((0,), (0,)), ((), ())), preferred_element_type=jnp.float32)


def fdot(left_side, right_side):
    return jnp.dot(left_side, right_side, precision=lax.Precision.HIGHEST, preferred_element_type=jnp.float32)


def column_sum(values):
    return jnp.sum(values.astype(jnp.float32), 0)


def gelu_parts(values):
    half = 0.5 * (1.0 + lax.erf(values * 0.5**0.5))
    density = jnp.exp(-0.5 * values * values) * (2.0 * jnp.pi) ** -0.5
    return values * half, half + values * density


def layer_norm(values, gain_row, bias_row):
    centred = values - jnp.mean(values, -1, keepdims=True)
    spread = jnp.mean(centred * centred, -1, keepdims=True)
    return centred * lax.rsqrt(spread + norm_epsilon) * gain_row + bias_row


def unit_rows(values):
    return values * lax.rsqrt(jnp.sum(values * values, -1, keepdims=True) + unit_epsilon)


def vector_pieces(vector):
    widths = [CIN, CIN, D, D, D, D, D] + [D, D, D, D, D, FF, D, D, D] * LAYERS + [PROJ, PROJ]
    pieces = []
    offset = 0
    for width in widths:
        pieces.append(vector[offset : offset + width])
        offset = offset + width
    return pieces


def with_halo(block, width):
    count = lax.axis_size("seq")
    forward = [(i, i + 1) for i in range(count - 1)]
    backward = [(i + 1, i) for i in range(count - 1)]
    low = lax.ppermute(block[:, block.shape[1] - width :], "seq", forward)
    high = lax.ppermute(block[:, :width], "seq", backward)
    return jnp.concatenate([low, block, high], axis=1)


def layer_forward(hidden, attn_w, expand_w, shrink_w, pieces, clip_count):
    q_bias, v_bias, o_bias, gain_one, bias_one, expand_bias, shrink_bias, gain_two, bias_two = pieces
    entries = gather_ring(lowered(hidden))
    query = lowered(bdot(entries[0], attn_w[:, :D]) + q_bias)
    keys = [lowered(bdot(entry, attn_w[:, D : 2 * D])) for entry in entries]
    values = [lowered(bdot(entry, attn_w[:, 2 * D : 3 * D]) + v_bias) for entry in entries]
    mixed, stat = attend(query, keys, values, clip_count)
    branch = bdot(mixed, attn_w[:, 3 * D :]) + o_bias
    middle, middle_pull = jax.vjp(layer_norm, hidden + branch, gain_one, bias_one)
    middle_low = lowered(middle)
    inner = bdot(middle_low, expand_w) + expand_bias
    activated, slope = gelu_parts(inner)
    active_low = lowered(activated)
    slope_low = lowered(slope)
    outer = bdot(active_low, shrink_w) + shrink_bias
    result, final_pull = jax.vjp(layer_norm, middle + outer, gain_two, bias_two)
    cache = (entries, query, keys, values, mixed, stat, middle_pull, middle_low, slope_low, active_low, final_pull)
    return result, cache


def feed_backward(grad_out, cache, expand_w, shrink_w):
    middle_low, slope_low, active_low, final_pull = cache[7:]
    grad_sum, grad_gain, grad_bias = final_pull(grad_out)
    grad_outer = lowered(grad_sum)
    grad_shrink = lowered(rows_dot(active_low, grad_outer))
    grad_inner = lowered(slope_low.astype(jnp.float32) * turned_dot(grad_outer, shrink_w))
    grad_expand = lowered(rows_dot(middle_low, grad_inner))
    grad_middle = grad_sum + turned_dot(grad_inner, expand_w)
    vectors = [column_sum(grad_inner), column_sum(grad_outer), grad_gain, grad_bias]
    return grad_middle, grad_expand, grad_shrink, vectors


def attend_backward(grad_middle, cache, attn_w, clip_count):
    entries, query, keys, values, mixed, stat, middle_pull = cache[:7]
    grad_sum, grad_gain, grad_bias = middle_pull(grad_middle)
    grad_branch = lowered(grad_sum)
    grad_out_proj = lowered(rows_dot(mixed, grad_branch))
    grad_mixed = lowered(turned_dot(grad_branch, attn_w[:, 3 * D :]))
    results = attend_back(query, grad_mixed, stat, keys, values, clip_count)
    grad_query, grad_keys, grad_values = results[0], results[1::2], results[2::2]
    back = [
        turned_dot(dk, attn_w[:, D : 2 * D]) + turned_dot(dv, attn_w[:, 2 * D : 3 * D])
        for dk, dv in zip(grad_keys, grad_values)
    ]
    arrived = return_ring([lowered(block) for block in back])
    grad_hidden = grad_sum + turned_dot(grad_query, attn_w[:, :D]) + back[0]
    for block in arrived:
        grad_hidden = grad_hidden + block.astype(jnp.float32)
    grads = [
        lowered(rows_dot(entries[0], grad_query)),
        lowered(sum(rows_dot(entry, dk) for entry, dk in zip(entries, grad_keys))),
        lowered(sum(rows_dot(entry, dv) for entry, dv in zip(entries, grad_values))),
        grad_out_proj,
    ]
    vectors = [
        column_sum(grad_query),
        sum(column_sum(dv) for dv in grad_values),
        column_sum(grad_branch),
        grad_gain,
        grad_bias,
    ]
    return grad_hidden, grads, vectors


def adam_update(weight, grad, first, second, rate, decay):
    first = beta_one * first + (1 - beta_one) * grad
    second = beta_two * second + (1 - beta_two) * grad * grad
    share_fraction = (
        first / (1 - beta_one**STEP) / (jnp.sqrt(second / (1 - beta_two**STEP)) + adam_epsilon)
    )
    return (weight - rate * (share_fraction + decay * weight), first, second)


def gather_rows(block):
    return lax.all_gather(block, "shard", axis=0, tiled=True)


def scatter_chunks(chunks):
    return lax.psum_scatter(chunks, "shard", scatter_dimension=0, tiled=False)


def trade(chunks):
    return lax.all_to_all(chunks, "shard", split_axis=0, concat_axis=0, tiled=True)


def on_device(
    features,
    time_mask,
    negatives,
    target_codes,
    feature_weight,
    feature_first,
    feature_second,
    conv_weight,
    conv_first,
    conv_second,
    attention_weight,
    attention_first,
    attention_second,
    left_basis_t,
    right_orthogonal_basis,
    expand_weight,
    expand_first,
    expand_second,
    shrink_weight,
    shrink_first,
    shrink_second,
    final_weight,
    final_first,
    final_second,
    target_weight,
    target_first,
    target_second,
    codebook_weight,
    codebook_first,
    codebook_second,
    vector_params,
    vector_first,
    vector_second,
):
    clip_count, frame_count = (features.shape[0], features.shape[1])
    row_count = clip_count * frame_count
    seq_count = lax.axis_size("seq")
    shards = lax.axis_size("shard")
    clip_frames = frame_count * seq_count
    small_items = [feature_weight, final_weight, target_weight, codebook_weight, vector_params]
    small_sizes = [item.size for item in small_items]
    small_total = sum(small_sizes)
    small_width = -(-(small_total + 2) // SMALL_LANES) * SMALL_LANES

    def split_small(flat):
        parts = []
        offset = 0
        for item, size in zip(small_items, small_sizes):
            parts.append(flat[:, offset : offset + size].reshape((-1,) + item.shape[1:]))
            offset = offset + size
        return parts

    small = jnp.concatenate([lowered(item).reshape(-1) for item in small_items])
    small = jnp.pad(small, (0, small_width - small_total))
    small_all = lax.all_gather(small, "shard", axis=0, tiled=False)
    feat_w, final_w, target_w, code_w, vector_low = split_small(small_all)
    conv_w = lax.all_gather(lowered(conv_weight).T, "shard", axis=0, tiled=False)
    attn_w, expand_w, shrink_w = [], [], []
    for layer in range(LAYERS):
        own = lowered(attention_weight[4 * layer : 4 * layer + 4]).transpose(1, 0, 2).reshape(-1, 4 * D)
        attn_w.append(gather_rows(own))
        expand_w.append(gather_rows(lowered(expand_weight[layer])))
        shrink_w.append(gather_rows(lowered(shrink_weight[layer])))
    parts = shards // (4 * LAYERS)
    left_low = trade(jnp.repeat(lowered(left_basis_t), parts, axis=0)).reshape(D, D)

    pieces = vector_pieces(vector_low.astype(jnp.float32))
    mask_on = (time_mask > 0).reshape(row_count, 1)
    feats = features.reshape(row_count, CIN).astype(jnp.float32)
    normed, norm_pull = jax.vjp(layer_norm, feats, pieces[0], pieces[1])
    normed_low = lowered(normed)
    projected = bdot(normed_low, feat_w) + pieces[2]
    masked = jnp.where(mask_on, pieces[3][None, :], projected)
    padded = with_halo(lowered(masked).reshape(clip_count, frame_count, D), KW // 2)
    strip_rows = frame_count * clip_count // 16 // PACK
    strips = to_strips(padded, frame_count)
    conv_out = from_strips(conv_forward(strips, conv_w, strip_rows, shards), clip_count) + pieces[4]
    conv_active, conv_slope = gelu_parts(conv_out)
    hidden, front_pull = jax.vjp(layer_norm, masked + conv_active, pieces[5], pieces[6])

    caches = []
    for layer in range(LAYERS):
        hidden, cache = layer_forward(
            hidden, attn_w[layer], expand_w[layer], shrink_w[layer], pieces[7 + 9 * layer : 16 + 9 * layer], clip_count
        )
        caches.append(cache)
    top_low = lowered(hidden)
    context, context_pull = jax.vjp(unit_rows, bdot(top_low, final_w) + pieces[-2])
    context_low = lowered(context).reshape(clip_count, frame_count, PROJ)

    first_frame = lax.axis_index("seq") * frame_count
    ring_draws = (negatives - first_frame + clip_frames) % clip_frames
    counts = count_draws(ring_draws.transpose(0, 2, 1), clip_frames).astype(jnp.float32)
    codes = jnp.concatenate(gather_ring(target_codes), 1).reshape(clip_count * clip_frames, QGROUPS)
    width = PROJ // QGROUPS
    code_f = code_w.astype(jnp.float32)
    target_f = target_w.astype(jnp.float32)
    table = jnp.concatenate(
        [fdot(code_f[g * width : (g + 1) * width].T, target_f[g * width : (g + 1) * width]) for g in range(QGROUPS)]
    )
    choice = jnp.concatenate(
        [(codes[:, g : g + 1] == jnp.arange(CODES)[None, :]).astype(jnp.float32) for g in range(QGROUPS)], 1
    )
    targets, target_pull = jax.vjp(unit_rows, fdot(choice, table) + pieces[-1])
    targets_low = lowered(targets).reshape(clip_count, clip_frames, PROJ)
    similar = jnp.einsum("clp,cfp->clf", targets_low, context_low, preferred_element_type=jnp.float32)
    logits = similar / contrastive_sharpness
    place = jnp.arange(clip_frames)[:, None] == jnp.arange(frame_count)[None, :]
    own = place.astype(jnp.float32)[None]
    weight = counts + own
    largest = jnp.max(jnp.where(weight > 0, logits, -jnp.inf), 1, keepdims=True)
    power = weight * jnp.exp(jnp.where(weight > 0, logits - largest, 0.0))
    running_totals = jnp.sum(power, 1, keepdims=True)
    mask_as_floats = time_mask.astype(jnp.float32)
    own_logit = jnp.sum(own * logits, 1)
    row_loss = largest[:, 0] + jnp.log(running_totals[:, 0]) - own_logit
    loss_sum = jnp.sum(mask_as_floats * row_loss)
    mask_count = jnp.sum(mask_as_floats)
    derivative_multiplier = 1.0 / (clip_count * shards * clip_frames)
    grad_similar = lowered(
        mask_as_floats[:, None, :]
        * (power / running_totals - own)
        * (derivative_multiplier / contrastive_sharpness)
    )
    grad_context = jnp.einsum("clf,clp->cfp", grad_similar, targets_low, preferred_element_type=jnp.float32)
    grad_targets = jnp.einsum("clf,cfp->clp", grad_similar, context_low, preferred_element_type=jnp.float32)
    (grad_raw,) = target_pull(grad_targets.reshape(-1, PROJ))
    grad_table = fdot(choice.T, grad_raw)
    tables = [grad_table[g * CODES : (g + 1) * CODES] for g in range(QGROUPS)]
    grad_target_w = jnp.concatenate([fdot(code_f[g * width : (g + 1) * width], tables[g]) for g in range(QGROUPS)])
    grad_codebook = jnp.concatenate(
        [fdot(target_f[g * width : (g + 1) * width], tables[g].T) for g in range(QGROUPS)]
    )
    grad_target_bias = column_sum(grad_raw)
    (grad_context_raw,) = context_pull(grad_context.reshape(row_count, PROJ))
    grad_context_low = lowered(grad_context_raw)
    grad_final_w = rows_dot(top_low, grad_context_low)
    grad_final_bias = column_sum(grad_context_low)
    grad_hidden = turned_dot(grad_context_low, final_w)

    attn_grads = [None] * LAYERS
    feed_sums = [None] * LAYERS
    layer_pieces = [None] * LAYERS
    for layer in reversed(range(LAYERS)):
        grad_middle, grad_expand, grad_shrink, feed_vectors = feed_backward(
            grad_hidden, caches[layer], expand_w[layer], shrink_w[layer]
        )
        chunks = jnp.concatenate(
            [grad_expand[:, j * D : (j + 1) * D].reshape(shards, -1, D) for j in range(FF // D)]
            + [grad_shrink.reshape(shards, -1, D)],
            1,
        )
        feed_sums[layer] = seq_sum(scatter_chunks(chunks))
        grad_hidden, attn_grads[layer], attn_vectors = attend_backward(
            grad_middle, caches[layer], attn_w[layer], clip_count
        )
        layer_pieces[layer] = attn_vectors + feed_vectors
    attn_chunks = jnp.stack(attn_grads[0] + attn_grads[1]).reshape(4 * LAYERS, D, parts, D // parts)
    attn_chunks = attn_chunks.transpose(0, 2, 1, 3).reshape(shards, D, D // parts)
    attn_sum = seq_sum(scatter_chunks(attn_chunks))

    grad_sum, grad_gain_enc, grad_bias_enc = front_pull(grad_hidden)
    grad_conv_low = lowered(grad_sum * conv_slope)
    grad_strips = to_strips(with_halo(grad_conv_low.reshape(clip_count, frame_count, D), KW // 2), frame_count)
    grad_back, conv_chunks = conv_backward(strips, grad_strips, conv_w, strip_rows, shards)
    grad_masked = grad_sum + from_strips(grad_back, clip_count)
    grad_embedding = jnp.sum(jnp.where(mask_on, grad_masked, 0.0), 0)
    grad_projected = lowered(jnp.where(mask_on, 0.0, grad_masked))
    grad_feat_w = rows_dot(normed_low, grad_projected)
    _, grad_gain_feat, grad_bias_feat = norm_pull(turned_dot(grad_projected, feat_w))
    vector_grads = [
        grad_gain_feat,
        grad_bias_feat,
        column_sum(grad_projected),
        grad_embedding,
        column_sum(grad_conv_low),
        grad_gain_enc,
        grad_bias_enc,
    ]
    for layer in range(LAYERS):
        vector_grads = vector_grads + layer_pieces[layer]
    vector_grads = jnp.concatenate(vector_grads + [grad_final_bias, grad_target_bias])
    small_grads = [
        lowered(item).reshape(shards, -1)
        for item in (grad_feat_w, grad_final_w, grad_target_w, grad_codebook, vector_grads)
    ]
    loss_tile = jnp.broadcast_to(lowered(jnp.stack([loss_sum, mask_count]))[None], (shards, 2))
    gap = jnp.zeros((shards, small_width - small_total - 2), jnp.bfloat16)
    small_chunks = jnp.concatenate(small_grads + [loss_tile, gap], 1)
    taps = conv_chunks.shape[2]
    last_chunks = jnp.concatenate([conv_chunks, small_chunks.reshape(shards, -1, taps)], 1)
    last_sum = seq_sum(scatter_chunks(last_chunks))
    sum_conv = last_sum[:D].T
    small_sum = last_sum[D:].reshape(1, -1)
    sum_loss = small_sum[0, small_total : small_total + 2]
    sum_feat, sum_final, sum_target, sum_code, sum_vector = split_small(small_sum)

    rows = D // shards
    columns = D // parts

    def to_rows(block):
        shaped = trade(lowered(block).reshape(shards, rows, columns)).reshape(4 * LAYERS, parts, rows, columns)
        return shaped.transpose(0, 2, 1, 3).reshape(4 * LAYERS, rows, D)

    def to_columns(block):
        shaped = lowered(block).reshape(4 * LAYERS, rows, parts, columns).transpose(0, 2, 1, 3)
        return trade(shaped.reshape(shards, rows, columns)).reshape(D, columns)

    right_low = lowered(right_orthogonal_basis)
    left_grad = to_rows(bdot(left_low, lowered(attn_sum)))
    rotated = jnp.einsum("mrd,mde->mre", left_grad, right_low, preferred_element_type=jnp.float32)
    rot_first = beta_rotated * attention_first + (1 - beta_rotated) * rotated
    rot_second = beta_rotated * attention_second + (1 - beta_rotated) * rotated * rotated
    share_fraction = (
        rot_first
        / (1 - beta_rotated**STEP)
        / (jnp.sqrt(rot_second / (1 - beta_rotated**STEP)) + adam_epsilon)
    )
    half_back = jnp.einsum("mre,mde->mrd", lowered(share_fraction), right_low, preferred_element_type=jnp.float32)
    update = to_rows(rows_dot(left_low, to_columns(half_back)))
    new_attention = attention_weight - rate_rotated * update.astype(jnp.float32)

    sum_expand = jnp.stack(
        [s[: -shrink_weight.shape[1]].reshape(FF // D, -1, D).transpose(1, 0, 2).reshape(-1, FF) for s in feed_sums]
    )
    sum_shrink = jnp.stack([s[-shrink_weight.shape[1] :] for s in feed_sums])
    feature_new = adam_update(feature_weight, sum_feat, feature_first, feature_second, rate_matrix, decay_rate)
    conv_new = adam_update(conv_weight, sum_conv, conv_first, conv_second, rate_matrix, decay_rate)
    expand_new = adam_update(expand_weight, sum_expand, expand_first, expand_second, rate_matrix, decay_rate)
    shrink_new = adam_update(shrink_weight, sum_shrink, shrink_first, shrink_second, rate_matrix, decay_rate)
    final_new = adam_update(final_weight, sum_final, final_first, final_second, rate_matrix, decay_rate)
    target_new = adam_update(target_weight, sum_target, target_first, target_second, rate_target, decay_rate)
    codebook_new = adam_update(codebook_weight, sum_code, codebook_first, codebook_second, rate_codebook, decay_rate)
    vector_new = adam_update(vector_params, sum_vector, vector_first, vector_second, rate_vector, 0.0)
    return (
        (sum_loss,)
        + feature_new
        + conv_new
        + (new_attention, rot_first, rot_second)
        + expand_new
        + shrink_new
        + final_new
        + target_new
        + codebook_new
        + vector_new
    )


def solution(mesh):
    return jax.shard_map(
        on_device,
        mesh=mesh,
        in_specs=(
            P("shard", "seq", None),
            P("shard", "seq"),
            P("shard", "seq", None),
            P("shard", "seq", None),
            P("shard", None),
            P("shard", None),
            P("shard", None),
            P("shard", None),
            P("shard", None),
            P("shard", None),
            P(None, "shard", None),
            P(None, "shard", None),
            P(None, "shard", None),
            P(None, "shard", None),
            P(),
            P(None, "shard", None),
            P(None, "shard", None),
            P(None, "shard", None),
            P(None, "shard", None),
            P(None, "shard", None),
            P(None, "shard", None),
            P("shard", None),
            P("shard", None),
            P("shard", None),
            P("shard", None),
            P("shard", None),
            P("shard", None),
            P("shard", None),
            P("shard", None),
            P("shard", None),
            P("shard"),
            P("shard"),
            P("shard"),
        ),
        out_specs=(
            P(),
            P("shard", None),
            P("shard", None),
            P("shard", None),
            P("shard", None),
            P("shard", None),
            P("shard", None),
            P(None, "shard", None),
            P(None, "shard", None),
            P(None, "shard", None),
            P(None, "shard", None),
            P(None, "shard", None),
            P(None, "shard", None),
            P(None, "shard", None),
            P(None, "shard", None),
            P(None, "shard", None),
            P("shard", None),
            P("shard", None),
            P("shard", None),
            P("shard", None),
            P("shard", None),
            P("shard", None),
            P("shard", None),
            P("shard", None),
            P("shard", None),
            P("shard"),
            P("shard"),
            P("shard"),
        ),
        check_vma=False,
    )
```

time: 5990 us -> 1240 us (0.21)
  local copies, waits for them, and re-layouts: 3690 us -> 168 us
  other arithmetic: 632 us -> 95.3 us
  matrix products: 760 us -> 274 us
  blocking collectives: 224 us -> 0 us
  Pallas kernels: 0 us -> 215 us
  waiting for transfers between devices: 574 us -> 383 us
    gather x18 -> x0, local copies, waits for them, and re-layouts: 2710 us -> none  [the longest x12 1800 us: conv_windows(): padded_clip[window_index].reshape(frame_count, KW, GROUPS, D // GROUPS)]
    unnamed x11 -> x10, other arithmetic: 477 us -> 1.53 us
    dot_general x212 -> x19, matrix products: 485 us -> 85.1 us  [bdot(): return jnp.dot(left_side, right_side, preferred_element_type=jnp.float32)]
    while x23 -> x0, local copies, waits for them, and re-layouts: 391 us -> none
    pallas_call x0 -> x7, Pallas kernels: none -> 215 us  [the longest x2 55.6 us: attend_back(): pl.pallas_call(functools.partial(attend_back_kernel, blocks), grid=(clips...]
    reduce_scatter x10 -> x4, waiting for transfers between devices: 334 us -> 137 us  [scatter_chunks(): return lax.psum_scatter(chunks, 'shard', scatter_dimension=0, tiled=False)]
    unnamed x514 -> x498, local copies, waits for them, and re-layouts: 204 us -> 76.2 us
    unnamed x2 -> x0, blocking collectives: 127 us -> none
  transfers between devices with their start and end apart: 29 -> 29, of which waited for: 15 -> 15; matrix products, arithmetic and copies ran while one was open for 54% -> 31% of each run, Pallas kernels for 0% -> 13%
where the time goes in v1:
time: 1240 us; the launch traced here: 1230 us
  waiting for transfers between devices  383 us (31%)
  matrix products  274 us (22%)
  Pallas kernels  215 us (17%)
  local copies, waits for them, and re-layouts  168 us (14%)
  other arithmetic  95.3 us (8%)
  starting transfers between devices  72.2 us (6%)
  between operations  17.4 us (1%)
    reduce_scatter x4, waiting for transfers between devices, scatter_chunks(): return lax.psum_scatter(chunks, 'shard', scatter_dimension=0, tiled=False)  137 us
    all_gather x6, waiting for transfers between devices, gather_rows(): return lax.all_gather(block, 'shard', axis=0, tiled=True)  123 us
    dot_general x19, matrix products, bdot(): return jnp.dot(left_side, right_side, preferred_element_type=jnp.float32)  85.1 us
    unnamed x498, local copies, waits for them, and re-layouts  76.2 us
    dot_general x19, matrix products, rows_dot(): lax.dot_general(left_side, right_side, (((0,), (0,)), ((), ())), preferre...  68.2 us
    dot_general x18, matrix products, turned_dot(): lax.dot_general(left_side, right_side, NT, preferred_element_type=jnp.flo...  67.6 us
    pallas_call x2, Pallas kernels, attend_back(): pl.pallas_call(functools.partial(attend_back_kernel, blocks), grid=(clips...  55.6 us
    pallas_call x1, Pallas kernels, conv_backward(): pl.pallas_call(functools.partial(conv_backward_kernel, rows, shards), gri...  55.2 us
  transfers between devices with their start and end apart: 29, of which 15 were waited for; matrix products, arithmetic and copies ran while one was open for 31% of the time, Pallas kernels for 13%

profile of v1, /device:TPU:0, one launch (start us, length us, event | category | flops | bytes accessed | tf_op | source)
XLA Modules:
  0.0 1225.5 jit_solution(9426163170861815199)
XLA Ops:
  29.3 28.1 %count_draws.1 = bf16[2,768,384]{2,1,0:T(8,128)(2,1)} custom-call(s32[2,100,384]{2,1,0:T(8,128)} %fusion.135.n_ref), custom_call_target="tpu_custom_call" | custom-call | tf_op jit(solution)/shard_map/count_draws/pallas_call | solution.py:352
  81.1 6.3 collective-permute-start
  88.4 5.0 multiply_reduce_fusion.17
  98.5 5.7 copy.157
  104.2 38.1 %all-gather.20.cloned.1.call-done = bf16[12288,384]{0,1:T(8,128)(2,1)} async-done(((bf16[768,384]{0,1:T(8,128)(2,1)}), bf16[12288,384]{0,1:T(8,128)(2,1)}) %all-gather.20.cloned.1.call-update) | async-done | bytes 9437200 | tf_op jit(solution)/shard_map/all_gather | solution.py:585
  142.3 12.7 %copy.116 = bf16[12288,384]{1,0:T(8,128)(2,1)} copy(bf16[12288,384]{0,1:T(8,128)(2,1)} %all-gather.20.cloned.1.call-done) | data formatting | bytes 18874368 | tf_op jit(solution)/shard_map/all_gather | solution.py:585
  155.0 39.0 %conv_forward.1 = f32[48,16,1024]{2,1,0:T(8,128)} custom-call(bf16[176,16,1024]{2,1,0:T(8,128)(2,1)} %bitcast.385, bf16[16,768,384]{2,1,0:T(8,128)(2,1)} %bitcast.383), custom_call_target="tpu_custom_call" | custom-call | tf_op jit(solution)/shard_map/conv_forward/pallas_call | solution.py:119
  194.0 3.8 copy.117
  201.7 3.7 fusion.194
  209.0 3.9 convolution_convert_fusion.15.refs_0_
  219.7 16.2 %collective-permute-done.3 = bf16[768,768]{1,0:T(8,128)(2,1)} collective-permute-done((bf16[768,768]{1,0:T(8,128)(2,1)}, bf16[768,768]{1,0:T(8,128)(2,1)}, u32[]{:S(2)}, u32[]{:S(2)}) %collective-permute-start.3) | collective-permute-done | bytes 1179680 | tf_op jit(solution)/shard_map/ppermute | solution.py:369
  242.6 18.6 %attend.2 = (bf16[768,768]{1,0:T(8,128)(2,1)}, f32[2,6,2,384]{3,2,1,0:T(2,128)}) custom-call(bf16[768,768]{1,0:T(8,128)(2,1)} %add_convert_fusion.12.q_ref, bf16[768,768]{1,0:T(8,128)(2,1)} %convolution_convert_fusion.15.refs_0_, bf16[768,768]{1,0:T(8,128)(2,1)} %add_convert_fusion.11.refs_1_, bf16[768,768]{1,0:T(8,128)(2,1)} %convolution_convert_fusion.14.refs_2_, ...), custom_call_target="tpu_custom_call" | custom-call | tf_op jit(solution)/shard_map/attend/pallas_call | solution.py:256
  265.9 10.9 multiply_convert_fusion.3
  276.8 29.8 %all-gather.24.cloned.1.call-done = bf16[1,3072,768]{2,1,0:T(8,128)(2,1)} async-done(((bf16[1,192,768]{2,1,0:T(8,128)(2,1)}), bf16[1,3072,768]{2,1,0:T(8,128)(2,1)}) %all-gather.24.cloned.1.call-update) | async-done | bytes 4718608 | tf_op jit(solution)/shard_map/all_gather | solution.py:517
  306.7 8.5 fusion.211
  324.0 37.3 %all-gather.18.cloned.1.call-done = bf16[768,3072]{1,0:T(8,128)(2,1)} async-done(((bf16[48,3072]{1,0:T(8,128)(2,1)}), bf16[768,3072]{1,0:T(8,128)(2,1)}) %all-gather.18.cloned.1.call-update) | async-done | bytes 4718608 | tf_op jit(solution)/shard_map/all_gather | solution.py:517
  361.3 3.9 convolution_convert_fusion.13.refs_0_
  378.8 18.6 %attend.3 = (bf16[768,768]{1,0:T(8,128)(2,1)}, f32[2,6,2,384]{3,2,1,0:T(2,128)}) custom-call(bf16[768,768]{1,0:T(8,128)(2,1)} %add_convert_fusion.9.q_ref, bf16[768,768]{1,0:T(8,128)(2,1)} %convolution_convert_fusion.13.refs_0_, bf16[768,768]{1,0:T(8,128)(2,1)} %add_convert_fusion.8.refs_1_, bf16[768,768]{1,0:T(8,128)(2,1)} %convolution_convert_fusion.12.refs_2_, ...), custom_call_target="tpu_custom_call" | custom-call | tf_op jit(solution)/shard_map/attend/pallas_call | solution.py:256
  403.0 12.5 %all-gather.26.cloned.1.call-done = bf16[1,768,3072]{2,1,0:T(8,128)(2,1)} async-done(((bf16[1,48,3072]{2,1,0:T(8,128)(2,1)}), bf16[1,768,3072]{2,1,0:T(8,128)(2,1)}) %all-gather.26.cloned.1.call-update) | async-done | bytes 4718608 | tf_op jit(solution)/shard_map/all_gather | solution.py:517
  415.6 10.9 multiply_convert_fusion.2
  426.5 43.4 %all-gather.28.cloned.1.call-done = bf16[1,3072,768]{2,1,0:T(8,128)(2,1)} async-done(((bf16[1,192,768]{2,1,0:T(8,128)(2,1)}), bf16[1,3072,768]{2,1,0:T(8,128)(2,1)}) %all-gather.28.cloned.1.call-update) | async-done | bytes 4718608 | tf_op jit(solution)/shard_map/all_gather | solution.py:517
  469.8 8.5 fusion.213
  490.9 11.0 fusion.215
  501.9 4.9 multiply_reduce_fusion.2
  508.5 3.9 convolution_convert_fusion.11.d_ref
  512.4 27.9 %attend_back.2 = (bf16[768,768]{1,0:T(8,128)(2,1)}, bf16[768,768]{1,0:T(8,128)(2,1)}, bf16[768,768]{1,0:T(8,128)(2,1)}, bf16[768,768]{1,0:T(8,128)(2,1)}, bf16[768,768]{1,0:T(8,128)(2,1)}) custom-call(bf16[768,768]{1,0:T(8,128)(2,1)} %add_convert_fusion.9.q_ref, bf16[768,768]{1,0:T(8,128)(2,1)} %convolution_convert_fusion.11.d_ref, ...), custom_call_target="tpu_custom_call" | custom-call | tf_op jit(solution)/shard_map/attend_back/pallas_call | solution.py:327
  547.3 4.0 fusion.222
  551.2 3.8 fusion.223
  557.5 16.4 %collective-permute-done.5 = bf16[768,768]{1,0:T(8,128)(2,1)S(1)} collective-permute-done((bf16[768,768]{1,0:T(8,128)(2,1)S(1)}, bf16[768,768]{1,0:T(8,128)(2,1)S(1)}, u32[]{:S(2)}, u32[]{:S(2)}) %collective-permute-start.5) | collective-permute-done | bytes 1179680 | tf_op jit(solution)/shard_map/ppermute | solution.py:374
  578.6 10.4 fusion.214
  589.1 5.0 multiply_reduce_fusion.4
  599.2 27.7 %attend_back.3 = (bf16[768,768]{1,0:T(8,128)(2,1)}, bf16[768,768]{1,0:T(8,128)(2,1)}, bf16[768,768]{1,0:T(8,128)(2,1)}, bf16[768,768]{1,0:T(8,128)(2,1)}, bf16[768,768]{1,0:T(8,128)(2,1)}) custom-call(bf16[768,768]{1,0:T(8,128)(2,1)} %add_convert_fusion.12.q_ref, bf16[768,768]{1,0:T(8,128)(2,1)} %convolution_convert_fusion.10.d_ref, ...), custom_call_target="tpu_custom_call" | custom-call | tf_op jit(solution)/shard_map/attend_back/pallas_call | solution.py:327
  626.9 3.9 fusion.61
  635.8 3.6 fusion.53
  648.8 3.7 fusion.57
  652.4 3.6 fusion.59
  658.3 7.1 fusion.195
  665.4 8.8 pad_maximum_fusion.1
  674.9 7.3 convolution_convert_fusion.1
  687.0 4.3 convolution_convert_fusion
  706.7 3.9 fusion.112
  731.1 3.6 add_convert_fusion.4
  736.3 7.1 convolution_convert_fusion.3
  748.2 4.3 convolution_convert_fusion.2
  763.6 4.4 multiply_reduce_fusion.5
  773.0 5.0 collective-permute-start.7
  783.5 5.7 copy.156
  789.1 55.2 %conv_backward.1 = (f32[48,16,1024]{2,1,0:T(8,128)}, bf16[16,768,384]{2,1,0:T(8,128)(2,1)}) custom-call(bf16[176,16,1024]{2,1,0:T(8,128)(2,1)} %bitcast.386, bf16[176,16,1024]{2,1,0:T(8,128)(2,1)} %bitcast.388, bf16[16,768,384]{2,1,0:T(8,128)(2,1)} %bitcast.384), custom_call_target="tpu_custom_call" | custom-call | tf_op jit(solution)/shard_map/conv_backward/pallas_call | solution.py:169
  844.4 3.7 copy.122
  901.4 9.2 pad_maximum_fusion
  913.1 3.7 all-to-all-start
  919.7 26.3 %all-to-all-done = bf16[16,48,768]{2,1,0:T(8,128)(2,1)S(1)} async-done(((bf16[16,48,768]{2,1,0:T(8,128)(2,1)}), bf16[16,48,768]{2,1,0:T(8,128)(2,1)S(1)}, u32[]{:S(2)}, u32[]{:S(2)}) %all-to-all-start) | async-done | bytes 1179680 | tf_op jit(solution)/shard_map/all_to_all | solution.py:525
  949.3 21.3 %all-to-all-start.1 = ((bf16[16,48,384]{2,1,0:T(8,128)(2,1)}), bf16[16,48,384]{2,1,0:T(8,128)(2,1)S(1)}, u32[]{:S(2)}, u32[]{:S(2)}) async-start(bf16[16,48,384]{2,1,0:T(8,128)(2,1)} %bitcast.65), calls=%async_computation.3 | async-start | bytes 1179648 | tf_op jit(solution)/shard_map/all_to_all | solution.py:525
  978.0 57.6 %reduce-scatter.9.cloned.1.call-done = bf16[1,384,768]{2,1,0:T(8,128)(2,1)} async-done(((bf16[16,384,768]{2,1,0:T(8,128)(2,1)}), bf16[1,384,768]{2,1,0:T(8,128)(2,1)}) %reduce-scatter.9.cloned.1.call-update) | async-done | bytes 589840 | tf_op jit(solution)/shard_map/reduce_scatter | solution.py:521
  1037.9 8.9 multiply_add_fusion.5
  1046.8 12.5 %fusion.69 = bf16[8,48,768]{2,1,0:T(8,128)(2,1)S(1)} fusion(f32[8,768,768]{2,1,0:T(8,128)} %param.47, f32[8,48,768]{2,1,0:T(8,128)S(1)} %get-tuple-element.242, f32[8,48,768]{2,1,0:T(8,128)S(1)} %get-tuple-element.241), kind=kOutput, calls=%fused_computation.186 | convolution fusion | flops 459472896 | bytes 21823488 | tf_op jit(solution)/shard_map/mre,mde->mrd/dot_general | solution.py:747
  1060.3 4.5 all-to-all-start.2
  1069.3 13.5 %all-to-all-done.2 = bf16[16,48,384]{2,1,0:T(8,128)(2,1)S(1)} async-done(((bf16[16,48,384]{2,1,0:T(8,128)(2,1)}), bf16[16,48,384]{2,1,0:T(8,128)(2,1)S(1)}, u32[]{:S(2)}, u32[]{:S(2)}) %all-to-all-start.2) | async-done | bytes 589856 | tf_op jit(solution)/shard_map/all_to_all | solution.py:525
  1085.8 13.3 %all-to-all-start.3 = ((bf16[16,48,384]{2,1,0:T(8,128)(2,1)}), bf16[16,48,384]{2,1,0:T(8,128)(2,1)}, u32[]{:S(2)}, u32[]{:S(2)}) async-start(bf16[16,48,384]{2,1,0:T(8,128)(2,1)} %bitcast.71), calls=%async_computation.5 | async-start | bytes 1179648 | tf_op jit(solution)/shard_map/all_to_all | solution.py:525
  1099.1 4.5 multiply_subtract_fusion.1
  1103.6 79.2 %reduce-scatter.5.cloned.1.call-done = bf16[1,892,384]{2,1,0:T(8,128)(2,1)} async-done(((bf16[16,892,384]{2,1,0:T(8,128)(2,1)}), bf16[1,892,384]{2,1,0:T(8,128)(2,1)}) %reduce-scatter.5.cloned.1.call-update) | async-done | bytes 685072 | tf_op jit(solution)/shard_map/reduce_scatter | solution.py:521
  1184.3 4.3 multiply_subtract_fusion
  1191.2 8.9 collective-permute-done.9
  1205.2 4.0 multiply_subtract_fusion.2
  (779 shorter events, 321.0 us)
Async XLA Ops:
  7.2 52.8 %all-gather.30.cloned.1.call-start = ((), (), s32[]{:S(2)}) async-start(), calls=%async_computation.19 | async-start | bytes 3237888 | tf_op jit(solution)/shard_map/all_gather | solution.py:583
  12.3 130.0 %all-gather.20.cloned.1.call-start = ((), (), s32[]{:S(2)}) async-start(), calls=%async_computation.14 | async-start | bytes 10027008 | tf_op jit(solution)/shard_map/all_gather | solution.py:585
  14.5 194.5 %all-gather.16.cloned.1.call-start = ((), (), s32[]{:S(2)}) async-start(), calls=%async_computation.8 | async-start | bytes 5013504 | tf_op jit(solution)/shard_map/all_gather | solution.py:517
  15.4 250.4 %all-gather.22.cloned.1.call-start = ((), (), s32[]{:S(2)}) async-start(), calls=%async_computation.15 | async-start | bytes 5013504 | tf_op jit(solution)/shard_map/all_gather | solution.py:517
  16.8 289.9 %all-gather.24.cloned.1.call-start = ((), (), s32[]{:S(2)}) async-start(), calls=%async_computation.16 | async-start | bytes 5013504 | tf_op jit(solution)/shard_map/all_gather | solution.py:517
  17.8 343.5 %all-gather.18.cloned.1.call-start = ((), (), s32[]{:S(2)}) async-start(), calls=%async_computation.9 | async-start | bytes 5013504 | tf_op jit(solution)/shard_map/all_gather | solution.py:517
  18.6 397.0 %all-gather.26.cloned.1.call-start = ((), (), s32[]{:S(2)}) async-start(), calls=%async_computation.17 | async-start | bytes 5013504 | tf_op jit(solution)/shard_map/all_gather | solution.py:517
  19.4 450.5 %all-gather.28.cloned.1.call-start = ((), (), s32[]{:S(2)}) async-start(), calls=%async_computation.18 | async-start | bytes 5013504 | tf_op jit(solution)/shard_map/all_gather | solution.py:517
  19.4 38.0 %collective-permute-start.2 = (s32[2,384,2]{1,2,0:T(2,128)S(1)}, s32[2,384,2]{1,2,0:T(2,128)S(1)}, u32[]{:S(2)}, u32[]{:S(2)}) collective-permute-start(s32[2,384,2]{1,2,0:T(2,128)S(1)} %copy-done.157), channel_id=1, source_target_pairs={{0,16},{16,0},{1,17},{17,1},{2,18},{18,2},{3,19},{19,3},{4,20},{20... | collective-permute-start | bytes 18440 | tf_op jit(solution)/shard_map/ppermute | solution.py:369
  22.5 894.4 %reduce-scatter.7.cloned.1.call-start = ((), (), s32[]{:S(2)}) async-start(), calls=%async_computation.11 | async-start | bytes 10027008 | tf_op jit(solution)/shard_map/reduce_scatter | solution.py:521
  62.0 13.6 %copy-start.15 = (bf16[16,1,47616]{2,0,1:T(8,128)(2,1)}, bf16[16,1,47616]{2,0,1:T(8,128)(2,1)S(1)}, u32[]{:S(2)}) copy-start(bf16[16,1,47616]{2,0,1:T(8,128)(2,1)S(1)} %copy.158) | copy-start | bytes 4571140
  75.6 11.8 copy-start.74
  75.7 12.0 copy-start.78
  75.7 12.0 copy-start.73
  79.8 15.0 %collective-permute-start.1 = (bf16[2,64,768]{2,1,0:T(8,128)(2,1)}, bf16[2,64,768]{2,1,0:T(8,128)(2,1)}, u32[]{:S(2)}, u32[]{:S(2)}) collective-permute-start(bf16[2,64,768]{2,1,0:T(8,128)(2,1)} %get-tuple-element.246), channel_id=1, source_target_pairs={{16,0},{17,1},{18,2},{19,3},{20,4},{21,5},{22,6},{23,7},{24,8},{25... | collective-permute-start | bytes 589832 | tf_op jit(solution)/shard_map/ppermute | solution.py:439
  81.1 13.7 %collective-permute-start = (bf16[2,64,768]{2,1,0:T(8,128)(2,1)}, bf16[2,64,768]{2,1,0:T(8,128)(2,1)}, u32[]{:S(2)}, u32[]{:S(2)}) collective-permute-start(bf16[2,64,768]{2,1,0:T(8,128)(2,1)} %get-tuple-element.245), channel_id=1, source_target_pairs={{0,16},{1,17},{2,18},{3,19},{4,20},{5,21},{6,22},{7,23},{8,24},{9,... | collective-permute-start | bytes 589832 | tf_op jit(solution)/shard_map/ppermute | solution.py:438
  205.4 55.9 %copy-start = (f32[768,768]{1,0:T(8,128)}, f32[768,768]{1,0:T(8,128)S(1)}, u32[]{:S(2)}) copy-start(f32[768,768]{1,0:T(8,128)S(1)} %get-tuple-element.218) | copy-start | bytes 7077892
  205.4 55.8 %copy-start.81 = (f32[768]{0:T(1024)}, f32[768]{0:T(1024)S(1)}, u32[]{:S(2)}) copy-start(f32[768]{0:T(1024)S(1)} %broadcast_multiply_fusion.4) | copy-start | bytes 9220
  207.5 28.4 %collective-permute-start.3 = (bf16[768,768]{1,0:T(8,128)(2,1)}, bf16[768,768]{1,0:T(8,128)(2,1)}, u32[]{:S(2)}, u32[]{:S(2)}) collective-permute-start(bf16[768,768]{1,0:T(8,128)(2,1)} %fusion.38), channel_id=1, source_target_pairs={{0,16},{16,0},{1,17},{17,1},{2,18},{18,2},{3,19},{19,3},{4,20},{20... | collective-permute-start | bytes 3538952 | tf_op jit(solution)/shard_map/ppermute | solution.py:369
  209.0 110.2 %copy-start.87 = (f32[1536]{0:T(1024)}, f32[1536]{0:T(1024)S(1)}, u32[]{:S(2)}) copy-start(f32[1536]{0:T(1024)S(1)} %add_rsqrt_fusion) | copy-start | bytes 18436
  242.6 18.6 %copy-start.95 = (f32[768]{0:T(1024)S(1)}, f32[768]{0:T(1024)}, u32[]{:S(2)}) copy-start(f32[768]{0:T(1024)} %copy-done.94) | copy-start | bytes 9220
  242.6 18.6 %copy-start.134 = (f32[768]{0:T(1024)S(1)}, f32[768]{0:T(1024)}, u32[]{:S(2)}) copy-start(f32[768]{0:T(1024)} %get-tuple-element.274) | copy-start | bytes 9220
  242.6 18.6 %copy-start.164 = (f32[768]{0:T(1024)S(1)}, f32[768]{0:T(1024)}, u32[]{:S(2)}) copy-start(f32[768]{0:T(1024)} %get-tuple-element.271) | copy-start | bytes 9220
  264.0 42.7 %copy-start.103 = (f32[768]{0:T(1024)}, f32[768]{0:T(1024)S(1)}, u32[]{:S(2)}) copy-start(f32[768]{0:T(1024)S(1)} %broadcast_multiply_fusion.3) | copy-start | bytes 9220
  317.7 54.3 %collective-permute-start.4 = (bf16[768,768]{1,0:T(8,128)(2,1)}, bf16[768,768]{1,0:T(8,128)(2,1)}, u32[]{:S(2)}, u32[]{:S(2)}) collective-permute-start(bf16[768,768]{1,0:T(8,128)(2,1)} %fusion.40), channel_id=1, source_target_pairs={{0,16},{16,0},{1,17},{17,1},{2,18},{18,2},{3,19},{19,3},{4,20},{20... | collective-permute-start | bytes 3538952 | tf_op jit(solution)/shard_map/ppermute | solution.py:369
  324.0 41.2 %copy-start.163 = (f32[768]{0:T(1024)S(1)}, f32[768]{0:T(1024)}, u32[]{:S(2)}) copy-start(f32[768]{0:T(1024)} %get-tuple-element.265) | copy-start | bytes 9220
  378.8 18.6 %copy-start.98 = (f32[768]{0:T(1024)S(1)}, f32[768]{0:T(1024)}, u32[]{:S(2)}) copy-start(f32[768]{0:T(1024)} %copy-done.97) | copy-start | bytes 9220
  378.8 18.6 %copy-start.132 = (f32[768]{0:T(1024)S(1)}, f32[768]{0:T(1024)}, u32[]{:S(2)}) copy-start(f32[768]{0:T(1024)} %get-tuple-element.266) | copy-start | bytes 9220
  378.8 18.6 %copy-start.161 = (f32[768]{0:T(1024)S(1)}, f32[768]{0:T(1024)}, u32[]{:S(2)}) copy-start(f32[768]{0:T(1024)} %get-tuple-element.263) | copy-start | bytes 9220
  400.0 69.8 %copy-start.105 = (f32[768]{0:T(1024)}, f32[768]{0:T(1024)S(1)}, u32[]{:S(2)}) copy-start(f32[768]{0:T(1024)S(1)} %broadcast_multiply_fusion.1) | copy-start | bytes 9220
  489.4 12.4 %slice-start.6 = ((s8[4718592]{0:T(1024)(128)(4,1)}), s8[4194304]{0:T(1024)(128)(4,1)S(1)}, s32[]{:S(2)}) async-start(s8[4718592]{0:T(1024)(128)(4,1)} %bitcast.460), calls=%async_computation.26 | async-start | bytes 8388608
  543.2 11.9 slice-start
  545.7 28.2 %collective-permute-start.5 = (bf16[768,768]{1,0:T(8,128)(2,1)S(1)}, bf16[768,768]{1,0:T(8,128)(2,1)S(1)}, u32[]{:S(2)}, u32[]{:S(2)}) collective-permute-start(bf16[768,768]{1,0:T(8,128)(2,1)S(1)} %add_convert_fusion.5), channel_id=1, source_target_pairs={{0,16},{16,0},{1,17},{17,1},{2,18},{18,2},{3,19},{19,3},{4,20},{20... | collective-permute-start | bytes 3538952 | tf_op jit(solution)/shard_map/ppermute | solution.py:374
  556.4 22.0 %slice-start.4 = ((s8[4718592]{0:T(1024)(128)(4,1)}), s8[4194304]{0:T(1024)(128)(4,1)S(1)}, s32[]{:S(2)}) async-start(s8[4718592]{0:T(1024)(128)(4,1)} %bitcast.458), calls=%async_computation.24 | async-start | bytes 8388608
  557.5 19.1 %copy-start.113 = (f32[768]{0:T(1024)S(1)}, f32[768]{0:T(1024)}, u32[]{:S(2)}) copy-start(f32[768]{0:T(1024)} %copy-done.112) | copy-start | bytes 9220
  557.5 20.9 %slice-start.5 = ((s8[4718592]{0:T(1024)(128)(4,1)}), s8[524288]{0:T(1024)(128)(4,1)S(1)}, s32[]{:S(2)}) async-start(s8[4718592]{0:T(1024)(128)(4,1)} %bitcast.458), calls=%async_computation.25 | async-start | bytes 1048576
  576.6 12.4 %slice-start.2 = ((s8[4718592]{0:T(1024)(128)(4,1)}), s8[4194304]{0:T(1024)(128)(4,1)S(1)}, s32[]{:S(2)}) async-start(s8[4718592]{0:T(1024)(128)(4,1)} %bitcast.456), calls=%async_computation.22 | async-start | bytes 8388608
  674.2 245.5 %reduce-scatter.11.cloned.1.call-start = ((), (), s32[]{:S(2)}) async-start(), calls=%async_computation.13 | async-start | bytes 10027008 | tf_op jit(solution)/shard_map/reduce_scatter | solution.py:521
  694.0 341.6 %reduce-scatter.9.cloned.1.call-start = ((), (), s32[]{:S(2)}) async-start(), calls=%async_computation.12 | async-start | bytes 10027008 | tf_op jit(solution)/shard_map/reduce_scatter | solution.py:521
  710.6 13.4 %copy-start.17 = (bf16[768,768]{1,0:T(8,128)(2,1)S(1)}, bf16[768,768]{1,0:T(8,128)(2,1)}, u32[]{:S(2)}) copy-start(bf16[768,768]{1,0:T(8,128)(2,1)} %get-tuple-element.49) | copy-start | bytes 3538948
  734.7 28.9 %collective-permute-start.6 = (bf16[768,768]{1,0:T(8,128)(2,1)}, bf16[768,768]{1,0:T(8,128)(2,1)}, u32[]{:S(2)}, u32[]{:S(2)}) collective-permute-start(bf16[768,768]{1,0:T(8,128)(2,1)} %add_convert_fusion.4), channel_id=1, source_target_pairs={{0,16},{16,0},{1,17},{17,1},{2,18},{18,2},{3,19},{19,3},{4,20},{20... | collective-permute-start | bytes 3538952 | tf_op jit(solution)/shard_map/ppermute | solution.py:374
  755.1 427.7 %reduce-scatter.5.cloned.1.call-start = ((), (), s32[]{:S(2)}) async-start(), calls=%async_computation.10 | async-start | bytes 11698176 | tf_op jit(solution)/shard_map/reduce_scatter | solution.py:521
  771.7 7.7 collective-permute-start.8
  773.0 7.7 collective-permute-start.7
  857.5 34.1 %copy-start.154 = (bf16[768]{0:T(1024)(128)(2,1)S(1)}, bf16[768]{0:T(1024)(128)(2,1)}, u32[]{:S(2)}) copy-start(bf16[768]{0:T(1024)(128)(2,1)} %get-tuple-element.195) | copy-start | bytes 4612
  857.5 35.5 %copy-start.153 = (bf16[768]{0:T(1024)(128)(2,1)S(1)}, bf16[768]{0:T(1024)(128)(2,1)}, u32[]{:S(2)}) copy-start(bf16[768]{0:T(1024)(128)(2,1)} %get-tuple-element.144) | copy-start | bytes 4612
  857.5 36.9 %copy-start.152 = (bf16[768]{0:T(1024)(128)(2,1)S(1)}, bf16[768]{0:T(1024)(128)(2,1)}, u32[]{:S(2)}) copy-start(bf16[768]{0:T(1024)(128)(2,1)} %get-tuple-element.156) | copy-start | bytes 4612
  859.0 40.5 %copy-start.37 = (bf16[16,12288]{1,0:T(8,128)(2,1)S(1)}, bf16[16,12288]{1,0:T(8,128)(2,1)}, u32[]{:S(2)}) copy-start(bf16[16,12288]{1,0:T(8,128)(2,1)} %reshape.570) | copy-start | bytes 1179652
  864.3 35.3 %copy-start.70 = (bf16[16,4096]{1,0:T(8,128)(2,1)S(1)}, bf16[16,4096]{1,0:T(8,128)(2,1)}, u32[]{:S(2)}) copy-start(bf16[16,4096]{1,0:T(8,128)(2,1)} %convert_element_type.457) | copy-start | bytes 393220
  864.3 35.3 %copy-start.62 = (bf16[16,5120]{1,0:T(8,128)(2,1)S(1)}, bf16[16,5120]{1,0:T(8,128)(2,1)}, u32[]{:S(2)}) copy-start(bf16[16,5120]{1,0:T(8,128)(2,1)} %convert_element_type.458) | copy-start | bytes 491524
  864.3 35.8 %copy-start.186 = (bf16[2]{0:T(256)(128)(2,1)S(1)}, bf16[2]{0:T(256)(128)(2,1)}, u32[]{:S(2)}) copy-start(bf16[2]{0:T(256)(128)(2,1)} %pad_maximum_fusion.8) | copy-start | bytes 16
  913.1 32.9 %all-to-all-start = ((bf16[16,48,768]{2,1,0:T(8,128)(2,1)}), bf16[16,48,768]{2,1,0:T(8,128)(2,1)S(1)}, u32[]{:S(2)}, u32[]{:S(2)}) async-start(bf16[16,48,768]{2,1,0:T(8,128)(2,1)} %bitcast.62), calls=%async_computation.2 | async-start | bytes 2359296 | tf_op jit(solution)/shard_map/all_to_all | solution.py:525
  916.9 29.1 %collective-permute-start.10 = (bf16[768,384]{1,0:T(8,128)(2,1)}, bf16[768,384]{1,0:T(8,128)(2,1)S(1)}, u32[]{:S(2)}, u32[]{:S(2)}) collective-permute-start(bf16[768,384]{1,0:T(8,128)(2,1)} %bitcast.464), channel_id=1, source_target_pairs={{0,16},{16,0},{1,17},{17,1},{2,18},{18,2},{3,19},{19,3},{4,20},{20... | collective-permute-start | bytes 1769480 | tf_op jit(solution)/shard_map/ppermute | solution.py:380
  919.7 55.5 %collective-permute-start.12 = (bf16[384,768]{1,0:T(8,128)(2,1)}, bf16[384,768]{1,0:T(8,128)(2,1)}, u32[]{:S(2)}, u32[]{:S(2)}) collective-permute-start(bf16[384,768]{1,0:T(8,128)(2,1)} %bitcast.449), channel_id=1, source_target_pairs={{0,16},{16,0},{1,17},{17,1},{2,18},{18,2},{3,19},{19,3},{4,20},{20... | collective-permute-start | bytes 1769480 | tf_op jit(solution)/shard_map/ppermute | solution.py:380
  946.0 24.6 %copy-start.23 = (f32[384,768]{1,0:T(8,128)S(1)}, f32[384,768]{1,0:T(8,128)}, u32[]{:S(2)}) copy-start(f32[384,768]{1,0:T(8,128)} %param.40) | copy-start | bytes 3538948
  949.3 87.8 %all-to-all-start.1 = ((bf16[16,48,384]{2,1,0:T(8,128)(2,1)}), bf16[16,48,384]{2,1,0:T(8,128)(2,1)S(1)}, u32[]{:S(2)}, u32[]{:S(2)}) async-start(bf16[16,48,384]{2,1,0:T(8,128)(2,1)} %bitcast.65), calls=%async_computation.3 | async-start | bytes 1179648 | tf_op jit(solution)/shard_map/all_to_all | solution.py:525
  1035.6 29.2 %collective-permute-start.11 = (bf16[384,768]{1,0:T(8,128)(2,1)}, bf16[384,768]{1,0:T(8,128)(2,1)}, u32[]{:S(2)}, u32[]{:S(2)}) collective-permute-start(bf16[384,768]{1,0:T(8,128)(2,1)} %bitcast.450), channel_id=1, source_target_pairs={{0,16},{16,0},{1,17},{17,1},{2,18},{18,2},{3,19},{19,3},{4,20},{20... | collective-permute-start | bytes 1769480 | tf_op jit(solution)/shard_map/ppermute | solution.py:380
  1046.8 12.5 %copy-start.30 = (f32[8,48,768]{2,1,0:T(8,128)}, f32[8,48,768]{2,1,0:T(8,128)S(1)}, u32[]{:S(2)}) copy-start(f32[8,48,768]{2,1,0:T(8,128)S(1)} %get-tuple-element.241) | copy-start | bytes 3538948
  1046.8 12.5 %copy-start.31 = (f32[8,48,768]{2,1,0:T(8,128)}, f32[8,48,768]{2,1,0:T(8,128)S(1)}, u32[]{:S(2)}) copy-start(f32[8,48,768]{2,1,0:T(8,128)S(1)} %get-tuple-element.242) | copy-start | bytes 3538948
  1060.3 22.5 %all-to-all-start.2 = ((bf16[16,48,384]{2,1,0:T(8,128)(2,1)}), bf16[16,48,384]{2,1,0:T(8,128)(2,1)S(1)}, u32[]{:S(2)}, u32[]{:S(2)}) async-start(bf16[16,48,384]{2,1,0:T(8,128)(2,1)} %bitcast.68), calls=%async_computation.4 | async-start | bytes 1179648 | tf_op jit(solution)/shard_map/all_to_all | solution.py:525
  1084.7 14.4 %copy-start.25 = (f32[2,48,3072]{2,1,0:T(8,128)S(1)}, f32[2,48,3072]{2,1,0:T(8,128)}, u32[]{:S(2)}) copy-start(f32[2,48,3072]{2,1,0:T(8,128)} %param.48) | copy-start | bytes 3538948
  1085.8 102.8 %all-to-all-start.3 = ((bf16[16,48,384]{2,1,0:T(8,128)(2,1)}), bf16[16,48,384]{2,1,0:T(8,128)(2,1)}, u32[]{:S(2)}, u32[]{:S(2)}) async-start(bf16[16,48,384]{2,1,0:T(8,128)(2,1)} %bitcast.71), calls=%async_computation.5 | async-start | bytes 1179648 | tf_op jit(solution)/shard_map/all_to_all | solution.py:525
  1099.1 85.2 %copy-start.27 = (f32[2,192,768]{2,1,0:T(8,128)S(1)}, f32[2,192,768]{2,1,0:T(8,128)}, u32[]{:S(2)}) copy-start(f32[2,192,768]{2,1,0:T(8,128)} %param.51) | copy-start | bytes 3538948
  1182.8 17.3 %collective-permute-start.9 = (bf16[892,384]{1,0:T(8,128)(2,1)}, bf16[892,384]{1,0:T(8,128)(2,1)}, u32[]{:S(2)}, u32[]{:S(2)}) collective-permute-start(bf16[892,384]{1,0:T(8,128)(2,1)} %bitcast.448), channel_id=1, source_target_pairs={{0,16},{16,0},{1,17},{17,1},{2,18},{18,2},{3,19},{19,3},{4,20},{20... | collective-permute-start | bytes 2055176 | tf_op jit(solution)/shard_map/ppermute | solution.py:380
  (178 other events, 712.5 us)
Sparse Core Ops, SparseCore 0:
  12.4 47.5 all-gather.29
  62.7 79.5 all-gather.19
  145.2 52.0 all-gather.15
  200.0 51.9 all-gather.21
  254.7 51.9 all-gather.23
  309.4 51.9 all-gather.17
  363.6 51.9 all-gather.25
  417.9 51.9 all-gather.27
  674.3 109.9 reduce-scatter.6
  788.8 111.1 reduce-scatter.10
  904.1 131.4 reduce-scatter.8
  1040.1 142.6 reduce-scatter.4

commit v2 on v1

--- a/solution.py
+++ b/solution.py
@@ -17,7 +17,7 @@
 QGROUPS = 2
 LAYERS = 2
 STEP = 10
-SMALL_LANES = 1536
+SMALL_LANES = 6144
 
 
 beta_one = 0.9
@@ -43,6 +43,7 @@
 HALF = KW // PACK
 STEPS = HALF + 1
 VMEM = 56 * 1024 * 1024
+SMALL_COST = pl.CostEstimate(flops=1024, bytes_accessed=1024, transcendentals=0)
 NT = (((1,), (1,)), ((), ()))
 NN = (((1,), (0,)), ((), ()))
 
@@ -129,68 +130,113 @@
             pltpu.VMEM((256, STEPS * 256), jnp.bfloat16),
             pltpu.VMEM((2, LANE, STEPS * 256), jnp.bfloat16),
         ],
+        cost_estimate=SMALL_COST,
         compiler_params=pltpu.CompilerParams(vmem_limit_bytes=VMEM, dimension_semantics=("arbitrary",)),
         name="conv_forward",
     )(x, w)
 
 
-def conv_backward_kernel(rows, shards, x_ref, d_ref, w_ref, dx_ref, dw_ref,
-                         xe_ref, xo_ref, de_ref, do_ref, taps_ref, wide_ref, prod_ref, grad_ref):
+def conv_input_kernel(rows, shards, d_ref, w_ref, dx_ref, even_ref, odd_ref, taps_ref, wide_ref):
+    m = rows * 16
+    pack_pair(d_ref, even_ref, odd_ref, rows + HALF)
+    widen_taps(w_ref, wide_ref, shards)
+    results = []
+    for group, packed in enumerate((even_ref, odd_ref)):
+        build_taps(wide_ref, taps_ref, group)
+        acc = jnp.zeros((m, 256), jnp.float32)
+        for q in range(STEPS):
+            left = packed[(HALF - q) * 16:(HALF - q) * 16 + m, :]
+            acc = acc + mm(left, taps_ref[:, q * 256:q * 256 + 256])
+        results.append(acc)
+    unpack_pair(results[0], results[1], dx_ref, rows)
+
+
+def conv_input_grad(d, w, rows, shards):
+    frames = PACK * (rows + HALF)
+    return pl.pallas_call(
+        functools.partial(conv_input_kernel, rows, shards),
+        grid=(GROUPS // 2,),
+        in_specs=[
+            pl.BlockSpec((frames, 16, 128), lambda g: (0, 0, g)),
+            pl.BlockSpec((shards, 2 * GC, w.shape[2]), lambda g: (0, g, 0)),
+        ],
+        out_specs=pl.BlockSpec((PACK * rows, 16, 128), lambda g: (0, 0, g)),
+        out_shape=jax.ShapeDtypeStruct((PACK * rows, 16, PADW), jnp.float32),
+        scratch_shapes=[pltpu.VMEM(((rows + HALF) * 16, 256), jnp.bfloat16)] * 2 + [
+            pltpu.VMEM((256, STEPS * 256), jnp.bfloat16),
+            pltpu.VMEM((2, LANE, STEPS * 256), jnp.bfloat16),
+        ],
+        cost_estimate=SMALL_COST,
+        compiler_params=pltpu.CompilerParams(vmem_limit_bytes=VMEM, dimension_semantics=("arbitrary",)),
+        name="conv_input_grad",
+    )(d, w)
+
+
+def conv_weight_kernel(rows, shards, x_ref, d_ref, dw_ref, xe_ref, xo_ref, de_ref, do_ref, prod_ref, grad_ref):
     m = rows * 16
     per = KW // shards
+    width = KW * LANE
     pack_pair(x_ref, xe_ref, xo_ref, rows + HALF)
-    pack_pair(d_ref, de_ref, do_ref, rows + HALF)
-    widen_taps(w_ref, wide_ref, shards)
-    results = []
+    pack_pair(d_ref, de_ref, do_ref, rows)
     for group, (x_packed, d_packed) in enumerate(((xe_ref, de_ref), (xo_ref, do_ref))):
-        build_taps(wide_ref, taps_ref, group)
-        d_turned = d_packed[HALF // 2 * 16:HALF // 2 * 16 + m, :].astype(jnp.float32).T.astype(jnp.bfloat16)
-        acc = jnp.zeros((m, 256), jnp.float32)
+        d_turned = d_packed[...].astype(jnp.float32).T.astype(jnp.bfloat16)
         for q in range(STEPS):
-            left = d_packed[(HALF - q) * 16:(HALF - q) * 16 + m, :]
-            acc = acc + mm(left, taps_ref[:, q * 256:q * 256 + 256])
             prod_ref[:, q * 256:q * 256 + 256] = mm(d_turned, x_packed[q * 16:q * 16 + m, :])
-        results.append(acc)
-        width = KW * LANE
         straight = prod_ref[0:GC, 0:width] + prod_ref[128:128 + GC, 128:128 + width]
-        turned = prod_ref[64:64 + GC, :] + pltpu.roll(prod_ref[192:192 + GC, :], STEPS * 256 - 128, 1)
-        grad = straight + pltpu.roll(turned, STEPS * 256 - 64, 1)[:, 0:width]
+        turned_part = prod_ref[64:64 + GC, :] + pltpu.roll(prod_ref[192:192 + GC, :], STEPS * 256 - 128, 1)
+        grad = straight + pltpu.roll(turned_part, STEPS * 256 - 64, 1)[:, 0:width]
         grad = grad.astype(jnp.bfloat16)
         for s in range(shards):
             start = (2 * s + group) * GC
             grad_ref[start:start + GC, :] = grad[:, s * per * LANE:(s + 1) * per * LANE]
     sel = spread_matrix(per * GC, per * LANE, GC, LANE)
     dw_ref[...] = mm(grad_ref[...], sel, NT).astype(jnp.bfloat16).reshape(shards, 2 * GC, per * GC)
-    unpack_pair(results[0], results[1], dx_ref, rows)
-
-
-def conv_backward(x, d, w, rows, shards):
-    frames = PACK * (rows + HALF)
+
+
+def conv_weight_grad(x, d, rows, shards):
+    per = KW // shards
+    first = HALF * PACK // 2
+    d = d[first:first + PACK * rows]
     return pl.pallas_call(
-        functools.partial(conv_backward_kernel, rows, shards),
+        functools.partial(conv_weight_kernel, rows, shards),
         grid=(GROUPS // 2,),
         in_specs=[
-            pl.BlockSpec((frames, 16, 128), lambda g: (0, 0, g)),
-            pl.BlockSpec((frames, 16, 128), lambda g: (0, 0, g)),
-            pl.BlockSpec((shards, 2 * GC, w.shape[2]), lambda g: (0, g, 0)),
+            pl.BlockSpec((PACK * (rows + HALF), 16, 128), lambda g: (0, 0, g)),
+            pl.BlockSpec((PACK * rows, 16, 128), lambda g: (0, 0, g)),
         ],
-        out_specs=[
-            pl.BlockSpec((PACK * rows, 16, 128), lambda g: (0, 0, g)),
-            pl.BlockSpec((shards, 2 * GC, w.shape[2]), lambda g: (0, g, 0)),
+        out_specs=pl.BlockSpec((shards, 2 * GC, per * GC), lambda g: (0, g, 0)),
+        out_shape=jax.ShapeDtypeStruct((shards, D, per * GC), jnp.bfloat16),
+        scratch_shapes=[
+            pltpu.VMEM(((rows + HALF) * 16, 256), jnp.bfloat16),
+            pltpu.VMEM(((rows + HALF) * 16, 256), jnp.bfloat16),
+            pltpu.VMEM((rows * 16, 256), jnp.bfloat16),
+            pltpu.VMEM((rows * 16, 256), jnp.bfloat16),
+            pltpu.VMEM((256, STEPS * 256), jnp.float32),
+            pltpu.VMEM((shards * 2 * GC, per * LANE), jnp.bfloat16),
         ],
-        out_shape=[
-            jax.ShapeDtypeStruct((PACK * rows, 16, PADW), jnp.float32),
-            jax.ShapeDtypeStruct(w.shape, jnp.bfloat16),
-        ],
-        scratch_shapes=[pltpu.VMEM(((rows + HALF) * 16, 256), jnp.bfloat16)] * 4 + [
-            pltpu.VMEM((256, STEPS * 256), jnp.bfloat16),
-            pltpu.VMEM((2, LANE, STEPS * 256), jnp.bfloat16),
-            pltpu.VMEM((256, STEPS * 256), jnp.float32),
-            pltpu.VMEM((shards * 2 * GC, KW // shards * LANE), jnp.bfloat16),
-        ],
+        cost_estimate=SMALL_COST,
         compiler_params=pltpu.CompilerParams(vmem_limit_bytes=VMEM, dimension_semantics=("arbitrary",)),
-        name="conv_backward",
-    )(x, d, w)
+        name="conv_weight_grad",
+    )(x, d)
+
+
+def line_up_kernel(*refs):
+    out_ref = refs[-1]
+    row = 0
+    for ref in refs[:-1]:
+        for j in range(ref.shape[1] // 256):
+            out_ref[row:row + 1, :] = ref[:, j * 256:j * 256 + 256]
+            row += 1
+
+
+def line_up(vectors):
+    vectors = [v.reshape(1, -1) for v in vectors]
+    total = sum(v.shape[1] for v in vectors)
+    return pl.pallas_call(
+        line_up_kernel,
+        out_shape=jax.ShapeDtypeStruct((total // 256, 256), jnp.float32),
+        name="line_up",
+    )(*vectors)
 
 
 def to_strips(padded, frame_count):
@@ -262,6 +308,7 @@
             jax.ShapeDtypeStruct((rows, D), jnp.bfloat16),
             jax.ShapeDtypeStruct((clips, HEADS // 2, 2, frames), jnp.float32),
         ],
+        cost_estimate=SMALL_COST,
         compiler_params=pltpu.CompilerParams(vmem_limit_bytes=VMEM, dimension_semantics=("arbitrary", "arbitrary")),
         name="attend",
     )(*operands)
@@ -330,6 +377,7 @@
         in_specs=[spec, spec, pl.BlockSpec((1, 1, 2, frames), lambda c, h: (c, h, 0, 0))] + [spec] * len(operands),
         out_specs=[spec] * (1 + 2 * blocks),
         out_shape=[shape] * (1 + 2 * blocks),
+        cost_estimate=SMALL_COST,
         compiler_params=pltpu.CompilerParams(vmem_limit_bytes=VMEM, dimension_semantics=("arbitrary", "arbitrary")),
         name="attend_back",
     )(query, grad, stat, *operands)
@@ -355,9 +403,129 @@
         in_specs=[pl.BlockSpec((1, draws, tile), lambda c, f: (c, 0, f))],
         out_specs=pl.BlockSpec((1, length, tile), lambda c, f: (c, 0, f)),
         out_shape=jax.ShapeDtypeStruct((clips, length, frames), jnp.bfloat16),
+        cost_estimate=SMALL_COST,
         compiler_params=pltpu.CompilerParams(vmem_limit_bytes=VMEM, dimension_semantics=("arbitrary", "arbitrary")),
         name="count_draws",
     )(negatives)
+
+
+MESH = pl.DeviceIdType.MESH
+AHEAD = 3
+OTHER = 2
+
+
+def reduce_kernel(count, seqs, sizes, *refs):
+    number = len(sizes)
+    sources = refs[:number]
+    outs = refs[number : 2 * number]
+    bits = count.bit_length() - 1
+    turns = seqs.bit_length() - 1
+    levels = bits + turns
+    held = refs[2 * number : 2 * number + levels]
+    send_sem, recv_sem = refs[2 * number + levels :]
+    me = lax.axis_index("shard")
+    place = lax.axis_index("seq")
+
+    def across(index, bit):
+        return index + (1 - 2 * ((index // 2**bit) % 2)) * 2**bit
+
+    partners = [{"shard": across(me, b)} for b in range(bits)] + [{"seq": across(place, t)} for t in range(turns)]
+    barrier = pltpu.get_barrier_semaphore()
+    for partner in partners:
+        pl.semaphore_signal(barrier, inc=1, device_id=partner, device_id_type=MESH)
+    pl.semaphore_wait(barrier, len(partners))
+
+    pieces = []
+    offset = 0
+    for source, out, (rows, cut) in zip(sources, outs, sizes):
+        for start in range(0, rows, cut):
+            pieces.append((source, out, start, offset + start, cut))
+        offset += rows
+    orders = [list(range(bits)), list(range(bits))]
+    if bits > 2:
+        orders[1] = [0] + list(range(2, bits)) + [1]
+    flights = {}
+
+    def moves(piece, level):
+        order = orders[1 if piece % 5 == OTHER else 0]
+        if level >= bits:
+            return [(0, 0)], partners[level]
+        bit = order[level]
+        left = sorted(order[level:])
+        low = 2 ** left.index(bit)
+        side = (me // 2**bit) % 2
+        pairs = []
+        for j in range(2 ** (bits - level - 1)):
+            base = (j // low) * 2 * low + j % low
+            pairs.append((base + side * low, base + (1 - side) * low))
+        return pairs, partners[bit]
+
+    def data(piece, level, index):
+        source, _, start, spot, cut = pieces[piece]
+        if level == 0:
+            return source.at[index, pl.ds(start, cut)]
+        return held[level - 1].at[index, pl.ds(spot, cut)]
+
+    def launch(piece, level):
+        pairs, partner = moves(piece, level)
+        _, _, _, spot, cut = pieces[piece]
+        copies = []
+        for j, (_, sent) in enumerate(pairs):
+            copies.append(
+                pltpu.make_async_remote_copy(
+                    src_ref=data(piece, level, sent),
+                    dst_ref=held[level].at[j, pl.ds(spot, cut)],
+                    send_sem=send_sem.at[piece, level, j],
+                    recv_sem=recv_sem.at[piece, level, j],
+                    device_id=partner,
+                    device_id_type=MESH,
+                )
+            )
+        for copy in copies:
+            copy.start()
+        flights[piece, level] = copies
+
+    def absorb(piece, level):
+        pairs, _ = moves(piece, level)
+        _, out, start, spot, cut = pieces[piece]
+        for j, (kept, _) in enumerate(pairs):
+            flights[piece, level][j].wait()
+            mine, other = data(piece, level, kept)[...], held[level][j, pl.ds(spot, cut)]
+            if level == levels - 1:
+                out[pl.ds(start, cut)] = mine.astype(jnp.float32) + other.astype(jnp.float32)
+            else:
+                held[level][j, pl.ds(spot, cut)] = mine + other
+
+    delay = [0, 1] + [1 + AHEAD * level for level in range(1, levels)]
+    for wave in range(len(pieces) + delay[-1]):
+        for level in range(levels, -1, -1):
+            piece = wave - delay[level]
+            if 0 <= piece < len(pieces):
+                if level > 0:
+                    absorb(piece, level - 1)
+                if level < levels:
+                    launch(piece, level)
+
+
+def reduce_chunks(call, mesh_sizes, cuts, *chunks):
+    count, seqs = mesh_sizes
+    bits, turns = count.bit_length() - 1, seqs.bit_length() - 1
+    lanes = chunks[0].shape[2]
+    sizes = [(c.shape[1], cut) for c, cut in zip(chunks, cuts)]
+    total = sum(rows for rows, _ in sizes)
+    number = sum(rows // cut for rows, cut in sizes)
+    slots = [2 ** (bits - 1 - level) for level in range(bits)] + [1] * turns
+    return pl.pallas_call(
+        functools.partial(reduce_kernel, count, seqs, sizes),
+        in_specs=[pl.BlockSpec(memory_space=pltpu.VMEM)] * len(chunks),
+        out_specs=[pl.BlockSpec(memory_space=pltpu.VMEM)] * len(chunks),
+        out_shape=[jax.ShapeDtypeStruct(c.shape[1:], jnp.float32) for c in chunks],
+        scratch_shapes=[pltpu.VMEM((n, total, lanes), jnp.bfloat16) for n in slots]
+        + [pltpu.SemaphoreType.DMA((number, bits + turns, count // 2))] * 2,
+        cost_estimate=SMALL_COST,
+        compiler_params=pltpu.CompilerParams(collective_id=call, has_side_effects=True, vmem_limit_bytes=VMEM),
+        name="reduce_chunks",
+    )(*chunks)
 
 
 def swap_moves(count, step):
@@ -402,7 +570,7 @@
 
 
 def column_sum(values):
-    return jnp.sum(values.astype(jnp.float32), 0)
+    return jnp.sum(values.astype(jnp.float32), 0, keepdims=True)
 
 
 def gelu_parts(values):
@@ -411,10 +579,24 @@
     return values * half, half + values * density
 
 
-def layer_norm(values, gain_row, bias_row):
+def norm_forward(values, gain_row, bias_row):
     centred = values - jnp.mean(values, -1, keepdims=True)
     spread = jnp.mean(centred * centred, -1, keepdims=True)
-    return centred * lax.rsqrt(spread + norm_epsilon) * gain_row + bias_row
+    scale = lax.rsqrt(spread + norm_epsilon)
+    level = centred * scale
+    return level * gain_row + bias_row, (level, scale, gain_row)
+
+
+def norm_vectors(grad, kept):
+    level = kept[0]
+    return jnp.sum(grad * level, 0, keepdims=True), jnp.sum(grad, 0, keepdims=True)
+
+
+def norm_backward(grad, kept):
+    level, scale, gain_row = kept
+    inside = grad * gain_row
+    centred = inside - jnp.mean(inside, -1, keepdims=True) - level * jnp.mean(inside * level, -1, keepdims=True)
+    return (scale * centred,) + norm_vectors(grad, kept)
 
 
 def unit_rows(values):
@@ -440,29 +622,31 @@
     return jnp.concatenate([low, block, high], axis=1)
 
 
-def layer_forward(hidden, attn_w, expand_w, shrink_w, pieces, clip_count):
+def layer_forward(hidden, attn_w, expand_w, shrink_w, pieces, clip_count, *waiting):
     q_bias, v_bias, o_bias, gain_one, bias_one, expand_bias, shrink_bias, gain_two, bias_two = pieces
     entries = gather_ring(lowered(hidden))
     query = lowered(bdot(entries[0], attn_w[:, :D]) + q_bias)
     keys = [lowered(bdot(entry, attn_w[:, D : 2 * D])) for entry in entries]
     values = [lowered(bdot(entry, attn_w[:, 2 * D : 3 * D]) + v_bias) for entry in entries]
     mixed, stat = attend(query, keys, values, clip_count)
+    if waiting:
+        mixed, *waiting = fence(mixed, *waiting)
     branch = bdot(mixed, attn_w[:, 3 * D :]) + o_bias
-    middle, middle_pull = jax.vjp(layer_norm, hidden + branch, gain_one, bias_one)
+    middle, middle_kept = norm_forward(hidden + branch, gain_one, bias_one)
     middle_low = lowered(middle)
     inner = bdot(middle_low, expand_w) + expand_bias
     activated, slope = gelu_parts(inner)
     active_low = lowered(activated)
     slope_low = lowered(slope)
     outer = bdot(active_low, shrink_w) + shrink_bias
-    result, final_pull = jax.vjp(layer_norm, middle + outer, gain_two, bias_two)
-    cache = (entries, query, keys, values, mixed, stat, middle_pull, middle_low, slope_low, active_low, final_pull)
-    return result, cache
+    result, final_kept = norm_forward(middle + outer, gain_two, bias_two)
+    cache = (entries, query, keys, values, mixed, stat, middle_kept, middle_low, slope_low, active_low, final_kept)
+    return (result, cache) + tuple(waiting or [None])
 
 
 def feed_backward(grad_out, cache, expand_w, shrink_w):
-    middle_low, slope_low, active_low, final_pull = cache[7:]
-    grad_sum, grad_gain, grad_bias = final_pull(grad_out)
+    middle_low, slope_low, active_low, final_kept = cache[7:]
+    grad_sum, grad_gain, grad_bias = norm_backward(grad_out, final_kept)
     grad_outer = lowered(grad_sum)
     grad_shrink = lowered(rows_dot(active_low, grad_outer))
     grad_inner = lowered(slope_low.astype(jnp.float32) * turned_dot(grad_outer, shrink_w))
@@ -472,13 +656,13 @@
     return grad_middle, grad_expand, grad_shrink, vectors
 
 
-def attend_backward(grad_middle, cache, attn_w, clip_count):
-    entries, query, keys, values, mixed, stat, middle_pull = cache[:7]
-    grad_sum, grad_gain, grad_bias = middle_pull(grad_middle)
+def attend_backward(grad_middle, cache, attn_w, clip_count, *waiting):
+    entries, query, keys, values, mixed, stat, middle_kept = cache[:7]
+    grad_sum, grad_gain, grad_bias = norm_backward(grad_middle, middle_kept)
     grad_branch = lowered(grad_sum)
-    grad_out_proj = lowered(rows_dot(mixed, grad_branch))
     grad_mixed = lowered(turned_dot(grad_branch, attn_w[:, 3 * D :]))
     results = attend_back(query, grad_mixed, stat, keys, values, clip_count)
+    results, grad_branch, *waiting = fence(results, grad_branch, *waiting)
     grad_query, grad_keys, grad_values = results[0], results[1::2], results[2::2]
     back = [
         turned_dot(dk, attn_w[:, D : 2 * D]) + turned_dot(dv, attn_w[:, 2 * D : 3 * D])
@@ -492,7 +676,7 @@
         lowered(rows_dot(entries[0], grad_query)),
         lowered(sum(rows_dot(entry, dk) for entry, dk in zip(entries, grad_keys))),
         lowered(sum(rows_dot(entry, dv) for entry, dv in zip(entries, grad_values))),
-        grad_out_proj,
+        lowered(rows_dot(mixed, grad_branch)),
     ]
     vectors = [
         column_sum(grad_query),
@@ -501,7 +685,7 @@
         grad_gain,
         grad_bias,
     ]
-    return grad_hidden, grads, vectors
+    return grad_hidden, grads, vectors, waiting
 
 
 def adam_update(weight, grad, first, second, rate, decay):
@@ -514,7 +698,27 @@
 
 
 def gather_rows(block):
-    return lax.all_gather(block, "shard", axis=0, tiled=True)
+    whole = lax.all_gather(block, "shard", axis=0, tiled=True)
+    return whole.reshape((-1,) + block.shape)
+
+
+def pass_kernel(*refs):
+    pass
+
+
+def fence(*values):
+    flat, tree = jax.tree.flatten(values)
+    spec = pl.BlockSpec(memory_space=pl.ANY)
+    flat = pl.pallas_call(
+        pass_kernel,
+        in_specs=[spec] * len(flat),
+        out_specs=[spec] * len(flat),
+        out_shape=[jax.ShapeDtypeStruct(v.shape, v.dtype) for v in flat],
+        input_output_aliases={i: i for i in range(len(flat))},
+        cost_estimate=SMALL_COST,
+        name="fence",
+    )(*flat)
+    return jax.tree.unflatten(tree, flat)
 
 
 def scatter_chunks(chunks):
@@ -580,22 +784,44 @@
 
     small = jnp.concatenate([lowered(item).reshape(-1) for item in small_items])
     small = jnp.pad(small, (0, small_width - small_total))
-    small_all = lax.all_gather(small, "shard", axis=0, tiled=False)
-    feat_w, final_w, target_w, code_w, vector_low = split_small(small_all)
-    conv_w = lax.all_gather(lowered(conv_weight).T, "shard", axis=0, tiled=False)
+    taps = conv_weight.shape[0]
+    (own_first,) = fence(jnp.concatenate([lowered(conv_weight).T, small.reshape(-1, taps)]))
+    first_all = gather_rows(own_first)
+    conv_w = first_all
+    feat_w, final_w, target_w, code_w, vector_low = split_small(first_all[:, D:].reshape(shards, -1))
     attn_w, expand_w, shrink_w = [], [], []
-    for layer in range(LAYERS):
-        own = lowered(attention_weight[4 * layer : 4 * layer + 4]).transpose(1, 0, 2).reshape(-1, 4 * D)
-        attn_w.append(gather_rows(own))
-        expand_w.append(gather_rows(lowered(expand_weight[layer])))
-        shrink_w.append(gather_rows(lowered(shrink_weight[layer])))
+    rows = D // shards
+
+    def own_attn(layer):
+        return jnp.concatenate([lowered(attention_weight[4 * layer + i]) for i in range(4)])
+
+    def own_feed(layer):
+        expand_own = lowered(expand_weight[layer])
+        return jnp.concatenate(
+            [expand_own[:, j * D : (j + 1) * D] for j in range(FF // D)] + [lowered(shrink_weight[layer])]
+        )
+
+    def use_attn(whole):
+        attn_w.append(jnp.concatenate([whole[:, j * rows : (j + 1) * rows].reshape(D, D) for j in range(4)], 1))
+
+    def use_feed(whole):
+        blocks = [whole[:, j * rows : (j + 1) * rows].reshape(D, D) for j in range(FF // D)]
+        expand_w.append(jnp.concatenate(blocks, 1))
+        shrink_w.append(whole[:, FF // D * rows :].reshape(FF, D))
+
+    first_frame = lax.axis_index("seq") * frame_count
+    ring_draws = (negatives - first_frame + clip_frames) % clip_frames
+    counts = count_draws(ring_draws.transpose(0, 2, 1), clip_frames)
+    counts, own_0 = fence(counts, jnp.concatenate([own_attn(0), own_feed(0)]))
+    whole = gather_rows(own_0)
+    use_attn(whole[:, : 4 * rows])
+    use_feed(whole[:, 4 * rows :])
     parts = shards // (4 * LAYERS)
-    left_low = trade(jnp.repeat(lowered(left_basis_t), parts, axis=0)).reshape(D, D)
 
     pieces = vector_pieces(vector_low.astype(jnp.float32))
     mask_on = (time_mask > 0).reshape(row_count, 1)
     feats = features.reshape(row_count, CIN).astype(jnp.float32)
-    normed, norm_pull = jax.vjp(layer_norm, feats, pieces[0], pieces[1])
+    normed, norm_kept = norm_forward(feats, pieces[0], pieces[1])
     normed_low = lowered(normed)
     projected = bdot(normed_low, feat_w) + pieces[2]
     masked = jnp.where(mask_on, pieces[3][None, :], projected)
@@ -604,21 +830,25 @@
     strips = to_strips(padded, frame_count)
     conv_out = from_strips(conv_forward(strips, conv_w, strip_rows, shards), clip_count) + pieces[4]
     conv_active, conv_slope = gelu_parts(conv_out)
-    hidden, front_pull = jax.vjp(layer_norm, masked + conv_active, pieces[5], pieces[6])
-
-    caches = []
-    for layer in range(LAYERS):
-        hidden, cache = layer_forward(
-            hidden, attn_w[layer], expand_w[layer], shrink_w[layer], pieces[7 + 9 * layer : 16 + 9 * layer], clip_count
-        )
-        caches.append(cache)
+    hidden, front_kept = norm_forward(masked + conv_active, pieces[5], pieces[6])
+
+    hidden, own_1 = fence(hidden, own_attn(1))
+    use_attn(gather_rows(own_1))
+    hidden, cache, own_1 = layer_forward(
+        hidden, attn_w[0], expand_w[0], shrink_w[0], pieces[7:16], clip_count, own_feed(1)
+    )
+    caches = [cache]
+    use_feed(gather_rows(own_1))
+    hidden, cache, _ = layer_forward(hidden, attn_w[1], expand_w[1], shrink_w[1], pieces[16:25], clip_count)
+    caches.append(cache)
     top_low = lowered(hidden)
     context, context_pull = jax.vjp(unit_rows, bdot(top_low, final_w) + pieces[-2])
     context_low = lowered(context).reshape(clip_count, frame_count, PROJ)
-
-    first_frame = lax.axis_index("seq") * frame_count
-    ring_draws = (negatives - first_frame + clip_frames) % clip_frames
-    counts = count_draws(ring_draws.transpose(0, 2, 1), clip_frames).astype(jnp.float32)
+    held = jnp.stack([lowered(left_basis_t), lowered(attention_first), lowered(attention_second)], 1)
+    context_low, held = fence(context_low, held)
+    traded = trade(jnp.repeat(held, parts, axis=0))
+
+    counts = counts.astype(jnp.float32)
     codes = jnp.concatenate(gather_ring(target_codes), 1).reshape(clip_count * clip_frames, QGROUPS)
     width = PROJ // QGROUPS
     code_f = code_w.astype(jnp.float32)
@@ -666,36 +896,63 @@
     grad_final_bias = column_sum(grad_context_low)
     grad_hidden = turned_dot(grad_context_low, final_w)
 
-    attn_grads = [None] * LAYERS
-    feed_sums = [None] * LAYERS
-    layer_pieces = [None] * LAYERS
-    for layer in reversed(range(LAYERS)):
-        grad_middle, grad_expand, grad_shrink, feed_vectors = feed_backward(
-            grad_hidden, caches[layer], expand_w[layer], shrink_w[layer]
-        )
-        chunks = jnp.concatenate(
-            [grad_expand[:, j * D : (j + 1) * D].reshape(shards, -1, D) for j in range(FF // D)]
-            + [grad_shrink.reshape(shards, -1, D)],
-            1,
-        )
-        feed_sums[layer] = seq_sum(scatter_chunks(chunks))
-        grad_hidden, attn_grads[layer], attn_vectors = attend_backward(
-            grad_middle, caches[layer], attn_w[layer], clip_count
-        )
-        layer_pieces[layer] = attn_vectors + feed_vectors
-    attn_chunks = jnp.stack(attn_grads[0] + attn_grads[1]).reshape(4 * LAYERS, D, parts, D // parts)
-    attn_chunks = attn_chunks.transpose(0, 2, 1, 3).reshape(shards, D, D // parts)
-    attn_sum = seq_sum(scatter_chunks(attn_chunks))
-
-    grad_sum, grad_gain_enc, grad_bias_enc = front_pull(grad_hidden)
+    columns = D // parts
+    def rotated_adam(first, second, grad):
+        first = beta_rotated * first + (1 - beta_rotated) * grad
+        second = beta_rotated * second + (1 - beta_rotated) * grad * grad
+        share = first / (1 - beta_rotated**STEP) / (jnp.sqrt(second / (1 - beta_rotated**STEP)) + adam_epsilon)
+        return share, first, second
+
+    def rotate(whole_grad):
+        left_low, first_low, second_low = [traded[:, i].reshape(D, D) for i in range(3)]
+        group = lax.axis_index("shard") // parts
+        right_low = lowered(lax.dynamic_index_in_dim(right_orthogonal_basis, group, 0, keepdims=False))
+        rotated = bdot(lowered(bdot(left_low, whole_grad)), right_low)
+        direction = rotated_adam(first_low.astype(jnp.float32), second_low.astype(jnp.float32), rotated)[0]
+        half_back = lowered(turned_dot(lowered(direction), right_low))
+        part_start = (lax.axis_index("shard") % parts) * columns
+        rotated_part = lax.dynamic_slice_in_dim(lowered(rotated), part_start, columns, 1)
+        update_part = lowered(rows_dot(left_low, lax.dynamic_slice_in_dim(half_back, part_start, columns, 1)))
+        sent = jnp.stack([rotated_part.reshape(shards, rows, columns), update_part.reshape(shards, rows, columns)], 1)
+        return sent
+
+    def feed_blocks(grad_expand, grad_shrink):
+        blocks = [grad_expand[:, j * D : (j + 1) * D].reshape(shards, -1, D) for j in range(FF // D)]
+        return blocks + [grad_shrink.reshape(shards, -1, D)]
+
+    def attn_blocks(grads):
+        return [grad.reshape(shards, -1, D) for grad in grads]
+
+    grad_middle, grad_expand, grad_shrink, feed_vectors_1 = feed_backward(
+        grad_hidden, caches[1], expand_w[1], shrink_w[1]
+    )
+    grad_hidden, grads, attn_vectors_1, (traded,) = attend_backward(
+        grad_middle, caches[1], attn_w[1], clip_count, traded
+    )
+    chunks = jnp.concatenate(attn_blocks(grads) + feed_blocks(grad_expand, grad_shrink), 1)
+    grad_hidden, chunks = fence(grad_hidden, chunks)
+    sum_1 = scatter_chunks(chunks)
+    grad_middle, grad_expand, grad_shrink, feed_vectors_0 = feed_backward(
+        grad_hidden, caches[0], expand_w[0], shrink_w[0]
+    )
+    feed_grads = feed_blocks(grad_expand, grad_shrink)
+    grad_hidden, grads, attn_vectors_0, _ = attend_backward(grad_middle, caches[0], attn_w[0], clip_count)
+    grad_hidden, chunks = fence(grad_hidden, jnp.concatenate(attn_blocks(grads) + feed_grads, 1))
+    sum_0 = scatter_chunks(chunks)
+    mesh_sizes = (shards, seq_count)
+    grad_sum, grad_gain_enc, grad_bias_enc = norm_backward(grad_hidden, front_kept)
     grad_conv_low = lowered(grad_sum * conv_slope)
     grad_strips = to_strips(with_halo(grad_conv_low.reshape(clip_count, frame_count, D), KW // 2), frame_count)
-    grad_back, conv_chunks = conv_backward(strips, grad_strips, conv_w, strip_rows, shards)
+    conv_chunks = conv_weight_grad(strips, grad_strips, strip_rows, shards)
+    grad_strips, conv_chunks, sum_1 = fence(grad_strips, conv_chunks, sum_1)
+    sum_1 = seq_sum(sum_1)
+    grad_back = conv_input_grad(grad_strips, conv_w, strip_rows, shards)
+    grad_back, sum_1 = fence(grad_back, sum_1)
     grad_masked = grad_sum + from_strips(grad_back, clip_count)
-    grad_embedding = jnp.sum(jnp.where(mask_on, grad_masked, 0.0), 0)
+    grad_embedding = jnp.sum(jnp.where(mask_on, grad_masked, 0.0), 0, keepdims=True)
     grad_projected = lowered(jnp.where(mask_on, 0.0, grad_masked))
     grad_feat_w = rows_dot(normed_low, grad_projected)
-    _, grad_gain_feat, grad_bias_feat = norm_pull(turned_dot(grad_projected, feat_w))
+    grad_gain_feat, grad_bias_feat = norm_vectors(turned_dot(grad_projected, feat_w), norm_kept)
     vector_grads = [
         grad_gain_feat,
         grad_bias_feat,
@@ -705,9 +962,8 @@
         grad_gain_enc,
         grad_bias_enc,
     ]
-    for layer in range(LAYERS):
-        vector_grads = vector_grads + layer_pieces[layer]
-    vector_grads = jnp.concatenate(vector_grads + [grad_final_bias, grad_target_bias])
+    vector_grads += attn_vectors_0 + feed_vectors_0 + attn_vectors_1 + feed_vectors_1
+    vector_grads = line_up(vector_grads + [grad_final_bias, grad_target_bias])
     small_grads = [
         lowered(item).reshape(shards, -1)
         for item in (grad_feat_w, grad_final_w, grad_target_w, grad_codebook, vector_grads)
@@ -715,39 +971,23 @@
     loss_tile = jnp.broadcast_to(lowered(jnp.stack([loss_sum, mask_count]))[None], (shards, 2))
     gap = jnp.zeros((shards, small_width - small_total - 2), jnp.bfloat16)
     small_chunks = jnp.concatenate(small_grads + [loss_tile, gap], 1)
-    taps = conv_chunks.shape[2]
-    last_chunks = jnp.concatenate([conv_chunks, small_chunks.reshape(shards, -1, taps)], 1)
-    last_sum = seq_sum(scatter_chunks(last_chunks))
-    sum_conv = last_sum[:D].T
-    small_sum = last_sum[D:].reshape(1, -1)
+    small_chunks, sum_0 = fence(small_chunks.reshape(shards, -1, taps), sum_0)
+    sum_0 = seq_sum(sum_0)
+    attn_rows = jnp.concatenate([sum_0[: 4 * rows], sum_1[: 4 * rows]]).reshape(4 * LAYERS, rows, D)
+    whole_grad = trade(jnp.repeat(lowered(attn_rows), parts, axis=0)).reshape(D, D)
+    sent = rotate(whole_grad)
+    sent, small_chunks = fence(sent, small_chunks)
+    rotation = trade(sent)
+    small_sum, sum_conv = reduce_chunks(0, mesh_sizes, (128, 96), small_chunks, conv_chunks)
+    small_sum = small_sum.reshape(1, -1)
+    sum_conv = sum_conv.T
+    arrived = rotation.reshape(4 * LAYERS, parts, 2, rows, columns).transpose(2, 0, 3, 1, 4)
+    arrived = arrived.reshape(2, 4 * LAYERS, rows, D).astype(jnp.float32)
+    _, rot_first, rot_second = rotated_adam(attention_first, attention_second, arrived[0])
+    new_attention = attention_weight - rate_rotated * arrived[1]
+    feed_sums = [sum_0[4 * rows :], sum_1[4 * rows :]]
     sum_loss = small_sum[0, small_total : small_total + 2]
     sum_feat, sum_final, sum_target, sum_code, sum_vector = split_small(small_sum)
-
-    rows = D // shards
-    columns = D // parts
-
-    def to_rows(block):
-        shaped = trade(lowered(block).reshape(shards, rows, columns)).reshape(4 * LAYERS, parts, rows, columns)
-        return shaped.transpose(0, 2, 1, 3).reshape(4 * LAYERS, rows, D)
-
-    def to_columns(block):
-        shaped = lowered(block).reshape(4 * LAYERS, rows, parts, columns).transpose(0, 2, 1, 3)
-        return trade(shaped.reshape(shards, rows, columns)).reshape(D, columns)
-
-    right_low = lowered(right_orthogonal_basis)
-    left_grad = to_rows(bdot(left_low, lowered(attn_sum)))
-    rotated = jnp.einsum("mrd,mde->mre", left_grad, right_low, preferred_element_type=jnp.float32)
-    rot_first = beta_rotated * attention_first + (1 - beta_rotated) * rotated
-    rot_second = beta_rotated * attention_second + (1 - beta_rotated) * rotated * rotated
-    share_fraction = (
-        rot_first
-        / (1 - beta_rotated**STEP)
-        / (jnp.sqrt(rot_second / (1 - beta_rotated**STEP)) + adam_epsilon)
-    )
-    half_back = jnp.einsum("mre,mde->mrd", lowered(share_fraction), right_low, preferred_element_type=jnp.float32)
-    update = to_rows(rows_dot(left_low, to_columns(half_back)))
-    new_attention = attention_weight - rate_rotated * update.astype(jnp.float32)
-
     sum_expand = jnp.stack(
         [s[: -shrink_weight.shape[1]].reshape(FF // D, -1, D).transpose(1, 0, 2).reshape(-1, FF) for s in feed_sums]
     )

time: 1240 us -> 1050 us (0.85)
  waiting for transfers between devices: 383 us -> 180 us
  Pallas kernels: 215 us -> 313 us
  matrix products: 274 us -> 230 us
  starting transfers between devices: 72.2 us -> 34.5 us
    reduce_scatter x4 -> x2, waiting for transfers between devices: 137 us -> 33.7 us  [scatter_chunks(): return lax.psum_scatter(chunks, 'shard', scatter_dimension=0, tiled=False)]
    pallas_call x1 -> x17, Pallas kernels: 55.2 us -> 153 us  [the longest x1 88 us: reduce_chunks(): pl.pallas_call(functools.partial(reduce_kernel, count, seqs, sizes), in_s...]
    all_gather x8 -> x4, waiting for transfers between devices: 162 us -> 89 us  [gather_rows(): whole = lax.all_gather(block, 'shard', axis=0, tiled=True)]
    slice x4 -> x13, local copies, waits for them, and re-layouts: 2.31 us -> 35.8 us  [the longest x2 19.1 us: use_attn(): whole[:, j * rows:(j + 1) * rows].reshape(D, D)]
    all_to_all x4 -> x3, starting transfers between devices: 42.8 us -> 13.7 us  [trade(): lax.all_to_all(chunks, 'shard', split_axis=0, concat_axis=0, tiled=True)]
    all_to_all x4 -> x3, waiting for transfers between devices: 39.8 us -> 14.2 us  [trade(): lax.all_to_all(chunks, 'shard', split_axis=0, concat_axis=0, tiled=True)]
    dot_general x2 -> x0, matrix products: 21.3 us -> none  [the longest x1 12.5 us: on_device(): jnp.einsum('mre,mde->mrd', lowered(share_fraction), right_low, preferred_...]
    broadcast_in_dim x1 -> x21, local copies, waits for them, and re-layouts: 1.09 us -> 19.2 us  [the longest x8 5.41 us: column_sum(): return jnp.sum(values.astype(jnp.float32), 0, keepdims=True)]
  transfers between devices with their start and end apart: 29 -> 20, of which waited for: 15 -> 9; matrix products, arithmetic and copies ran while one was open for 31% -> 36% of each run, Pallas kernels for 13% -> 22%
where the time goes in v2:
time: 1050 us; the launch traced here: 1030 us
  Pallas kernels  313 us (30%)
  matrix products  230 us (22%)
  waiting for transfers between devices  180 us (17%)
  local copies, waits for them, and re-layouts  175 us (17%)
  other arithmetic  84.5 us (8%)
  starting transfers between devices  34.5 us (3%)
  between operations  18.3 us (2%)
    all_gather x4, waiting for transfers between devices, gather_rows(): whole = lax.all_gather(block, 'shard', axis=0, tiled=True)  89 us
    pallas_call x1, Pallas kernels, reduce_chunks(): pl.pallas_call(functools.partial(reduce_kernel, count, seqs, sizes), in_s...  88 us
    dot_general x19, matrix products, bdot(): return jnp.dot(left_side, right_side, preferred_element_type=jnp.float32)  75.2 us
    dot_general x19, matrix products, turned_dot(): lax.dot_general(left_side, right_side, NT, preferred_element_type=jnp.flo...  68 us
    unnamed x617, local copies, waits for them, and re-layouts  63.3 us
    dot_general x19, matrix products, rows_dot(): lax.dot_general(left_side, right_side, (((0,), (0,)), ((), ())), preferre...  58.1 us
    pallas_call x2, Pallas kernels, attend_back(): pl.pallas_call(functools.partial(attend_back_kernel, blocks), grid=(clips...  55.4 us
    pallas_call x1, Pallas kernels, conv_forward(): pl.pallas_call(functools.partial(conv_forward_kernel, rows, shards), grid...  39 us
  transfers between devices with their start and end apart: 20, of which 9 were waited for; matrix products, arithmetic and copies ran while one was open for 36% of the time, Pallas kernels for 22%

profile of v2, /device:TPU:0, one launch (start us, length us, event | category | flops | bytes accessed | tf_op | source)
XLA Modules:
  0.0 1034.7 jit_solution(7736509790299539332)
XLA Ops:
  16.4 28.2 %count_draws.1.refs_0_ = bf16[2,768,384]{2,1,0:T(8,128)(2,1)} custom-call(s32[2,100,384]{2,1,0:T(8,128)} %fusion.69.n_ref), custom_call_target="tpu_custom_call" | custom-call | flops 1024 | bytes 1024 | tf_op jit(solution)/shard_map/count_draws/pallas_call | solution.py:400
  49.0 59.3 %all-gather.5.cloned.1.call-done = bf16[14336,384]{1,0:T(8,128)(2,1)} async-done(((bf16[896,384]{1,0:T(8,128)(2,1)}), bf16[14336,384]{1,0:T(8,128)(2,1)}) %all-gather.5.cloned.1.call-update) | async-done | bytes 11010064 | tf_op jit(solution)/shard_map/all_gather | solution.py:701
  114.6 3.4 collective-permute-start
  122.6 4.1 collective-permute-done.1
  129.3 5.7 copy.173
  135.0 39.0 %conv_forward.1 = f32[48,16,1024]{2,1,0:T(8,128)} custom-call(bf16[176,16,1024]{2,1,0:T(8,128)(2,1)} %bitcast.392, bf16[16,896,384]{2,1,0:T(8,128)(2,1)} %bitcast.395), custom_call_target="tpu_custom_call" | custom-call | flops 1024 | bytes 1024 | tf_op jit(solution)/shard_map/conv_forward/pallas_call | solution.py:120
  174.0 3.7 copy.132
  178.4 2.8 fusion.108
  181.3 3.7 fusion.124
  190.2 29.7 %all-gather.7.cloned.1.call-done = bf16[9216,768]{1,0:T(8,128)(2,1)} async-done(((bf16[576,768]{1,0:T(8,128)(2,1)}), bf16[9216,768]{1,0:T(8,128)(2,1)}) %all-gather.7.cloned.1.call-update) | async-done | bytes 14155792 | tf_op jit(solution)/shard_map/all_gather | solution.py:701
  219.9 14.9 %fusion.125 = (bf16[16,48,768]{2,1,0:T(8,128)(2,1)}, bf16[16,48,768]{2,1,0:T(8,128)(2,1)}, bf16[16,48,768]{2,1,0:T(8,128)(2,1)}, bf16[16,48,768]{2,1,0:T(8,128)(...) fusion(bf16[16,576,768]{2,1,0:T(8,128)(2,1)} %bitcast.415), kind=kLoop, calls=%fused_computation.426 | loop fusion | bytes 18874368 | tf_op jit(solution)/shard_map/slice | solution.py:805
  241.2 3.4 add_convert_fusion.10.refs_3_
  244.6 3.4 convolution_convert_fusion.15.refs_2_
  248.0 18.6 %attend.2 = (bf16[768,768]{1,0:T(8,128)(2,1)}, f32[2,6,2,384]{3,2,1,0:T(2,128)}) custom-call(bf16[768,768]{1,0:T(8,128)(2,1)} %add_convert_fusion.12.q_ref, bf16[768,768]{1,0:T(8,128)(2,1)} %convolution_convert_fusion.16.refs_0_, bf16[768,768]{1,0:T(8,128)(2,1)} %add_convert_fusion.11.refs_1_, bf16[768,768]{1,0:T(8,128)(2,1)} %convolution_convert_fusion.15.refs_2_, ...), custom_call_target="tpu_custom_call" | custom-call | flops 1024 | bytes 1024 | tf_op jit(solution)/shard_map/attend/pallas_call | solution.py:302
  282.0 3.1 slice.605
  290.0 9.8 multiply_convert_fusion.3
  299.9 6.1 fusion.141
  310.5 4.2 fusion.129
  314.7 4.2 convolution_convert_fusion.14.refs_0_
  318.9 17.5 %collective-permute-done.3 = bf16[768,768]{1,0:T(8,128)(2,1)} collective-permute-done((bf16[768,768]{1,0:T(8,128)(2,1)}, bf16[768,768]{1,0:T(8,128)(2,1)}, u32[]{:S(2)}, u32[]{:S(2)}) %collective-permute-start.3) | collective-permute-done | bytes 1179680 | tf_op jit(solution)/shard_map/ppermute | solution.py:537
  336.3 3.4 convolution_convert_fusion.13.refs_2_
  339.7 3.4 add_convert_fusion.9.q_ref
  343.2 3.4 add_convert_fusion.8.refs_1_
  346.5 3.4 add_convert_fusion.7.refs_3_
  350.8 18.8 %attend.3 = (bf16[768,768]{1,0:T(8,128)(2,1)}, f32[2,6,2,384]{3,2,1,0:T(2,128)}) custom-call(bf16[768,768]{1,0:T(8,128)(2,1)} %add_convert_fusion.9.q_ref, bf16[768,768]{1,0:T(8,128)(2,1)} %convolution_convert_fusion.14.refs_0_, bf16[768,768]{1,0:T(8,128)(2,1)} %add_convert_fusion.8.refs_1_, bf16[768,768]{1,0:T(8,128)(2,1)} %convolution_convert_fusion.13.refs_2_, ...), custom_call_target="tpu_custom_call" | custom-call | flops 1024 | bytes 1024 | tf_op jit(solution)/shard_map/attend/pallas_call | solution.py:302
  374.9 2.8 slice.623
  383.3 10.5 %multiply_convert_fusion.2 = (bf16[768,3072]{1,0:T(8,128)(2,1)S(1)}, f32[768,3072]{1,0:T(8,128)}) fusion(f32[3072]{0:T(1024)S(1)} %copy-done.225, bf16[768,768]{1,0:T(8,128)(2,1)} %bitcast.498, bf16[768,768]{1,0:T(8,128)(2,1)} %bitcast.500, bf16[768,768]{1,0:T(8,128)(2,1)} %bitcast.502, bf16[768,768]{1,0:T(8,128)(2,1)S(1)} %bitcast.496, ...), kind=kOutput, calls=%fused_computation.16 | convolution fusion | flops 3659857920 | bytes 21258240 | tf_op jit(solution)/shard_map/dot_general | solution.py:557
  393.8 4.1 fusion.143
  402.1 3.5 broadcast_in_dim.100
  405.6 4.6 all-to-all-start
  422.4 11.6 %convert_reduce_fusion = (f32[3072]{0:T(1024)}, bf16[768,3072]{1,0:T(8,128)(2,1)}) fusion(bf16[3072,768]{1,0:T(8,128)(2,1)S(1)} %bitcast.457, f32[768,768]{1,0:T(8,128)S(1)} %get-tuple-element.241, f32[768,3072]{1,0:T(8,128)} %get-tuple-element.349, f32[3072]{0:T(1024)S(1)} %copy-done.226), kind=kOutput, calls=%fused_computation.12 | convolution fusion | flops 3659854848 | bytes 21258240 | tf_op jit(solution)/shard_map/dot_general | solution.py:561
  434.0 7.5 multiply_reduce_fusion.2
  445.6 27.5 %attend_back.2 = (bf16[768,768]{1,0:T(8,128)(2,1)}, bf16[768,768]{1,0:T(8,128)(2,1)}, bf16[768,768]{1,0:T(8,128)(2,1)}, bf16[768,768]{1,0:T(8,128)(2,1)}, bf16[768,768]{1,0:T(8,128)(2,1)}) custom-call(bf16[768,768]{1,0:T(8,128)(2,1)} %add_convert_fusion.9.q_ref, bf16[768,768]{1,0:T(8,128)(2,1)} %convolution_convert_fusion.12.d_ref, ...), custom_call_target="tpu_custom_call" | custom-call | flops 1024 | bytes 1024 | tf_op jit(solution)/shard_map/attend_back/pallas_call | solution.py:374
  473.1 6.8 convolution_convert_fusion.3
  482.9 8.2 convolution_convert_fusion.2
  491.0 2.8 convolution_convert_fusion.10
  522.4 11.0 %collective-permute-done.5 = bf16[768,768]{1,0:T(8,128)(2,1)} collective-permute-done((bf16[768,768]{1,0:T(8,128)(2,1)}, bf16[768,768]{1,0:T(8,128)(2,1)}, u32[]{:S(2)}, u32[]{:S(2)}) %collective-permute-start.5) | collective-permute-done | bytes 1179680 | tf_op jit(solution)/shard_map/ppermute | solution.py:542
  533.4 4.0 convert_add_fusion.1.refs_0_
  537.7 3.4 multiply_reduce_fusion.3
  542.7 13.2 %convert_reduce_fusion.1 = (f32[3072]{0:T(1024)}, bf16[768,3072]{1,0:T(8,128)(2,1)S(1)}) fusion(bf16[3072,768]{1,0:T(8,128)(2,1)} %bitcast.452, f32[768,768]{1,0:T(8,128)S(1)} %get-tuple-element.243, f32[768,3072]{1,0:T(8,128)} %get-tuple-element.343, f32[3072]{0:T(1024)S(1)} %copy-done.224), kind=kOutput, calls=%fused_computation.13 | convolution fusion | flops 3659854848 | bytes 21258240 | tf_op jit(solution)/shard_map/dot_general | solution.py:561
  556.0 5.1 multiply_reduce_fusion.4
  564.6 27.9 %attend_back.3 = (bf16[768,768]{1,0:T(8,128)(2,1)}, bf16[768,768]{1,0:T(8,128)(2,1)}, bf16[768,768]{1,0:T(8,128)(2,1)}, bf16[768,768]{1,0:T(8,128)(2,1)}, bf16[768,768]{1,0:T(8,128)(2,1)}) custom-call(bf16[768,768]{1,0:T(8,128)(2,1)} %add_convert_fusion.12.q_ref, bf16[768,768]{1,0:T(8,128)(2,1)} %convolution_convert_fusion.9.d_ref, ...), custom_call_target="tpu_custom_call" | custom-call | flops 1024 | bytes 1024 | tf_op jit(solution)/shard_map/attend_back/pallas_call | solution.py:374
  615.4 6.9 convolution_convert_fusion.1
  624.3 7.1 convolution_convert_fusion
  638.6 4.1 convert_add_fusion.refs_0_
  649.0 3.9 fusion.45
  662.9 3.3 collective-permute-start.7
  688.0 3.2 copy.172
  695.9 31.3 %conv_weight_grad.1.refs_1_ = bf16[16,768,384]{2,1,0:T(8,128)(2,1)} custom-call(bf16[176,16,1024]{2,1,0:T(8,128)(2,1)} %bitcast.393, bf16[48,16,1024]{2,1,0:T(8,128)(2,1)} %slice.654.d_ref), custom_call_target="tpu_custom_call" | custom-call | flops 1024 | bytes 1024 | tf_op jit(solution)/shard_map/conv_weight_grad/pallas_call | solution.py:200
  727.2 4.0 collective-permute-start.9
  743.5 31.6 %conv_input_grad.1.refs_0_ = f32[48,16,1024]{2,1,0:T(8,128)} custom-call(bf16[176,16,1024]{2,1,0:T(8,128)(2,1)} %get-tuple-element.116.d_ref, bf16[16,896,384]{2,1,0:T(8,128)(2,1)} %bitcast.396), custom_call_target="tpu_custom_call" | custom-call | flops 1024 | bytes 1024 | tf_op jit(solution)/shard_map/conv_input_grad/pallas_call | solution.py:156
  777.2 3.7 copy.140
  781.7 3.0 fusion.107
  798.9 33.7 %reduce-scatter.5.cloned.1.call-done = bf16[1,576,768]{2,1,0:T(8,128)(2,1)} async-done(((bf16[16,576,768]{2,1,0:T(8,128)(2,1)}), bf16[1,576,768]{2,1,0:T(8,128)(2,1)}) %reduce-scatter.5.cloned.1.call-update) | async-done | bytes 884752 | tf_op jit(solution)/shard_map/reduce_scatter | solution.py:725
  838.3 4.4 convert_multiply_fusion.1
  845.8 7.6 collective-permute-done.10
  856.3 5.1 all-to-all-start.1
  866.3 3.7 multiply_subtract_fusion
  872.4 14.2 %all-to-all-done.1 = bf16[16,48,768]{2,1,0:T(8,128)(2,1)} async-done(((bf16[16,48,768]{2,1,0:T(8,128)(2,1)}), bf16[16,48,768]{2,1,0:T(8,128)(2,1)}, u32[]{:S(2)}, u32[]{:S(2)}) %all-to-all-start.1) | async-done | bytes 1179680 | tf_op jit(solution)/shard_map/all_to_all | solution.py:729
  886.6 7.5 fusion.25
  899.4 88.0 %reduce_chunks.1 = (f32[128,384]{1,0:T(8,128)}, f32[768,384]{1,0:T(8,128)}) custom-call(bf16[16,128,384]{2,1,0:T(8,128)(2,1)} %get-tuple-element.123.refs_0_, bf16[16,768,384]{2,1,0:T(8,128)(2,1)} %get-tuple-element.124.refs_1_), custom_call_target="tpu_custom_call" | custom-call | flops 1024 | bytes 1024 | tf_op jit(solution)/shard_map/reduce_chunks/pallas_call | solution.py:518
  989.3 4.0 all-to-all-start.2
  993.3 4.0 multiply_subtract_fusion.2
  997.2 2.8 copy.150
  (915 shorter events, 287.6 us)
Async XLA Ops:
  7.2 101.0 %all-gather.5.cloned.1.call-start = ((), (), s32[]{:S(2)}) async-start(), calls=%async_computation.5 | async-start | bytes 11698176 | tf_op jit(solution)/shard_map/all_gather | solution.py:701
  14.3 30.3 %copy-start.47 = (f32[8,48,768]{2,1,0:T(8,128)S(1)}, f32[8,48,768]{2,1,0:T(8,128)}, u32[]{:S(2)}) copy-start(f32[8,48,768]{2,1,0:T(8,128)} %param.43) | copy-start | bytes 3538948
  14.3 30.4 %copy-start.62 = (f32[2,48,3072]{2,1,0:T(8,128)S(1)}, f32[2,48,3072]{2,1,0:T(8,128)}, u32[]{:S(2)}) copy-start(f32[2,48,3072]{2,1,0:T(8,128)} %param.48) | copy-start | bytes 3538948
  14.4 205.6 %all-gather.7.cloned.1.call-start = ((), (), s32[]{:S(2)}) async-start(), calls=%async_computation.6 | async-start | bytes 15040512 | tf_op jit(solution)/shard_map/all_gather | solution.py:701
  16.4 28.3 %copy-start.60 = (f32[2,192,768]{2,1,0:T(8,128)S(1)}, f32[2,192,768]{2,1,0:T(8,128)}, u32[]{:S(2)}) copy-start(f32[2,192,768]{2,1,0:T(8,128)} %param.51) | copy-start | bytes 3538948
  47.4 263.1 %all-gather.9.cloned.1.call-start = ((), (), s32[]{:S(2)}) async-start(), calls=%async_computation.7 | async-start | bytes 5013504 | tf_op jit(solution)/shard_map/all_gather | solution.py:701
  47.5 133.8 %copy-start.260 = (pred[768]{0:T(1024)(128)(4,1)}, pred[768]{0:T(1024)(128)(4,1)S(1)}, u32[]{:S(2)}) copy-start(pred[768]{0:T(1024)(128)(4,1)S(1)} %broadcast_in_dim.95) | copy-start | bytes 2308
  47.5 133.8 %copy-start.262 = (pred[768]{0:T(1024)(128)(4,1)}, pred[768]{0:T(1024)(128)(4,1)S(1)}, u32[]{:S(2)}) copy-start(pred[768]{0:T(1024)(128)(4,1)S(1)} %get-tuple-element.371) | copy-start | bytes 2308
  47.5 133.8 %copy-start.265 = (pred[768]{0:T(1024)(128)(4,1)}, pred[768]{0:T(1024)(128)(4,1)S(1)}, u32[]{:S(2)}) copy-start(pred[768]{0:T(1024)(128)(4,1)S(1)} %get-tuple-element.372) | copy-start | bytes 2308
  47.5 133.8 %copy-start.248 = (s32[768]{0:T(1024)}, s32[768]{0:T(1024)S(1)}, u32[]{:S(2)}) copy-start(s32[768]{0:T(1024)S(1)} %get-tuple-element.369) | copy-start | bytes 9220
  47.5 133.8 %copy-start.251 = (s32[768]{0:T(1024)}, s32[768]{0:T(1024)S(1)}, u32[]{:S(2)}) copy-start(s32[768]{0:T(1024)S(1)} %get-tuple-element.370) | copy-start | bytes 9220
  47.6 133.8 %copy-start.254 = (s32[768]{0:T(1024)}, s32[768]{0:T(1024)S(1)}, u32[]{:S(2)}) copy-start(s32[768]{0:T(1024)S(1)} %get-tuple-element.367) | copy-start | bytes 9220
  47.6 133.8 %copy-start.257 = (s32[768]{0:T(1024)}, s32[768]{0:T(1024)S(1)}, u32[]{:S(2)}) copy-start(s32[768]{0:T(1024)S(1)} %get-tuple-element.368) | copy-start | bytes 9220
  48.6 63.7 %copy-start.171 = (f32[2,384]{1,0:T(2,128)}, f32[2,384]{1,0:T(2,128)S(1)}, u32[]{:S(2)}) copy-start(f32[2,384]{1,0:T(2,128)S(1)} %broadcast_multiply_fusion.15) | copy-start | bytes 9220
  49.0 63.3 %copy-start.190 = (f32[2,384]{1,0:T(2,128)}, f32[2,384]{1,0:T(2,128)S(1)}, u32[]{:S(2)}) copy-start(f32[2,384]{1,0:T(2,128)S(1)} %add_rsqrt_fusion.7) | copy-start | bytes 9220
  114.6 7.9 collective-permute-start
  118.0 8.7 collective-permute-start.1
  120.2 65.3 %copy-start.164 = (f32[768]{0:T(1024)}, f32[768]{0:T(1024)S(1)}, u32[]{:S(2)}) copy-start(f32[768]{0:T(1024)S(1)} %get-tuple-element.329) | copy-start | bytes 9220
  188.3 186.6 %all-gather.11.cloned.1.call-start = ((), (), s32[]{:S(2)}) async-start(), calls=%async_computation.8 | async-start | bytes 10027008 | tf_op jit(solution)/shard_map/all_gather | solution.py:701
  190.1 49.0 %copy-start.110 = (bf16[768,768]{1,0:T(8,128)(2,1)}, bf16[768,768]{1,0:T(8,128)(2,1)S(1)}, u32[]{:S(2)}) copy-start(bf16[768,768]{1,0:T(8,128)(2,1)S(1)} %convert_element_type.442) | copy-start | bytes 3538948
  190.2 51.1 %collective-permute-start.2 = (bf16[768,768]{1,0:T(8,128)(2,1)S(1)}, bf16[768,768]{1,0:T(8,128)(2,1)}, u32[]{:S(2)}, u32[]{:S(2)}) collective-permute-start(bf16[768,768]{1,0:T(8,128)(2,1)S(1)} %convert_element_type.442), channel_id=1, source_target_pairs={{0,16},{16,0},{1,17},{17,1},{2,18},{18,2},{3,19},{19,3},{4,20},{20... | collective-permute-start | bytes 3538952 | tf_op jit(solution)/shard_map/ppermute | solution.py:537
  267.3 7.5 collective-permute-start.4
  280.5 28.7 %copy-start.14 = (f32[1536,256]{1,0:T(8,128)}, f32[1536,256]{1,0:T(8,128)S(1)}, u32[]{:S(2)}) copy-start(f32[1536,256]{1,0:T(8,128)S(1)} %get-tuple-element.353) | copy-start | bytes 4718596
  280.5 28.7 %copy-start.160 = (f32[1536]{0:T(1024)}, f32[1536]{0:T(1024)S(1)}, u32[]{:S(2)}) copy-start(f32[1536]{0:T(1024)S(1)} %add_rsqrt_fusion) | copy-start | bytes 18436
  285.1 14.7 %copy-start.54 = (bf16[16,192,768]{2,1,0:T(8,128)(2,1)}, bf16[16,192,768]{2,1,0:T(8,128)(2,1)S(1)}, u32[]{:S(2)}) copy-start(bf16[16,192,768]{2,1,0:T(8,128)(2,1)S(1)} %slice.605) | copy-start | bytes 14155780
  308.1 28.2 %collective-permute-start.3 = (bf16[768,768]{1,0:T(8,128)(2,1)}, bf16[768,768]{1,0:T(8,128)(2,1)}, u32[]{:S(2)}, u32[]{:S(2)}) collective-permute-start(bf16[768,768]{1,0:T(8,128)(2,1)} %fusion.28), channel_id=1, source_target_pairs={{0,16},{16,0},{1,17},{17,1},{2,18},{18,2},{3,19},{19,3},{4,20},{20... | collective-permute-start | bytes 3538952 | tf_op jit(solution)/shard_map/ppermute | solution.py:537
  314.6 21.7 %copy-start.98 = (bf16[16,48,768]{2,1,0:T(8,128)(2,1)}, bf16[16,48,768]{2,1,0:T(8,128)(2,1)S(1)}, u32[]{:S(2)}) copy-start(bf16[16,48,768]{2,1,0:T(8,128)(2,1)S(1)} %get-tuple-element.276) | copy-start | bytes 3538948
  314.6 25.1 %copy-start.101 = (bf16[16,48,768]{2,1,0:T(8,128)(2,1)}, bf16[16,48,768]{2,1,0:T(8,128)(2,1)S(1)}, u32[]{:S(2)}) copy-start(bf16[16,48,768]{2,1,0:T(8,128)(2,1)S(1)} %get-tuple-element.277) | copy-start | bytes 3538948
  314.7 31.9 %copy-start.42 = (bf16[16,48,768]{2,1,0:T(8,128)(2,1)}, bf16[16,48,768]{2,1,0:T(8,128)(2,1)S(1)}, u32[]{:S(2)}) copy-start(bf16[16,48,768]{2,1,0:T(8,128)(2,1)S(1)} %get-tuple-element.275) | copy-start | bytes 3538948
  318.9 20.8 %copy-start.241 = (f32[768]{0:T(1024)S(1)}, f32[768]{0:T(1024)}, u32[]{:S(2)}) copy-start(f32[768]{0:T(1024)} %get-tuple-element.319) | copy-start | bytes 9220
  350.8 18.8 %copy-start.103 = (bf16[16,48,768]{2,1,0:T(8,128)(2,1)S(1)}, bf16[16,48,768]{2,1,0:T(8,128)(2,1)}, u32[]{:S(2)}) copy-start(bf16[16,48,768]{2,1,0:T(8,128)(2,1)} %get-tuple-element.274) | copy-start | bytes 3538948
  350.8 18.9 %copy-start.239 = (f32[768]{0:T(1024)S(1)}, f32[768]{0:T(1024)}, u32[]{:S(2)}) copy-start(f32[768]{0:T(1024)} %get-tuple-element.317) | copy-start | bytes 9220
  372.4 21.4 %copy-start.177 = (f32[768]{0:T(1024)}, f32[768]{0:T(1024)S(1)}, u32[]{:S(2)}) copy-start(f32[768]{0:T(1024)S(1)} %broadcast_multiply_fusion.11) | copy-start | bytes 9220
  380.0 13.8 %copy-start.55 = (bf16[16,192,768]{2,1,0:T(8,128)(2,1)}, bf16[16,192,768]{2,1,0:T(8,128)(2,1)S(1)}, u32[]{:S(2)}) copy-start(bf16[16,192,768]{2,1,0:T(8,128)(2,1)S(1)} %slice.623) | copy-start | bytes 14155780
  405.6 85.4 %all-to-all-start = ((bf16[16,3,48,768]{3,2,1,0:T(8,128)(2,1)}), bf16[16,3,48,768]{3,2,1,0:T(8,128)(2,1)}, u32[]{:S(2)}, u32[]{:S(2)}) async-start(bf16[16,3,48,768]{3,2,1,0:T(8,128)(2,1)} %bitcast.417), calls=%async_computation | async-start | bytes 7077888 | tf_op jit(solution)/shard_map/all_to_all | solution.py:729
  410.3 316.9 %reduce-scatter.3.cloned.1.call-start = ((), (), s32[]{:S(2)}) async-start(), calls=%async_computation.9 | async-start | bytes 15040512 | tf_op jit(solution)/shard_map/reduce_scatter | solution.py:725
  445.6 27.5 %copy-start.237 = (f32[768]{0:T(1024)S(1)}, f32[768]{0:T(1024)}, u32[]{:S(2)}) copy-start(f32[768]{0:T(1024)} %get-tuple-element.315) | copy-start | bytes 9220
  505.0 28.4 %collective-permute-start.5 = (bf16[768,768]{1,0:T(8,128)(2,1)}, bf16[768,768]{1,0:T(8,128)(2,1)}, u32[]{:S(2)}, u32[]{:S(2)}) collective-permute-start(bf16[768,768]{1,0:T(8,128)(2,1)} %add_convert_fusion.5), channel_id=1, source_target_pairs={{0,16},{16,0},{1,17},{17,1},{2,18},{18,2},{3,19},{19,3},{4,20},{20... | collective-permute-start | bytes 3538952 | tf_op jit(solution)/shard_map/ppermute | solution.py:542
  519.4 14.0 %copy-start.25 = (f32[768,768]{1,0:T(8,128)S(1)}, f32[768,768]{1,0:T(8,128)}, u32[]{:S(2)}) copy-start(f32[768,768]{1,0:T(8,128)} %get-tuple-element.251) | copy-start | bytes 7077892
  537.5 295.2 %reduce-scatter.5.cloned.1.call-start = ((), (), s32[]{:S(2)}) async-start(), calls=%async_computation.10 | async-start | bytes 15040512 | tf_op jit(solution)/shard_map/reduce_scatter | solution.py:725
  542.6 13.2 %copy-start.78 = (f32[768,768]{1,0:T(8,128)}, f32[768,768]{1,0:T(8,128)S(1)}, u32[]{:S(2)}) copy-start(f32[768,768]{1,0:T(8,128)S(1)} %get-tuple-element.243) | copy-start | bytes 7077892
  542.7 13.2 %copy-start.27 = (f32[768,768]{1,0:T(8,128)S(1)}, f32[768,768]{1,0:T(8,128)}, u32[]{:S(2)}) copy-start(f32[768,768]{1,0:T(8,128)} %copy-done.26) | copy-start | bytes 7077892
  542.7 13.2 %copy-start.91 = (bf16[16,48,768]{2,1,0:T(8,128)(2,1)S(1)}, bf16[16,48,768]{2,1,0:T(8,128)(2,1)}, u32[]{:S(2)}) copy-start(bf16[16,48,768]{2,1,0:T(8,128)(2,1)} %get-tuple-element.255) | copy-start | bytes 3538948
  542.7 13.2 %copy-start.93 = (bf16[16,48,768]{2,1,0:T(8,128)(2,1)S(1)}, bf16[16,48,768]{2,1,0:T(8,128)(2,1)}, u32[]{:S(2)}) copy-start(bf16[16,48,768]{2,1,0:T(8,128)(2,1)} %get-tuple-element.256) | copy-start | bytes 3538948
  542.7 13.2 %copy-start.95 = (bf16[16,48,768]{2,1,0:T(8,128)(2,1)S(1)}, bf16[16,48,768]{2,1,0:T(8,128)(2,1)}, u32[]{:S(2)}) copy-start(bf16[16,48,768]{2,1,0:T(8,128)(2,1)} %get-tuple-element.257) | copy-start | bytes 3538948
  542.7 13.2 %copy-start.97 = (bf16[16,48,768]{2,1,0:T(8,128)(2,1)S(1)}, bf16[16,48,768]{2,1,0:T(8,128)(2,1)}, u32[]{:S(2)}) copy-start(bf16[16,48,768]{2,1,0:T(8,128)(2,1)} %get-tuple-element.258) | copy-start | bytes 3538948
  542.7 13.2 %copy-start.176 = (f32[768]{0:T(1024)S(1)}, f32[768]{0:T(1024)}, u32[]{:S(2)}) copy-start(f32[768]{0:T(1024)} %copy-done.175) | copy-start | bytes 9220
  542.7 13.2 %copy-start.197 = (f32[768]{0:T(1024)S(1)}, f32[768]{0:T(1024)}, u32[]{:S(2)}) copy-start(f32[768]{0:T(1024)} %get-tuple-element.324) | copy-start | bytes 9220
  542.7 13.2 %copy-start.201 = (f32[768]{0:T(1024)S(1)}, f32[768]{0:T(1024)}, u32[]{:S(2)}) copy-start(f32[768]{0:T(1024)} %copy-done.200) | copy-start | bytes 9220
  598.6 40.0 %collective-permute-start.6 = (bf16[768,768]{1,0:T(8,128)(2,1)}, bf16[768,768]{1,0:T(8,128)(2,1)}, u32[]{:S(2)}, u32[]{:S(2)}) collective-permute-start(bf16[768,768]{1,0:T(8,128)(2,1)} %add_convert_fusion.2), channel_id=1, source_target_pairs={{0,16},{16,0},{1,17},{17,1},{2,18},{18,2},{3,19},{19,3},{4,20},{20... | collective-permute-start | bytes 3538952 | tf_op jit(solution)/shard_map/ppermute | solution.py:542
  661.1 18.2 %copy-start.206 = (f32[768]{0:T(1024)S(1)}, f32[768]{0:T(1024)}, u32[]{:S(2)}) copy-start(f32[768]{0:T(1024)} %get-tuple-element.240) | copy-start | bytes 9220
  662.9 21.1 %collective-permute-start.7 = (bf16[2,64,768]{2,1,0:T(8,128)(2,1)}, bf16[2,64,768]{2,1,0:T(8,128)(2,1)}, u32[]{:S(2)}, u32[]{:S(2)}) collective-permute-start(bf16[2,64,768]{2,1,0:T(8,128)(2,1)} %get-tuple-element.297), channel_id=1, source_target_pairs={{0,16},{1,17},{2,18},{3,19},{4,20},{5,21},{6,22},{7,23},{8,24},{9,... | collective-permute-start | bytes 589832 | tf_op jit(solution)/shard_map/ppermute | solution.py:620
  666.2 17.7 %collective-permute-start.8 = (bf16[2,64,768]{2,1,0:T(8,128)(2,1)}, bf16[2,64,768]{2,1,0:T(8,128)(2,1)}, u32[]{:S(2)}, u32[]{:S(2)}) collective-permute-start(bf16[2,64,768]{2,1,0:T(8,128)(2,1)} %get-tuple-element.298), channel_id=1, source_target_pairs={{16,0},{17,1},{18,2},{19,3},{20,4},{21,5},{22,6},{23,7},{24,8},{25... | collective-permute-start | bytes 589832 | tf_op jit(solution)/shard_map/ppermute | solution.py:621
  727.2 13.3 %copy-start.51 = (bf16[768,768]{1,0:T(8,128)(2,1)S(1)}, bf16[768,768]{1,0:T(8,128)(2,1)}, u32[]{:S(2)}) copy-start(bf16[768,768]{1,0:T(8,128)(2,1)} %get-tuple-element.108) | copy-start | bytes 3538948
  727.2 14.1 %copy-start.19 = (bf16[768,768]{1,0:T(8,128)(2,1)S(1)}, bf16[768,768]{1,0:T(8,128)(2,1)}, u32[]{:S(2)}) copy-start(bf16[768,768]{1,0:T(8,128)(2,1)} %get-tuple-element.110) | copy-start | bytes 3538948
  727.2 47.9 %collective-permute-start.9 = (bf16[576,768]{1,0:T(8,128)(2,1)}, bf16[576,768]{1,0:T(8,128)(2,1)S(1)}, u32[]{:S(2)}, u32[]{:S(2)}) collective-permute-start(bf16[576,768]{1,0:T(8,128)(2,1)} %get-tuple-element.117), channel_id=1, source_target_pairs={{0,16},{16,0},{1,17},{17,1},{2,18},{18,2},{3,19},{19,3},{4,20},{20... | collective-permute-start | bytes 2654216 | tf_op jit(solution)/shard_map/ppermute | solution.py:548
  743.5 31.6 %copy-start.72 = (bf16[576,768]{1,0:T(8,128)(2,1)S(1)}, bf16[576,768]{1,0:T(8,128)(2,1)}, u32[]{:S(2)}) copy-start(bf16[576,768]{1,0:T(8,128)(2,1)} %get-tuple-element.117) | copy-start | bytes 2654212
  798.9 35.2 %copy-start.117 = (f32[384,768]{1,0:T(8,128)S(1)}, f32[384,768]{1,0:T(8,128)}, u32[]{:S(2)}) copy-start(f32[384,768]{1,0:T(8,128)} %param.41) | copy-start | bytes 3538948
  832.7 20.8 %collective-permute-start.10 = (bf16[576,768]{1,0:T(8,128)(2,1)}, bf16[576,768]{1,0:T(8,128)(2,1)}, u32[]{:S(2)}, u32[]{:S(2)}) collective-permute-start(bf16[576,768]{1,0:T(8,128)(2,1)} %get-tuple-element.120), channel_id=1, source_target_pairs={{0,16},{16,0},{1,17},{17,1},{2,18},{18,2},{3,19},{19,3},{4,20},{20... | collective-permute-start | bytes 2654216 | tf_op jit(solution)/shard_map/ppermute | solution.py:548
  856.3 30.3 %all-to-all-start.1 = ((bf16[16,48,768]{2,1,0:T(8,128)(2,1)}), bf16[16,48,768]{2,1,0:T(8,128)(2,1)}, u32[]{:S(2)}, u32[]{:S(2)}) async-start(bf16[16,48,768]{2,1,0:T(8,128)(2,1)} %bitcast.109), calls=%async_computation.3 | async-start | bytes 2359296 | tf_op jit(solution)/shard_map/all_to_all | solution.py:729
  870.0 16.6 %copy-start.119 = (bf16[16,1,48,768]{3,2,1,0:T(8,128)(2,1)S(1)}, bf16[16,1,48,768]{3,2,1,0:T(8,128)(2,1)}, u32[]{:S(2)}) copy-start(bf16[16,1,48,768]{3,2,1,0:T(8,128)(2,1)} %slice.513) | copy-start | bytes 3538948
  989.3 29.5 %all-to-all-start.2 = ((bf16[16,2,48,384]{3,2,1,0:T(8,128)(2,1)}), bf16[16,2,48,384]{3,2,1,0:T(8,128)(2,1)S(1)}, u32[]{:S(2)}, u32[]{:S(2)}) async-start(bf16[16,2,48,384]{3,2,1,0:T(8,128)(2,1)} %get-tuple-element.127), calls=%async_computation.4 | async-start | bytes 2359296 | tf_op jit(solution)/shard_map/all_to_all | solution.py:729
  997.2 13.3 %copy-start.69 = (f32[384,768]{0,1:T(8,128)S(1)}, f32[384,768]{0,1:T(8,128)}, u32[]{:S(2)}) copy-start(f32[384,768]{0,1:T(8,128)} %get-tuple-element.231) | copy-start | bytes 3538948
  997.2 14.8 %copy-start.68 = (f32[384,768]{0,1:T(8,128)S(1)}, f32[384,768]{0,1:T(8,128)}, u32[]{:S(2)}) copy-start(f32[384,768]{0,1:T(8,128)} %get-tuple-element.232) | copy-start | bytes 3538948
  (233 other events, 894.2 us)
Sparse Core Ops, SparseCore 0:
  14.4 93.8 all-gather.4
  111.1 108.7 all-gather.6
  222.2 51.5 all-gather.8
  276.0 79.9 all-gather.10
  537.6 146.3 reduce-scatter.2
  688.0 144.6 reduce-scatter.4

commit v3 on v2

--- a/solution.py
+++ b/solution.py
@@ -17,7 +17,7 @@
 QGROUPS = 2
 LAYERS = 2
 STEP = 10
-SMALL_LANES = 6144
+SMALL_ROWS = 160
 
 
 beta_one = 0.9
@@ -44,6 +44,7 @@
 STEPS = HALF + 1
 VMEM = 56 * 1024 * 1024
 SMALL_COST = pl.CostEstimate(flops=1024, bytes_accessed=1024, transcendentals=0)
+CONV_COST = pl.CostEstimate(flops=35 * 10**9, bytes_accessed=10**7, transcendentals=0)
 NT = (((1,), (1,)), ((), ()))
 NN = (((1,), (0,)), ((), ()))
 
@@ -115,14 +116,14 @@
     unpack_pair(results[0], results[1], y_ref, rows)
 
 
-def conv_forward(x, w, rows, shards):
+def conv_forward(x, w, first, rows, shards):
     frames = PACK * (rows + HALF)
     return pl.pallas_call(
         functools.partial(conv_forward_kernel, rows, shards),
         grid=(GROUPS // 2,),
         in_specs=[
             pl.BlockSpec((frames, 16, 128), lambda g: (0, 0, g)),
-            pl.BlockSpec((shards, 2 * GC, w.shape[2]), lambda g: (0, g, 0)),
+            pl.BlockSpec((shards, 2 * GC, w.shape[2]), lambda g: (0, first + g, 0)),
         ],
         out_specs=pl.BlockSpec((PACK * rows, 16, 128), lambda g: (0, 0, g)),
         out_shape=jax.ShapeDtypeStruct((PACK * rows, 16, PADW), jnp.float32),
@@ -151,14 +152,14 @@
     unpack_pair(results[0], results[1], dx_ref, rows)
 
 
-def conv_input_grad(d, w, rows, shards):
+def conv_input_grad(d, w, first, rows, shards):
     frames = PACK * (rows + HALF)
     return pl.pallas_call(
         functools.partial(conv_input_kernel, rows, shards),
         grid=(GROUPS // 2,),
         in_specs=[
             pl.BlockSpec((frames, 16, 128), lambda g: (0, 0, g)),
-            pl.BlockSpec((shards, 2 * GC, w.shape[2]), lambda g: (0, g, 0)),
+            pl.BlockSpec((shards, 2 * GC, w.shape[2]), lambda g: (0, first + g, 0)),
         ],
         out_specs=pl.BlockSpec((PACK * rows, 16, 128), lambda g: (0, 0, g)),
         out_shape=jax.ShapeDtypeStruct((PACK * rows, 16, PADW), jnp.float32),
@@ -166,7 +167,7 @@
             pltpu.VMEM((256, STEPS * 256), jnp.bfloat16),
             pltpu.VMEM((2, LANE, STEPS * 256), jnp.bfloat16),
         ],
-        cost_estimate=SMALL_COST,
+        cost_estimate=CONV_COST,
         compiler_params=pltpu.CompilerParams(vmem_limit_bytes=VMEM, dimension_semantics=("arbitrary",)),
         name="conv_input_grad",
     )(d, w)
@@ -214,29 +215,101 @@
             pltpu.VMEM((256, STEPS * 256), jnp.float32),
             pltpu.VMEM((shards * 2 * GC, per * LANE), jnp.bfloat16),
         ],
-        cost_estimate=SMALL_COST,
+        cost_estimate=CONV_COST,
         compiler_params=pltpu.CompilerParams(vmem_limit_bytes=VMEM, dimension_semantics=("arbitrary",)),
         name="conv_weight_grad",
     )(x, d)
 
 
-def line_up_kernel(*refs):
-    out_ref = refs[-1]
-    row = 0
-    for ref in refs[:-1]:
-        for j in range(ref.shape[1] // 256):
-            out_ref[row:row + 1, :] = ref[:, j * 256:j * 256 + 256]
-            row += 1
-
-
-def line_up(vectors):
+def turned_adam_kernel(rule, grad_ref, weight_ref, first_ref, second_ref, new_ref, new_first_ref, new_second_ref):
+    new, first, second = rule(weight_ref[...], grad_ref[...].T, first_ref[...], second_ref[...])
+    new_ref[...] = new
+    new_first_ref[...] = first
+    new_second_ref[...] = second
+
+
+def turned_adam(rule, weight, grad, first, second):
+    return tuple(
+        pl.pallas_call(
+            functools.partial(turned_adam_kernel, rule),
+            out_shape=[jax.ShapeDtypeStruct(weight.shape, jnp.float32)] * 3,
+            cost_estimate=SMALL_COST,
+            compiler_params=pltpu.CompilerParams(vmem_limit_bytes=VMEM),
+            name="turned_adam",
+        )(grad, weight, first, second)
+    )
+
+
+def put_pieces(out_ref, start, block, taps):
+    depth, width = block.shape[-2:]
+    for at in range(0, width, taps):
+        size = min(taps, width - at)
+        out_ref[..., start:start + depth, 0:size] = block[..., at:at + size]
+        start += depth
+    return start
+
+
+def pack_weights_kernel(conv_ref, *refs):
+    vector_ref, out_ref, held = refs[-3:]
+    taps = conv_ref.shape[0]
+    out_ref[0:D, :] = conv_ref[...].T.astype(jnp.bfloat16)
+    held[...] = jnp.zeros_like(held)
+    start = 0
+    for ref in refs[:-3]:
+        start = put_pieces(held, start, ref[...], taps)
+    size = vector_ref.shape[1]
+    for at in range(0, size, taps):
+        width = min(taps, size - at)
+        held[start:start + 1, 0:width] = vector_ref[:, at:at + width]
+        start += 1
+    out_ref[D:, :] = held[...].astype(jnp.bfloat16)
+
+
+def pack_weights(conv, blocks, vector, rows):
+    taps = conv.shape[0]
+    return pl.pallas_call(
+        pack_weights_kernel,
+        out_shape=jax.ShapeDtypeStruct((D + rows, taps), jnp.bfloat16),
+        scratch_shapes=[pltpu.VMEM((rows, taps), jnp.float32)],
+        cost_estimate=SMALL_COST,
+        compiler_params=pltpu.CompilerParams(vmem_limit_bytes=VMEM),
+        name="pack_weights",
+    )(conv, *blocks, vector.reshape(1, -1))
+
+
+def pack_grads_kernel(blocks, *refs):
+    extra_ref, out_ref, held, flat = refs[-4:]
+    shards, _, taps = out_ref.shape
+    held[...] = jnp.zeros_like(held)
+    start = 0
+    for ref in refs[:blocks]:
+        start = put_pieces(held, start, ref[...], taps)
+    place = 0
+    for ref in refs[blocks:-4]:
+        flat[:, place:place + ref.shape[1]] = ref[...]
+        place += ref.shape[1]
+    size = place // shards
+    for s in range(shards):
+        for row, at in enumerate(range(0, size, taps)):
+            width = min(taps, size - at)
+            held[s, start + row:start + row + 1, 0:width] = flat[:, s * size + at:s * size + at + width]
+    start += -(-size // taps)
+    held[:, start:start + 1, 0:128] = jnp.broadcast_to(extra_ref[...][None], (shards, 1, 128))
+    out_ref[...] = held[...].astype(jnp.bfloat16)
+
+
+def pack_grads(blocks, vectors, extra, shards, rows, taps):
+    blocks = [block.reshape(shards, -1, block.shape[-1]) for block in blocks]
     vectors = [v.reshape(1, -1) for v in vectors]
     total = sum(v.shape[1] for v in vectors)
     return pl.pallas_call(
-        line_up_kernel,
-        out_shape=jax.ShapeDtypeStruct((total // 256, 256), jnp.float32),
-        name="line_up",
-    )(*vectors)
+        functools.partial(pack_grads_kernel, len(blocks)),
+        out_shape=jax.ShapeDtypeStruct((shards, rows, taps), jnp.bfloat16),
+        scratch_shapes=[pltpu.VMEM((shards, rows, taps), jnp.float32), pltpu.VMEM((1, total), jnp.float32)],
+        cost_estimate=SMALL_COST,
+        compiler_params=pltpu.CompilerParams(vmem_limit_bytes=VMEM),
+        name="pack_grads",
+    )(*blocks, *vectors, extra)
 
 
 def to_strips(padded, frame_count):
@@ -291,9 +364,19 @@
     stat_ref[0, 0, 1:2, :] = rows[HDIM:HDIM + 1, :]
 
 
+def head_spec(item, frames):
+    if isinstance(item, tuple):
+        return pl.BlockSpec((None, frames, 128), lambda c, h: (item[1], c, h))
+    return pl.BlockSpec((frames, 128), lambda c, h: (c, h))
+
+
+def head_array(item):
+    return item[0] if isinstance(item, tuple) else item
+
+
 def attend(query, keys, values, clips):
     blocks = len(keys)
-    rows = query.shape[0]
+    rows = head_array(query).shape[-2]
     frames = rows // clips
     spec = pl.BlockSpec((frames, 128), lambda c, h: (c, h))
     operands = [query]
@@ -302,7 +385,7 @@
     return pl.pallas_call(
         functools.partial(attend_kernel, blocks),
         grid=(clips, HEADS // 2),
-        in_specs=[spec] * len(operands),
+        in_specs=[head_spec(item, frames) for item in operands],
         out_specs=[spec, pl.BlockSpec((1, 1, 2, frames), lambda c, h: (c, h, 0, 0))],
         out_shape=[
             jax.ShapeDtypeStruct((rows, D), jnp.bfloat16),
@@ -311,7 +394,7 @@
         cost_estimate=SMALL_COST,
         compiler_params=pltpu.CompilerParams(vmem_limit_bytes=VMEM, dimension_semantics=("arbitrary", "arbitrary")),
         name="attend",
-    )(*operands)
+    )(*[head_array(item) for item in operands])
 
 
 def attend_back_kernel(blocks, q_ref, d_ref, stat_ref, *refs):
@@ -364,7 +447,7 @@
 
 def attend_back(query, grad, stat, keys, values, clips):
     blocks = len(keys)
-    rows = query.shape[0]
+    rows = grad.shape[0]
     frames = rows // clips
     spec = pl.BlockSpec((frames, 128), lambda c, h: (c, h))
     operands = []
@@ -374,13 +457,14 @@
     return pl.pallas_call(
         functools.partial(attend_back_kernel, blocks),
         grid=(clips, HEADS // 2),
-        in_specs=[spec, spec, pl.BlockSpec((1, 1, 2, frames), lambda c, h: (c, h, 0, 0))] + [spec] * len(operands),
+        in_specs=[head_spec(query, frames), spec, pl.BlockSpec((1, 1, 2, frames), lambda c, h: (c, h, 0, 0))]
+        + [head_spec(item, frames) for item in operands],
         out_specs=[spec] * (1 + 2 * blocks),
         out_shape=[shape] * (1 + 2 * blocks),
         cost_estimate=SMALL_COST,
         compiler_params=pltpu.CompilerParams(vmem_limit_bytes=VMEM, dimension_semantics=("arbitrary", "arbitrary")),
         name="attend_back",
-    )(query, grad, stat, *operands)
+    )(head_array(query), grad, stat, *[head_array(item) for item in operands])
 
 
 def count_kernel(draws, n_ref, out_ref):
@@ -409,20 +493,356 @@
     )(negatives)
 
 
+def square(ref):
+    return ref[...].reshape(D, D)
+
+
+def project_kernel(x_ref, w_ref, b_ref, out_ref):
+    out_ref[0] = (mm(x_ref[...], square(w_ref)) + b_ref[0]).astype(jnp.bfloat16)
+
+
+def project(entry, whole, first, biases):
+    count = len(biases)
+    rows = entry.shape[0]
+    shards, _, _ = whole.shape
+    depth = D // shards
+    return pl.pallas_call(
+        project_kernel,
+        grid=(count,),
+        in_specs=[
+            pl.BlockSpec((rows, D), lambda i: (0, 0)),
+            pl.BlockSpec((shards, depth, D), lambda i: (0, first + i, 0)),
+            pl.BlockSpec((1, 1, D), lambda i: (i, 0, 0)),
+        ],
+        out_specs=pl.BlockSpec((1, rows, D), lambda i: (i, 0, 0)),
+        out_shape=jax.ShapeDtypeStruct((count, rows, D), jnp.bfloat16),
+        cost_estimate=SMALL_COST,
+        compiler_params=pltpu.CompilerParams(vmem_limit_bytes=VMEM, dimension_semantics=("arbitrary",)),
+        name="project",
+    )(entry, whole, jnp.stack(biases).reshape(count, 1, D))
+
+
+def norm_rows(values, gain_row, bias_row):
+    centred = values - jnp.mean(values, -1, keepdims=True)
+    scale = lax.rsqrt(jnp.mean(centred * centred, -1, keepdims=True) + norm_epsilon)
+    level = centred * scale
+    return level * gain_row + bias_row, level, scale
+
+
+def norm_rows_back(grad, level, scale, gain_row):
+    inside = grad * gain_row
+    centred = inside - jnp.mean(inside, -1, keepdims=True) - level * jnp.mean(inside * level, -1, keepdims=True)
+    return scale * centred
+
+
+def gelu_parts(values):
+    half = 0.5 * (1.0 + lax.erf(values * 0.5**0.5))
+    density = jnp.exp(-0.5 * values * values) * (2.0 * jnp.pi) ** -0.5
+    return values * half, half + values * density
+
+
+def feed_kernel(
+    hidden_ref, mixed_ref, wo_ref, e_ref, s_ref, ob_ref, g1_ref, b1_ref, eb_ref, sb_ref, g2_ref, b2_ref,
+    low_ref, level1_ref, scale1_ref, active_ref, slope_ref, result_ref, result_low_ref, level2_ref, scale2_ref,
+    middle_ref, total_ref,
+):
+    step = pl.program_id(0)
+
+    @pl.when(step == 0)
+    def _():
+        branch = mm(mixed_ref[...], square(wo_ref)) + ob_ref[...]
+        middle, level, scale = norm_rows(hidden_ref[...] + branch, g1_ref[...], b1_ref[...])
+        middle_ref[...] = middle
+        low_ref[...] = middle.astype(jnp.bfloat16)
+        level1_ref[...] = level
+        scale1_ref[...] = scale
+        total_ref[...] = jnp.zeros_like(total_ref)
+
+    inner = mm(low_ref[...], square(e_ref)) + eb_ref[...]
+    active, slope = gelu_parts(inner)
+    active = active.astype(jnp.bfloat16)
+    active_ref[...] = active
+    slope_ref[...] = slope.astype(jnp.bfloat16)
+    total_ref[...] += mm(active, square(s_ref))
+
+    @pl.when(step == pl.num_programs(0) - 1)
+    def _():
+        result, level, scale = norm_rows(middle_ref[...] + (total_ref[...] + sb_ref[...]), g2_ref[...], b2_ref[...])
+        result_ref[...] = result
+        result_low_ref[...] = result.astype(jnp.bfloat16)
+        level2_ref[...] = level
+        scale2_ref[...] = scale
+
+
+def feed_forward(hidden, mixed, attn_whole, feed_whole, first, place, vectors):
+    rows = hidden.shape[0]
+    shards = attn_whole.shape[0]
+    depth = D // shards
+    parts = FF // D
+    row = pl.BlockSpec((1, D), lambda j: (0, 0))
+    flat = pl.BlockSpec((rows, D), lambda j: (0, 0))
+    column = pl.BlockSpec((rows, 1), lambda j: (0, 0))
+    tile = pl.BlockSpec((rows, D), lambda j: (0, j))
+    o_bias, gain_one, bias_one, expand_bias, shrink_bias, gain_two, bias_two = [v.reshape(1, -1) for v in vectors]
+
+    def shape(width, dtype):
+        return jax.ShapeDtypeStruct((rows, width), dtype)
+
+    return pl.pallas_call(
+        feed_kernel,
+        grid=(parts,),
+        in_specs=[
+            flat,
+            flat,
+            pl.BlockSpec((shards, depth, D), lambda j: (0, place + 3, 0)),
+            pl.BlockSpec((shards, depth, D), lambda j: (0, first + j, 0)),
+            pl.BlockSpec((shards // parts, parts * depth, D), lambda j: (j, first // parts + 1, 0)),
+            row, row, row,
+            pl.BlockSpec((1, D), lambda j: (0, j)),
+            row, row, row,
+        ],
+        out_specs=[flat, flat, column, tile, tile, flat, flat, flat, column],
+        out_shape=[
+            shape(D, jnp.bfloat16), shape(D, jnp.float32), shape(1, jnp.float32),
+            shape(FF, jnp.bfloat16), shape(FF, jnp.bfloat16),
+            shape(D, jnp.float32), shape(D, jnp.bfloat16), shape(D, jnp.float32), shape(1, jnp.float32),
+        ],
+        scratch_shapes=[pltpu.VMEM((rows, D), jnp.float32)] * 2,
+        cost_estimate=SMALL_COST,
+        compiler_params=pltpu.CompilerParams(vmem_limit_bytes=VMEM, dimension_semantics=("arbitrary",)),
+        name="feed_forward",
+    )(hidden, mixed, attn_whole, feed_whole, feed_whole, o_bias, gain_one, bias_one, expand_bias, shrink_bias, gain_two, bias_two)
+
+
+def row_sum(values):
+    return jnp.sum(values, 0, keepdims=True)
+
+
+def feed_back_kernel(arrivals, base, *refs):
+    if base:
+        refs = refs[1:]
+    grad_ref = refs[0]
+    extra = refs[1 : 1 + arrivals]
+    (
+        level2_ref, scale2_ref, g2_ref, slope_ref, active_ref, low_ref, e_ref, s_ref, level1_ref, scale1_ref, g1_ref, wo_ref,
+        sum_ref, branch_ref, mixed_ref, vec_ref, eb_ref, chunk_ref,
+        outer_ref, turned_ref, total_ref, e_slot, s_slot, e_sem, s_sem,
+    ) = refs[1 + arrivals :]
+    step = pl.program_id(0)
+    last = pl.num_programs(0) - 1
+    slot = lax.rem(step, 2)
+    shards, depth = e_slot.shape[1:3]
+    group = s_slot.shape[1]
+
+    @pl.when(step == 0)
+    def _():
+        grad = grad_ref[...]
+        for ref in extra:
+            grad = grad + ref[...].astype(jnp.float32)
+        level = level2_ref[...]
+        total = norm_rows_back(grad, level, scale2_ref[...], g2_ref[...])
+        outer = total.astype(jnp.bfloat16)
+        outer_ref[...] = outer
+        total_ref[...] = total
+        vec_ref[3:4, :] = row_sum(outer.astype(jnp.float32))
+        vec_ref[4:5, :] = row_sum(grad * level)
+        vec_ref[5:6, :] = row_sum(grad)
+        turned_ref[...] = turned(low_ref[...])
+
+    def copies(at, index):
+        e_copy = pltpu.make_async_copy(
+            e_slot.at[at], chunk_ref.at[:, pl.ds(base + index * depth, depth), :], e_sem.at[at]
+        )
+        s_copy = pltpu.make_async_copy(
+            s_slot.at[at],
+            chunk_ref.at[pl.ds(index * group, group), pl.ds(base + (last + 1) * depth, (last + 1) * depth), :],
+            s_sem.at[at],
+        )
+        return e_copy, s_copy
+
+    @pl.when(step >= 2)
+    def _():
+        for copy in copies(slot, step - 2):
+            copy.wait()
+
+    outer = outer_ref[...]
+    inner = (mm(outer, square(s_ref), NT) * slope_ref[...].astype(jnp.float32)).astype(jnp.bfloat16)
+    eb_ref[...] = row_sum(inner.astype(jnp.float32))
+    total_ref[...] += mm(inner, square(e_ref), NT)
+    e_slot[slot] = mm(turned_ref[...], inner).astype(jnp.bfloat16).reshape(shards, depth, D)
+    s_slot[slot] = mm(turned(active_ref[...]), outer).astype(jnp.bfloat16).reshape(group, (last + 1) * depth, D)
+    for copy in copies(slot, step):
+        copy.start()
+
+    @pl.when(step == last)
+    def _():
+        grad = total_ref[...]
+        level = level1_ref[...]
+        total = norm_rows_back(grad, level, scale1_ref[...], g1_ref[...])
+        branch = total.astype(jnp.bfloat16)
+        sum_ref[...] = total
+        branch_ref[...] = branch
+        vec_ref[0:1, :] = row_sum(branch.astype(jnp.float32))
+        vec_ref[1:2, :] = row_sum(grad * level)
+        vec_ref[2:3, :] = row_sum(grad)
+        vec_ref[6:8, :] = jnp.zeros((2, D), jnp.float32)
+        mixed_ref[...] = mm(branch, square(wo_ref), NT).astype(jnp.bfloat16)
+        for index in (last - 1, last):
+            for copy in copies(lax.rem(index, 2), index):
+                copy.wait()
+
+
+def feed_back(grads, cache, attn_whole, feed_whole, first, place, gain_one, gain_two, chunks):
+    level1, scale1, low, slope, active, level2, scale2 = cache
+    rows = low.shape[0]
+    shards = attn_whole.shape[0]
+    depth = D // shards
+    parts = FF // D
+    flat = pl.BlockSpec((rows, D), lambda j: (0, 0))
+    row = pl.BlockSpec((1, D), lambda j: (0, 0))
+    column = pl.BlockSpec((rows, 1), lambda j: (0, 0))
+    tile = pl.BlockSpec((rows, D), lambda j: (0, j))
+    return pl.pallas_call(
+        functools.partial(feed_back_kernel, len(grads) - 1, 0 if chunks is None else 4 * depth),
+        grid=(parts,),
+        in_specs=[pl.BlockSpec(memory_space=pl.ANY)] * (chunks is not None)
+        + [flat] * len(grads)
+        + [
+            flat, column, row, tile, tile, flat,
+            pl.BlockSpec((shards, depth, D), lambda j: (0, first + j, 0)),
+            pl.BlockSpec((shards // parts, parts * depth, D), lambda j: (j, first // parts + 1, 0)),
+            flat, column, row,
+            pl.BlockSpec((shards, depth, D), lambda j: (0, place + 3, 0)),
+        ],
+        out_specs=[
+            flat, flat, flat,
+            pl.BlockSpec((8, D), lambda j: (0, 0)),
+            pl.BlockSpec((1, D), lambda j: (0, j)),
+            pl.BlockSpec(memory_space=pl.ANY),
+        ],
+        out_shape=[
+            jax.ShapeDtypeStruct((rows, D), jnp.float32),
+            jax.ShapeDtypeStruct((rows, D), jnp.bfloat16),
+            jax.ShapeDtypeStruct((rows, D), jnp.bfloat16),
+            jax.ShapeDtypeStruct((8, D), jnp.float32),
+            jax.ShapeDtypeStruct((1, FF), jnp.float32),
+            jax.ShapeDtypeStruct((shards, (4 * (chunks is not None) + 2 * parts) * depth, D), jnp.bfloat16),
+        ],
+        input_output_aliases={} if chunks is None else {0: 5},
+        scratch_shapes=[
+            pltpu.VMEM((rows, D), jnp.bfloat16),
+            pltpu.VMEM((D, rows), jnp.bfloat16),
+            pltpu.VMEM((rows, D), jnp.float32),
+            pltpu.VMEM((2, shards, depth, D), jnp.bfloat16),
+            pltpu.VMEM((2, shards // parts, parts * depth, D), jnp.bfloat16),
+            pltpu.SemaphoreType.DMA((2,)),
+            pltpu.SemaphoreType.DMA((2,)),
+        ],
+        cost_estimate=SMALL_COST,
+        compiler_params=pltpu.CompilerParams(vmem_limit_bytes=VMEM, dimension_semantics=("arbitrary",)),
+        name="feed_back",
+    )(
+        *([] if chunks is None else [chunks]), *grads, level2, scale2, gain_two.reshape(1, D), slope, active, low, feed_whole, feed_whole,
+        level1, scale1, gain_one.reshape(1, D), attn_whole,
+    )
+
+
+def entry_back_kernel(blocks, sum_ref, dq_ref, *refs):
+    keys, values = refs[0 : 2 * blocks : 2], refs[1 : 2 * blocks : 2]
+    wq_ref, wk_ref, wv_ref = refs[2 * blocks : 2 * blocks + 3]
+    outs = refs[2 * blocks + 3 :]
+    key_w, value_w = square(wk_ref), square(wv_ref)
+    for j in range(blocks):
+        back = mm(keys[j][...], key_w, NT) + mm(values[j][...], value_w, NT)
+        if j == 0:
+            outs[0][...] = sum_ref[...] + mm(dq_ref[...], square(wq_ref), NT) + back
+        else:
+            outs[j][...] = back.astype(jnp.bfloat16)
+
+
+def entry_back(grad_sum, dq, pairs, attn_whole, place):
+    rows = dq.shape[0]
+    shards = attn_whole.shape[0]
+    flat = pl.BlockSpec((rows, D), lambda i: (0, 0))
+    weights = [pl.BlockSpec((shards, D // shards, D), lambda i, m=m: (0, place + m, 0)) for m in range(3)]
+    return pl.pallas_call(
+        functools.partial(entry_back_kernel, len(pairs) // 2),
+        grid=(1,),
+        in_specs=[flat] * (2 + len(pairs)) + weights,
+        out_specs=[flat] * (len(pairs) // 2),
+        out_shape=[
+            jax.ShapeDtypeStruct((rows, D), jnp.float32 if j == 0 else jnp.bfloat16) for j in range(len(pairs) // 2)
+        ],
+        cost_estimate=SMALL_COST,
+        compiler_params=pltpu.CompilerParams(vmem_limit_bytes=VMEM, dimension_semantics=("arbitrary",)),
+        name="entry_back",
+    )(grad_sum, dq, *pairs, attn_whole, attn_whole, attn_whole)
+
+
+def attn_grads_kernel(blocks, *refs):
+    entries = refs[:blocks]
+    dq_ref, mixed_ref, branch_ref = refs[blocks : blocks + 3]
+    pairs = refs[blocks + 3 : 3 * blocks + 3]
+    out_ref, vec_ref, slots, sem = refs[3 * blocks + 3 :]
+    shards, depth = slots.shape[1:3]
+    entry_turned = [turned(e[...]) for e in entries]
+
+    def put(i, value):
+        slots[i] = value.astype(jnp.bfloat16).reshape(shards, depth, D)
+        pltpu.make_async_copy(slots.at[i], out_ref.at[:, pl.ds(i * depth, depth), :], sem.at[i]).start()
+
+    put(0, mm(entry_turned[0], dq_ref[...]))
+    put(1, functools.reduce(jnp.add, [mm(e, k[...]) for e, k in zip(entry_turned, pairs[0::2])]))
+    put(2, functools.reduce(jnp.add, [mm(e, v[...]) for e, v in zip(entry_turned, pairs[1::2])]))
+    put(3, mm(turned(mixed_ref[...]), branch_ref[...]))
+    vec_ref[0:1, :] = row_sum(dq_ref[...].astype(jnp.float32))
+    vec_ref[1:2, :] = functools.reduce(jnp.add, [row_sum(v[...].astype(jnp.float32)) for v in pairs[1::2]])
+    vec_ref[2:8, :] = jnp.zeros((6, D), jnp.float32)
+    for i in range(4):
+        pltpu.make_async_copy(slots.at[i], out_ref.at[:, pl.ds(i * depth, depth), :], sem.at[i]).wait()
+
+
+def attn_grads(entries, dq, mixed, branch, pairs, shards, room):
+    blocks = len(entries)
+    rows = dq.shape[0]
+    flat = pl.BlockSpec((rows, D), lambda i: (0, 0))
+    operands = list(entries) + [dq, mixed, branch] + list(pairs)
+    return pl.pallas_call(
+        functools.partial(attn_grads_kernel, blocks),
+        grid=(1,),
+        in_specs=[flat] * len(operands),
+        out_specs=[pl.BlockSpec(memory_space=pl.ANY), pl.BlockSpec((8, D), lambda i: (0, 0))],
+        out_shape=[
+            jax.ShapeDtypeStruct((shards, room, D), jnp.bfloat16),
+            jax.ShapeDtypeStruct((8, D), jnp.float32),
+        ],
+        scratch_shapes=[
+            pltpu.VMEM((4, shards, D // shards, D), jnp.bfloat16),
+            pltpu.SemaphoreType.DMA((4,)),
+        ],
+        cost_estimate=SMALL_COST,
+        compiler_params=pltpu.CompilerParams(vmem_limit_bytes=VMEM, dimension_semantics=("arbitrary",)),
+        name="attn_grads",
+    )(*operands)
+
+
 MESH = pl.DeviceIdType.MESH
 AHEAD = 3
 OTHER = 2
 
 
-def reduce_kernel(count, seqs, sizes, *refs):
+def reduce_kernel(count, seqs, sizes, trades, *refs):
     number = len(sizes)
+    if trades:
+        give_ref, take_ref = refs[number], refs[2 * number + 1]
+        refs = refs[:number] + refs[number + 1 : 2 * number + 1] + refs[2 * number + 2 :]
     sources = refs[:number]
     outs = refs[number : 2 * number]
     bits = count.bit_length() - 1
     turns = seqs.bit_length() - 1
     levels = bits + turns
     held = refs[2 * number : 2 * number + levels]
-    send_sem, recv_sem = refs[2 * number + levels :]
+    send_sem, recv_sem, give_sem, take_sem = refs[2 * number + levels :]
     me = lax.axis_index("shard")
     place = lax.axis_index("seq")
 
@@ -430,10 +850,12 @@
         return index + (1 - 2 * ((index // 2**bit) % 2)) * 2**bit
 
     partners = [{"shard": across(me, b)} for b in range(bits)] + [{"seq": across(place, t)} for t in range(turns)]
+    others = [{"shard": lax.rem(me + k, count)} for k in range(1, count)]
+    greeted = others + partners[bits:] if trades else partners
     barrier = pltpu.get_barrier_semaphore()
-    for partner in partners:
+    for partner in greeted:
         pl.semaphore_signal(barrier, inc=1, device_id=partner, device_id_type=MESH)
-    pl.semaphore_wait(barrier, len(partners))
+    pl.semaphore_wait(barrier, len(greeted))
 
     pieces = []
     offset = 0
@@ -496,6 +918,24 @@
             else:
                 held[level][j, pl.ds(spot, cut)] = mine + other
 
+    swaps = []
+    if trades:
+        for k in range(1, count):
+            target = lax.rem(me + k, count)
+            swaps.append(
+                pltpu.make_async_remote_copy(
+                    src_ref=give_ref.at[target],
+                    dst_ref=take_ref.at[me],
+                    send_sem=give_sem.at[k],
+                    recv_sem=take_sem.at[k],
+                    device_id={"shard": target},
+                    device_id_type=MESH,
+                )
+            )
+        own = pltpu.make_async_copy(give_ref.at[me], take_ref.at[me], give_sem.at[0])
+        own.start()
+        for swap in swaps:
+            swap.start()
     delay = [0, 1] + [1 + AHEAD * level for level in range(1, levels)]
     for wave in range(len(pieces) + delay[-1]):
         for level in range(levels, -1, -1):
@@ -505,9 +945,13 @@
                     absorb(piece, level - 1)
                 if level < levels:
                     launch(piece, level)
-
-
-def reduce_chunks(call, mesh_sizes, cuts, *chunks):
+    if trades:
+        own.wait()
+        for swap in swaps:
+            swap.wait()
+
+
+def reduce_chunks(mesh_sizes, cuts, chunks, give):
     count, seqs = mesh_sizes
     bits, turns = count.bit_length() - 1, seqs.bit_length() - 1
     lanes = chunks[0].shape[2]
@@ -515,17 +959,20 @@
     total = sum(rows for rows, _ in sizes)
     number = sum(rows // cut for rows, cut in sizes)
     slots = [2 ** (bits - 1 - level) for level in range(bits)] + [1] * turns
+    spec = pl.BlockSpec(memory_space=pltpu.VMEM)
     return pl.pallas_call(
-        functools.partial(reduce_kernel, count, seqs, sizes),
-        in_specs=[pl.BlockSpec(memory_space=pltpu.VMEM)] * len(chunks),
-        out_specs=[pl.BlockSpec(memory_space=pltpu.VMEM)] * len(chunks),
-        out_shape=[jax.ShapeDtypeStruct(c.shape[1:], jnp.float32) for c in chunks],
+        functools.partial(reduce_kernel, count, seqs, sizes, True),
+        in_specs=[spec] * (len(chunks) + 1),
+        out_specs=[spec] * (len(chunks) + 1),
+        out_shape=[jax.ShapeDtypeStruct(c.shape[1:], jnp.float32) for c in chunks]
+        + [jax.ShapeDtypeStruct(give.shape, give.dtype)],
         scratch_shapes=[pltpu.VMEM((n, total, lanes), jnp.bfloat16) for n in slots]
-        + [pltpu.SemaphoreType.DMA((number, bits + turns, count // 2))] * 2,
+        + [pltpu.SemaphoreType.DMA((number, bits + turns, count // 2))] * 2
+        + [pltpu.SemaphoreType.DMA((count,))] * 2,
         cost_estimate=SMALL_COST,
-        compiler_params=pltpu.CompilerParams(collective_id=call, has_side_effects=True, vmem_limit_bytes=VMEM),
+        compiler_params=pltpu.CompilerParams(collective_id=0, has_side_effects=True, vmem_limit_bytes=VMEM),
         name="reduce_chunks",
-    )(*chunks)
+    )(*chunks, give)
 
 
 def swap_moves(count, step):
@@ -571,12 +1018,6 @@
 
 def column_sum(values):
     return jnp.sum(values.astype(jnp.float32), 0, keepdims=True)
-
-
-def gelu_parts(values):
-    half = 0.5 * (1.0 + lax.erf(values * 0.5**0.5))
-    density = jnp.exp(-0.5 * values * values) * (2.0 * jnp.pi) ** -0.5
-    return values * half, half + values * density
 
 
 def norm_forward(values, gain_row, bias_row):
@@ -622,15 +1063,16 @@
     return jnp.concatenate([low, block, high], axis=1)
 
 
-def layer_forward(hidden, attn_w, expand_w, shrink_w, pieces, clip_count, *waiting):
+def layer_forward(hidden, hidden_low, weights, pieces, clip_count, waiting):
+    attn_w, expand_w, shrink_w = weights
     q_bias, v_bias, o_bias, gain_one, bias_one, expand_bias, shrink_bias, gain_two, bias_two = pieces
-    entries = gather_ring(lowered(hidden))
+    entries = gather_ring(hidden_low)
     query = lowered(bdot(entries[0], attn_w[:, :D]) + q_bias)
     keys = [lowered(bdot(entry, attn_w[:, D : 2 * D])) for entry in entries]
     values = [lowered(bdot(entry, attn_w[:, 2 * D : 3 * D]) + v_bias) for entry in entries]
     mixed, stat = attend(query, keys, values, clip_count)
-    if waiting:
-        mixed, *waiting = fence(mixed, *waiting)
+    if waiting is not None:
+        mixed, waiting = fence(mixed, waiting)
     branch = bdot(mixed, attn_w[:, 3 * D :]) + o_bias
     middle, middle_kept = norm_forward(hidden + branch, gain_one, bias_one)
     middle_low = lowered(middle)
@@ -641,7 +1083,7 @@
     outer = bdot(active_low, shrink_w) + shrink_bias
     result, final_kept = norm_forward(middle + outer, gain_two, bias_two)
     cache = (entries, query, keys, values, mixed, stat, middle_kept, middle_low, slope_low, active_low, final_kept)
-    return (result, cache) + tuple(waiting or [None])
+    return result, lowered(result), cache, waiting
 
 
 def feed_backward(grad_out, cache, expand_w, shrink_w):
@@ -688,6 +1130,67 @@
     return grad_hidden, grads, vectors, waiting
 
 
+def fused_forward(hidden, hidden_low, weights, pieces, clip_count, waiting):
+    attn_whole, feed_whole, first = weights
+    place = 0
+    none = jnp.zeros_like(pieces[0])
+    entries = [hidden_low]
+    packs = [project(hidden_low, attn_whole, place, [pieces[0], none, pieces[1]])]
+    for entry in gather_ring(hidden_low)[1:]:
+        entries.append(entry)
+        packs.append(project(entry, attn_whole, place + 1, [none, pieces[1]]))
+    query = (packs[0], 0)
+    keys = [(pack, 1 if j == 0 else 0) for j, pack in enumerate(packs)]
+    values = [(pack, 2 if j == 0 else 1) for j, pack in enumerate(packs)]
+    mixed, stat = attend(query, keys, values, clip_count)
+    if waiting is not None:
+        mixed, waiting = fence(mixed, waiting)
+    low, level1, scale1, active, slope, result, result_low, level2, scale2 = feed_forward(
+        hidden, mixed, attn_whole, feed_whole, first, place, pieces[2:]
+    )
+    cache = (entries, query, keys, values, mixed, stat, (level1, scale1, low, slope, active, level2, scale2))
+    return result, result_low, cache, waiting
+
+
+def fused_backward(grads, cache, weights, pieces, clip_count, chunks, room, waiting):
+    attn_whole, feed_whole, first = weights
+    entries, query, keys, values, mixed, stat, kept = cache
+    shards = lax.axis_size("shard")
+    grad_sum, branch, grad_mixed, sums, grad_expand_bias, feed_chunks = feed_back(
+        grads, kept, attn_whole, feed_whole, first, 0, pieces[3], pieces[7], chunks
+    )
+    if waiting is not None:
+        grad_mixed, held = fence(grad_mixed, waiting[1])
+        waiting = waiting[0](held)
+    results = attend_back(query, grad_mixed, stat, keys, values, clip_count)
+    if waiting is not None:
+        results, waiting = fence(results, waiting)
+    backs = entry_back(grad_sum, results[0], results[1:], attn_whole, 0)
+    results, backs, branch = fence(results, backs, branch)
+    arrived = return_ring(backs)
+    attn_chunks, more = attn_grads(entries, results[0], mixed, branch, results[1:], shards, room)
+    arrived, more = fence(arrived, more)
+    vectors = [more[0:1], more[1:2], sums[0:1], sums[1:2], sums[2:3], grad_expand_bias, sums[3:4], sums[4:5], sums[5:6]]
+    return [backs[0]] + arrived, feed_chunks, attn_chunks, vectors, waiting
+
+
+def plain_backward(grads, cache, weights, pieces, clip_count, chunks, room, waiting):
+    attn_w, expand_w, shrink_w = weights
+    shards = lax.axis_size("shard")
+    grad = grads[0]
+    for part in grads[1:]:
+        grad = grad + part.astype(jnp.float32)
+    grad_middle, grad_expand, grad_shrink, feed_vectors = feed_backward(grad, cache, expand_w, shrink_w)
+    rest = [] if waiting is None else [waiting[0](waiting[1])]
+    grad_hidden, attn_list, attn_vectors, rest = attend_backward(grad_middle, cache, attn_w, clip_count, *rest)
+    blocks = [] if chunks is None else [chunks]
+    blocks += [grad_expand[:, j * D : (j + 1) * D].reshape(shards, -1, D) for j in range(FF // D)]
+    blocks.append(grad_shrink.reshape(shards, -1, D))
+    attn_chunks = jnp.concatenate([item.reshape(shards, -1, D) for item in attn_list], 1)
+    vectors = attn_vectors + feed_vectors
+    return [grad_hidden], jnp.concatenate(blocks, 1), attn_chunks, vectors, rest[0] if rest else None
+
+
 def adam_update(weight, grad, first, second, rate, decay):
     first = beta_one * first + (1 - beta_one) * grad
     second = beta_two * second + (1 - beta_two) * grad * grad
@@ -695,6 +1198,10 @@
         first / (1 - beta_one**STEP) / (jnp.sqrt(second / (1 - beta_two**STEP)) + adam_epsilon)
     )
     return (weight - rate * (share_fraction + decay * weight), first, second)
+
+
+def matrix_rule(weight, grad, first, second):
+    return adam_update(weight, grad, first, second, rate_matrix, decay_rate)
 
 
 def gather_rows(block):
@@ -769,27 +1276,24 @@
     seq_count = lax.axis_size("seq")
     shards = lax.axis_size("shard")
     clip_frames = frame_count * seq_count
-    small_items = [feature_weight, final_weight, target_weight, codebook_weight, vector_params]
-    small_sizes = [item.size for item in small_items]
-    small_total = sum(small_sizes)
-    small_width = -(-(small_total + 2) // SMALL_LANES) * SMALL_LANES
-
-    def split_small(flat):
-        parts = []
-        offset = 0
-        for item, size in zip(small_items, small_sizes):
-            parts.append(flat[:, offset : offset + size].reshape((-1,) + item.shape[1:]))
-            offset = offset + size
-        return parts
-
-    small = jnp.concatenate([lowered(item).reshape(-1) for item in small_items])
-    small = jnp.pad(small, (0, small_width - small_total))
     taps = conv_weight.shape[0]
-    (own_first,) = fence(jnp.concatenate([lowered(conv_weight).T, small.reshape(-1, taps)]))
-    first_all = gather_rows(own_first)
-    conv_w = first_all
-    feat_w, final_w, target_w, code_w, vector_low = split_small(first_all[:, D:].reshape(shards, -1))
-    attn_w, expand_w, shrink_w = [], [], []
+    small_items = [feature_weight, final_weight, target_weight, codebook_weight]
+
+    def split_small(packed):
+        blocks = []
+        start = 0
+        for item in small_items:
+            depth, width = item.shape
+            count = -(-width // taps)
+            pieces = [packed[..., start + j * depth : start + (j + 1) * depth, :] for j in range(count)]
+            blocks.append(jnp.concatenate(pieces, -1)[..., :width])
+            start += count * depth
+        size = vector_params.shape[0]
+        count = -(-size // taps)
+        vector = packed[..., start : start + count, :].reshape(packed.shape[:-2] + (-1,))[..., :size]
+        return blocks, vector, packed[..., start + count, :2]
+
+    parts = shards // (4 * LAYERS)
     rows = D // shards
 
     def own_attn(layer):
@@ -801,24 +1305,43 @@
             [expand_own[:, j * D : (j + 1) * D] for j in range(FF // D)] + [lowered(shrink_weight[layer])]
         )
 
-    def use_attn(whole):
-        attn_w.append(jnp.concatenate([whole[:, j * rows : (j + 1) * rows].reshape(D, D) for j in range(4)], 1))
-
-    def use_feed(whole):
-        blocks = [whole[:, j * rows : (j + 1) * rows].reshape(D, D) for j in range(FF // D)]
-        expand_w.append(jnp.concatenate(blocks, 1))
-        shrink_w.append(whole[:, FF // D * rows :].reshape(FF, D))
+    first_all = gather_rows(pack_weights(conv_weight, small_items, vector_params, SMALL_ROWS))
+    conv_w = first_all
+    blocks, vector_low, _ = split_small(first_all[:, D:])
+    feat_w, final_w, target_w, code_w = [block.reshape(-1, block.shape[-1]) for block in blocks]
+
+    def spread_halves(block):
+        number = block.shape[1]
+        columns = D // parts
+        cut = block.reshape(4 * LAYERS, number, rows, parts, columns).transpose(0, 3, 1, 2, 4)
+        return trade(cut.reshape(shards, number, rows, columns))
+
+    def join_halves(got):
+        number = got.shape[1]
+        got = got.transpose(1, 0, 2, 3).reshape(number, D, D // parts)
+        if parts != 2:
+            groups = [[i * parts + j for j in range(parts)] for i in range(shards // parts)]
+            return lax.all_gather(got, "shard", axis=2, tiled=True, axis_index_groups=groups)
+        other = lax.ppermute(got, "shard", [(i, i ^ 1) for i in range(shards)])
+        second = lax.axis_index("shard") % 2 == 1
+        return jnp.concatenate([jnp.where(second, other, got), jnp.where(second, got, other)], 2)
+
+    def plain_weights(attn_whole, feed_whole):
+        blocks = [attn_whole[:, j * rows : (j + 1) * rows].reshape(D, D) for j in range(4)]
+        columns = [feed_whole[:, j * rows : (j + 1) * rows].reshape(D, D) for j in range(FF // D)]
+        shrink = feed_whole[:, FF // D * rows :].reshape(FF, D)
+        return jnp.concatenate(blocks, 1), jnp.concatenate(columns, 1), shrink
 
     first_frame = lax.axis_index("seq") * frame_count
     ring_draws = (negatives - first_frame + clip_frames) % clip_frames
     counts = count_draws(ring_draws.transpose(0, 2, 1), clip_frames)
+    held = jnp.stack([lowered(left_basis_t), lowered(attention_first), lowered(attention_second)], 1)
     counts, own_0 = fence(counts, jnp.concatenate([own_attn(0), own_feed(0)]))
-    whole = gather_rows(own_0)
-    use_attn(whole[:, : 4 * rows])
-    use_feed(whole[:, 4 * rows :])
-    parts = shards // (4 * LAYERS)
-
-    pieces = vector_pieces(vector_low.astype(jnp.float32))
+    whole_0 = gather_rows(own_0)
+    fused = rows % 16 == 0
+    weights = [(whole_0, whole_0, 4) if fused else plain_weights(whole_0[:, : 4 * rows], whole_0[:, 4 * rows :])]
+
+    pieces = vector_pieces(vector_low.reshape(-1).astype(jnp.float32))
     mask_on = (time_mask > 0).reshape(row_count, 1)
     feats = features.reshape(row_count, CIN).astype(jnp.float32)
     normed, norm_kept = norm_forward(feats, pieces[0], pieces[1])
@@ -828,27 +1351,11 @@
     padded = with_halo(lowered(masked).reshape(clip_count, frame_count, D), KW // 2)
     strip_rows = frame_count * clip_count // 16 // PACK
     strips = to_strips(padded, frame_count)
-    conv_out = from_strips(conv_forward(strips, conv_w, strip_rows, shards), clip_count) + pieces[4]
+    conv_out = from_strips(conv_forward(strips, conv_w, 0, strip_rows, shards), clip_count) + pieces[4]
     conv_active, conv_slope = gelu_parts(conv_out)
     hidden, front_kept = norm_forward(masked + conv_active, pieces[5], pieces[6])
 
-    hidden, own_1 = fence(hidden, own_attn(1))
-    use_attn(gather_rows(own_1))
-    hidden, cache, own_1 = layer_forward(
-        hidden, attn_w[0], expand_w[0], shrink_w[0], pieces[7:16], clip_count, own_feed(1)
-    )
-    caches = [cache]
-    use_feed(gather_rows(own_1))
-    hidden, cache, _ = layer_forward(hidden, attn_w[1], expand_w[1], shrink_w[1], pieces[16:25], clip_count)
-    caches.append(cache)
-    top_low = lowered(hidden)
-    context, context_pull = jax.vjp(unit_rows, bdot(top_low, final_w) + pieces[-2])
-    context_low = lowered(context).reshape(clip_count, frame_count, PROJ)
-    held = jnp.stack([lowered(left_basis_t), lowered(attention_first), lowered(attention_second)], 1)
-    context_low, held = fence(context_low, held)
-    traded = trade(jnp.repeat(held, parts, axis=0))
-
-    counts = counts.astype(jnp.float32)
+    hidden_low = lowered(hidden)
     codes = jnp.concatenate(gather_ring(target_codes), 1).reshape(clip_count * clip_frames, QGROUPS)
     width = PROJ // QGROUPS
     code_f = code_w.astype(jnp.float32)
@@ -859,7 +1366,24 @@
     choice = jnp.concatenate(
         [(codes[:, g : g + 1] == jnp.arange(CODES)[None, :]).astype(jnp.float32) for g in range(QGROUPS)], 1
     )
-    targets, target_pull = jax.vjp(unit_rows, fdot(choice, table) + pieces[-1])
+    raw_targets = fdot(choice, table) + pieces[-1]
+    target_kept = lax.rsqrt(jnp.sum(raw_targets * raw_targets, -1, keepdims=True) + unit_epsilon)
+    targets = raw_targets * target_kept
+    forward = fused_forward if fused else layer_forward
+    hidden, hidden_low, own_1 = fence(hidden, hidden_low, own_attn(1))
+    attn_whole_1 = gather_rows(own_1)
+    hidden, hidden_low, cache, own_1 = forward(hidden, hidden_low, weights[0], pieces[7:16], clip_count, own_feed(1))
+    feed_whole_1 = gather_rows(own_1)
+    caches = [cache]
+    weights.append((attn_whole_1, feed_whole_1, 0) if fused else plain_weights(attn_whole_1, feed_whole_1))
+    hidden, top_low, cache, (targets, target_kept) = forward(
+        hidden, hidden_low, weights[1], pieces[16:25], clip_count, (targets, target_kept)
+    )
+    caches.append(cache)
+    context, context_pull = jax.vjp(unit_rows, bdot(top_low, final_w) + pieces[-2])
+    context_low = lowered(context).reshape(clip_count, frame_count, PROJ)
+
+    counts = counts.astype(jnp.float32)
     targets_low = lowered(targets).reshape(clip_count, clip_frames, PROJ)
     similar = jnp.einsum("clp,cfp->clf", targets_low, context_low, preferred_element_type=jnp.float32)
     logits = similar / contrastive_sharpness
@@ -882,7 +1406,8 @@
     )
     grad_context = jnp.einsum("clf,clp->cfp", grad_similar, targets_low, preferred_element_type=jnp.float32)
     grad_targets = jnp.einsum("clf,cfp->clp", grad_similar, context_low, preferred_element_type=jnp.float32)
-    (grad_raw,) = target_pull(grad_targets.reshape(-1, PROJ))
+    grad_targets = grad_targets.reshape(-1, PROJ)
+    grad_raw = target_kept * (grad_targets - targets * jnp.sum(grad_targets * targets, -1, keepdims=True))
     grad_table = fdot(choice.T, grad_raw)
     tables = [grad_table[g * CODES : (g + 1) * CODES] for g in range(QGROUPS)]
     grad_target_w = jnp.concatenate([fdot(code_f[g * width : (g + 1) * width], tables[g]) for g in range(QGROUPS)])
@@ -904,7 +1429,7 @@
         return share, first, second
 
     def rotate(whole_grad):
-        left_low, first_low, second_low = [traded[:, i].reshape(D, D) for i in range(3)]
+        left_low, first_low, second_low = traded[0], traded[1], traded[2]
         group = lax.axis_index("shard") // parts
         right_low = lowered(lax.dynamic_index_in_dim(right_orthogonal_basis, group, 0, keepdims=False))
         rotated = bdot(lowered(bdot(left_low, whole_grad)), right_low)
@@ -916,38 +1441,31 @@
         sent = jnp.stack([rotated_part.reshape(shards, rows, columns), update_part.reshape(shards, rows, columns)], 1)
         return sent
 
-    def feed_blocks(grad_expand, grad_shrink):
-        blocks = [grad_expand[:, j * D : (j + 1) * D].reshape(shards, -1, D) for j in range(FF // D)]
-        return blocks + [grad_shrink.reshape(shards, -1, D)]
-
-    def attn_blocks(grads):
-        return [grad.reshape(shards, -1, D) for grad in grads]
-
-    grad_middle, grad_expand, grad_shrink, feed_vectors_1 = feed_backward(
-        grad_hidden, caches[1], expand_w[1], shrink_w[1]
+    backward = fused_backward if fused else plain_backward
+    grads, chunks, attn_chunks, vectors_1, _ = backward(
+        [grad_hidden], caches[1], weights[1], pieces[16:25], clip_count, None, 4 * rows + 8 * rows * fused, None
     )
-    grad_hidden, grads, attn_vectors_1, (traded,) = attend_backward(
-        grad_middle, caches[1], attn_w[1], clip_count, traded
+    (chunks,) = fence(chunks)
+    sum_feed_1 = scatter_chunks(chunks)
+    grads, chunks, attn_chunks, vectors_0, traded = backward(
+        grads, caches[0], weights[0], pieces[7:16], clip_count, attn_chunks, 4 * rows, (spread_halves, held)
     )
-    chunks = jnp.concatenate(attn_blocks(grads) + feed_blocks(grad_expand, grad_shrink), 1)
-    grad_hidden, chunks = fence(grad_hidden, chunks)
-    sum_1 = scatter_chunks(chunks)
-    grad_middle, grad_expand, grad_shrink, feed_vectors_0 = feed_backward(
-        grad_hidden, caches[0], expand_w[0], shrink_w[0]
-    )
-    feed_grads = feed_blocks(grad_expand, grad_shrink)
-    grad_hidden, grads, attn_vectors_0, _ = attend_backward(grad_middle, caches[0], attn_w[0], clip_count)
-    grad_hidden, chunks = fence(grad_hidden, jnp.concatenate(attn_blocks(grads) + feed_grads, 1))
-    sum_0 = scatter_chunks(chunks)
-    mesh_sizes = (shards, seq_count)
+    (chunks,) = fence(chunks)
+    sum_feed_0 = scatter_chunks(chunks)
+    (attn_chunks,) = fence(attn_chunks)
+    sum_attn = scatter_chunks(attn_chunks)
+    grad_hidden = grads[0]
+    for part in grads[1:]:
+        grad_hidden = grad_hidden + part.astype(jnp.float32)
     grad_sum, grad_gain_enc, grad_bias_enc = norm_backward(grad_hidden, front_kept)
     grad_conv_low = lowered(grad_sum * conv_slope)
     grad_strips = to_strips(with_halo(grad_conv_low.reshape(clip_count, frame_count, D), KW // 2), frame_count)
     conv_chunks = conv_weight_grad(strips, grad_strips, strip_rows, shards)
-    grad_strips, conv_chunks, sum_1 = fence(grad_strips, conv_chunks, sum_1)
-    sum_1 = seq_sum(sum_1)
-    grad_back = conv_input_grad(grad_strips, conv_w, strip_rows, shards)
-    grad_back, sum_1 = fence(grad_back, sum_1)
+    grad_strips, conv_chunks, sum_feed_1 = fence(grad_strips, conv_chunks, sum_feed_1)
+    grad_back = conv_input_grad(grad_strips, conv_w, 0, strip_rows, shards)
+    traded = join_halves(traded)
+    sum_feed_1 = seq_sum(sum_feed_1)
+    grad_back, sum_feed_1, sum_feed_0, traded = fence(grad_back, sum_feed_1, sum_feed_0, traded)
     grad_masked = grad_sum + from_strips(grad_back, clip_count)
     grad_embedding = jnp.sum(jnp.where(mask_on, grad_masked, 0.0), 0, keepdims=True)
     grad_projected = lowered(jnp.where(mask_on, 0.0, grad_masked))
@@ -962,38 +1480,31 @@
         grad_gain_enc,
         grad_bias_enc,
     ]
-    vector_grads += attn_vectors_0 + feed_vectors_0 + attn_vectors_1 + feed_vectors_1
-    vector_grads = line_up(vector_grads + [grad_final_bias, grad_target_bias])
-    small_grads = [
-        lowered(item).reshape(shards, -1)
-        for item in (grad_feat_w, grad_final_w, grad_target_w, grad_codebook, vector_grads)
-    ]
-    loss_tile = jnp.broadcast_to(lowered(jnp.stack([loss_sum, mask_count]))[None], (shards, 2))
-    gap = jnp.zeros((shards, small_width - small_total - 2), jnp.bfloat16)
-    small_chunks = jnp.concatenate(small_grads + [loss_tile, gap], 1)
-    small_chunks, sum_0 = fence(small_chunks.reshape(shards, -1, taps), sum_0)
-    sum_0 = seq_sum(sum_0)
-    attn_rows = jnp.concatenate([sum_0[: 4 * rows], sum_1[: 4 * rows]]).reshape(4 * LAYERS, rows, D)
-    whole_grad = trade(jnp.repeat(lowered(attn_rows), parts, axis=0)).reshape(D, D)
+    vector_grads += vectors_0 + vectors_1
+    vector_grads += [grad_final_bias, grad_target_bias]
+    extra = jnp.pad(jnp.stack([loss_sum, mask_count])[None], ((0, 0), (0, 126)))
+    small_grads = [grad_feat_w, grad_final_w, grad_target_w, grad_codebook]
+    small_chunks = pack_grads(small_grads, vector_grads, extra, shards, SMALL_ROWS, taps)
+    sum_feed_0 = seq_sum(sum_feed_0)
+    small_chunks, sum_attn, sum_feed_0 = fence(small_chunks, sum_attn, sum_feed_0)
+    attn_rows = jnp.concatenate([seq_sum(sum_attn), sum_feed_0[: 4 * rows]]).reshape(4 * LAYERS, 1, rows, D)
+    whole_grad = join_halves(spread_halves(lowered(attn_rows)))[0]
     sent = rotate(whole_grad)
-    sent, small_chunks = fence(sent, small_chunks)
-    rotation = trade(sent)
-    small_sum, sum_conv = reduce_chunks(0, mesh_sizes, (128, 96), small_chunks, conv_chunks)
-    small_sum = small_sum.reshape(1, -1)
-    sum_conv = sum_conv.T
+    small_sum, sum_conv, rotation = reduce_chunks(
+        (shards, seq_count), (SMALL_ROWS, 96), [small_chunks, conv_chunks], sent
+    )
     arrived = rotation.reshape(4 * LAYERS, parts, 2, rows, columns).transpose(2, 0, 3, 1, 4)
     arrived = arrived.reshape(2, 4 * LAYERS, rows, D).astype(jnp.float32)
     _, rot_first, rot_second = rotated_adam(attention_first, attention_second, arrived[0])
     new_attention = attention_weight - rate_rotated * arrived[1]
-    feed_sums = [sum_0[4 * rows :], sum_1[4 * rows :]]
-    sum_loss = small_sum[0, small_total : small_total + 2]
-    sum_feat, sum_final, sum_target, sum_code, sum_vector = split_small(small_sum)
+    feed_sums = [sum_feed_0[4 * rows :], sum_feed_1]
+    (sum_feat, sum_final, sum_target, sum_code), sum_vector, sum_loss = split_small(small_sum)
     sum_expand = jnp.stack(
         [s[: -shrink_weight.shape[1]].reshape(FF // D, -1, D).transpose(1, 0, 2).reshape(-1, FF) for s in feed_sums]
     )
     sum_shrink = jnp.stack([s[-shrink_weight.shape[1] :] for s in feed_sums])
     feature_new = adam_update(feature_weight, sum_feat, feature_first, feature_second, rate_matrix, decay_rate)
-    conv_new = adam_update(conv_weight, sum_conv, conv_first, conv_second, rate_matrix, decay_rate)
+    conv_new = turned_adam(matrix_rule, conv_weight, sum_conv, conv_first, conv_second)
     expand_new = adam_update(expand_weight, sum_expand, expand_first, expand_second, rate_matrix, decay_rate)
     shrink_new = adam_update(shrink_weight, sum_shrink, shrink_first, shrink_second, rate_matrix, decay_rate)
     final_new = adam_update(final_weight, sum_final, final_first, final_second, rate_matrix, decay_rate)

time: 1050 us -> 946 us (0.901)
  Pallas kernels: 313 us -> 502 us
  matrix products: 230 us -> 54.2 us
  local copies, waits for them, and re-layouts: 175 us -> 80.8 us
  other arithmetic: 84.5 us -> 62.4 us
  waiting for transfers between devices: 180 us -> 193 us
    pallas_call x2 -> x16, Pallas kernels: 89.6 us -> 280 us  [the longest x1 99.9 us: reduce_chunks(): pl.pallas_call(functools.partial(reduce_kernel, count, seqs, sizes, True)...]
    dot_general x19 -> x3, matrix products: 75.2 us -> 8.4 us  [bdot(): return jnp.dot(left_side, right_side, preferred_element_type=jnp.float32)]
    dot_general x19 -> x3, matrix products: 68 us -> 8.34 us  [turned_dot(): lax.dot_general(left_side, right_side, NT, preferred_element_type=jnp.flo...]
    dot_general x19 -> x3, matrix products: 58.1 us -> 6.7 us  [rows_dot(): lax.dot_general(left_side, right_side, (((0,), (0,)), ((), ())), preferre...]
    unnamed x617 -> x231, local copies, waits for them, and re-layouts: 63.3 us -> 15.7 us
    slice x18 -> x10, local copies, waits for them, and re-layouts: 40.1 us -> 11.7 us  [the longest x2 2.83 us: fused_backward(): more[1:2]]
    all_gather x4, waiting for transfers between devices: 89 us -> 111 us  [gather_rows(): whole = lax.all_gather(block, 'shard', axis=0, tiled=True)]
    reduce_scatter x2 -> x3, waiting for transfers between devices: 33.7 us -> 17.6 us  [scatter_chunks(): return lax.psum_scatter(chunks, 'shard', scatter_dimension=0, tiled=False)]
  transfers between devices with their start and end apart: 20 -> 23, of which waited for: 9 -> 15; matrix products, arithmetic and copies ran while one was open for 36% -> 15% of each run, Pallas kernels for 22% -> 37%
where the time goes in v3:
time: 946 us; the launch traced here: 938 us
  Pallas kernels  502 us (53%)
  waiting for transfers between devices  193 us (20%)
  local copies, waits for them, and re-layouts  80.8 us (9%)
  other arithmetic  62.4 us (7%)
  matrix products  54.2 us (6%)
  starting transfers between devices  28.7 us (3%)
  between operations  16.3 us (2%)
    all_gather x4, waiting for transfers between devices, gather_rows(): whole = lax.all_gather(block, 'shard', axis=0, tiled=True)  111 us
    pallas_call x1, Pallas kernels, reduce_chunks(): pl.pallas_call(functools.partial(reduce_kernel, count, seqs, sizes, True)...  99.9 us
    pallas_call x2, Pallas kernels, feed_back(): pl.pallas_call(functools.partial(feed_back_kernel, len(grads) - 1, 0 if c...  56.5 us
    pallas_call x2, Pallas kernels, attend_back(): pl.pallas_call(functools.partial(attend_back_kernel, blocks), grid=(clips...  55.6 us
    pallas_call x2, Pallas kernels, feed_forward(): pl.pallas_call(feed_kernel, grid=(parts,), in_specs=[flat, flat, pl.Block...  42.3 us
    pallas_call x1, Pallas kernels, conv_forward(): pl.pallas_call(functools.partial(conv_forward_kernel, rows, shards), grid...  39.2 us
    pallas_call x2, Pallas kernels, attend(): pl.pallas_call(functools.partial(attend_kernel, blocks), grid=(clips, HEA...  37.1 us
    pallas_call x1, Pallas kernels, conv_input_grad(): pl.pallas_call(functools.partial(conv_input_kernel, rows, shards), grid=(...  31.6 us
  transfers between devices with their start and end apart: 23, of which 15 were waited for; matrix products, arithmetic and copies ran while one was open for 15% of the time, Pallas kernels for 37%

profile of v3, /device:TPU:0, one launch (start us, length us, event | category | flops | bytes accessed | tf_op | source)
XLA Modules:
  0.0 938.0 jit_solution(295760097358641859)
XLA Ops:
  8.6 2.5 pack_weights.1
  12.1 28.1 %count_draws.1.refs_0_ = bf16[2,768,384]{2,1,0:T(8,128)(2,1)} custom-call(s32[2,100,384]{2,1,0:T(8,128)} %fusion.64.n_ref), custom_call_target="tpu_custom_call" | custom-call | flops 1024 | bytes 1024 | tf_op jit(solution)/shard_map/count_draws/pallas_call | solution.py:484
  44.4 63.1 %all-gather.5.cloned.1.call-done = bf16[14848,384]{1,0:T(8,128)(2,1)} async-done(((bf16[928,384]{1,0:T(8,128)(2,1)}), bf16[14848,384]{1,0:T(8,128)(2,1)}) %all-gather.5.cloned.1.call-update) | async-done | bytes 11403280 | tf_op jit(solution)/shard_map/all_gather | solution.py:1208
  111.2 3.4 collective-permute-start
  116.4 2.8 collective-permute-done
  119.1 4.1 collective-permute-done.1
  123.4 2.1 convolution_convert_fusion.1
  125.9 5.7 copy.196
  131.6 39.2 %conv_forward.1 = f32[48,16,1024]{2,1,0:T(8,128)} custom-call(bf16[176,16,1024]{2,1,0:T(8,128)(2,1)} %bitcast.313, bf16[16,928,384]{2,1,0:T(8,128)(2,1)} %bitcast.334), custom_call_target="tpu_custom_call" | custom-call | flops 1024 | bytes 1024 | tf_op jit(solution)/shard_map/conv_forward/pallas_call | solution.py:121
  170.8 3.7 copy.164
  175.1 2.8 fusion.108
  178.0 3.7 fusion.122
  182.2 2.3 fusion.121
  186.1 33.1 %all-gather.7.cloned.1.call-done = bf16[9216,768]{1,0:T(8,128)(2,1)} async-done(((bf16[576,768]{1,0:T(8,128)(2,1)}), bf16[9216,768]{1,0:T(8,128)(2,1)}) %all-gather.7.cloned.1.call-update) | async-done | bytes 14155792 | tf_op jit(solution)/shard_map/all_gather | solution.py:1208
  219.2 6.6 project.4.q_ref.refs_0_.refs_1_
  226.8 5.0 project.5.refs_2_.refs_3_
  231.8 18.6 %attend.2 = (bf16[768,768]{1,0:T(8,128)(2,1)}, f32[2,6,2,384]{3,2,1,0:T(2,128)}) custom-call(bf16[3,768,768]{2,1,0:T(8,128)(2,1)} %project.4.q_ref.refs_0_.refs_1_, bf16[3,768,768]{2,1,0:T(8,128)(2,1)} %project.4.q_ref.refs_0_.refs_1_, bf16[3,768,768]{2,1,0:T(8,128)(2,1)} %project.4.q_ref.refs_0_.refs_1_, bf16[2,768,768]{2,1,0:T(8,128)(2,1)} %project.5.refs_2_.refs_3_, ...), custom_call_target="tpu_custom_call" | custom-call | flops 1024 | bytes 1024 | tf_op jit(solution)/shard_map/attend/pallas_call | solution.py:385
  266.8 21.0 %feed_forward.2 = (bf16[768,768]{1,0:T(8,128)(2,1)}, f32[768,768]{1,0:T(8,128)}, f32[768,1]{1,0:T(8,128)}, bf16[768,3072]{1,0:T(8,128)(2,1)}, bf16[768,3072]{1,0...) custom-call(f32[768,768]{1,0:T(8,128)} %get-tuple-element.135.hidden_ref,, ...), custom_call_target="tpu_custom_call" | custom-call | flops 1024 | bytes 1024 | tf_op jit(solution)/shard_map/feed_forward/pallas_call | solution.py:591
  290.4 2.3 multiply_reduce_fusion.6
  295.3 6.6 project.6.q_ref.refs_0_.refs_1_
  301.9 13.7 %collective-permute-done.3.x_ref.refs_1_ = bf16[768,768]{1,0:T(8,128)(2,1)} collective-permute-done((bf16[768,768]{1,0:T(8,128)(2,1)}, bf16[768,768]{1,0:T(8,128)(2,1)}, u32[]{:S(2)}, u32[]{:S(2)}) %collective-permute-start.3) | collective-permute-done | bytes 1179680 | tf_op jit(solution)/shard_map/ppermute | solution.py:984
  315.6 5.0 project.7.refs_2_.refs_3_
  321.1 18.6 %attend.3 = (bf16[768,768]{1,0:T(8,128)(2,1)}, f32[2,6,2,384]{3,2,1,0:T(2,128)}) custom-call(bf16[3,768,768]{2,1,0:T(8,128)(2,1)} %project.6.q_ref.refs_0_.refs_1_, bf16[3,768,768]{2,1,0:T(8,128)(2,1)} %project.6.q_ref.refs_0_.refs_1_, bf16[3,768,768]{2,1,0:T(8,128)(2,1)} %project.6.q_ref.refs_0_.refs_1_, bf16[2,768,768]{2,1,0:T(8,128)(2,1)} %project.7.refs_2_.refs_3_, ...), custom_call_target="tpu_custom_call" | custom-call | flops 1024 | bytes 1024 | tf_op jit(solution)/shard_map/attend/pallas_call | solution.py:385
  341.2 15.2 %all-gather.11.cloned.1.call-done = bf16[6144,768]{1,0:T(8,128)(2,1)} async-done(((bf16[384,768]{1,0:T(8,128)(2,1)}), bf16[6144,768]{1,0:T(8,128)(2,1)}) %all-gather.11.cloned.1.call-update) | async-done | bytes 9437200 | tf_op jit(solution)/shard_map/all_gather | solution.py:1208
  356.4 21.3 %feed_forward.3 = (bf16[768,768]{1,0:T(8,128)(2,1)}, f32[768,768]{1,0:T(8,128)}, f32[768,1]{1,0:T(8,128)}, bf16[768,3072]{1,0:T(8,128)(2,1)}, bf16[768,3072]{1,0...) custom-call(f32[768,768]{1,0:T(8,128)} %get-tuple-element.143.hidden_ref,, ...), custom_call_target="tpu_custom_call" | custom-call | flops 1024 | bytes 1024 | tf_op jit(solution)/shard_map/feed_forward/pallas_call | solution.py:591
  387.8 27.8 %feed_back.2 = (f32[768,768]{1,0:T(8,128)}, bf16[768,768]{1,0:T(8,128)(2,1)}, bf16[768,768]{1,0:T(8,128)(2,1)}, f32[8,768]{1,0:T(8,128)}, f32[1,3072]{1,0:T(1,128)}, /*index=5*/bf16[16,384,768]{2,1,0:T(8,128)(2,1)}) custom-call(f32[768,768]{1,0:T(8,128)} %fusion.142.refs_0_, f32[768,768]{1,0:T(8,128)} %get-tuple-element.147.refs_1_, ...), custom_call_target="tpu_custom_call" | custom-call | flops 1024 | bytes 1024 | tf_op jit(solution)/shard_map/feed_back/pallas_call | solution.py:705
  415.7 27.8 %attend_back.2 = (bf16[768,768]{1,0:T(8,128)(2,1)}, bf16[768,768]{1,0:T(8,128)(2,1)}, bf16[768,768]{1,0:T(8,128)(2,1)}, bf16[768,768]{1,0:T(8,128)(2,1)}, bf16[768,768]{1,0:T(8,128)(2,1)}) custom-call(bf16[3,768,768]{2,1,0:T(8,128)(2,1)} %project.6.q_ref.refs_0_.refs_1_, bf16[768,768]{1,0:T(8,128)(2,1)} %get-tuple-element.154.d_ref, ...), custom_call_target="tpu_custom_call" | custom-call | flops 1024 | bytes 1024 | tf_op jit(solution)/shard_map/attend_back/pallas_call | solution.py:457
  443.5 11.8 %entry_back.2 = (f32[768,768]{1,0:T(8,128)}, bf16[768,768]{1,0:T(8,128)(2,1)}) custom-call(f32[768,768]{1,0:T(8,128)} %get-tuple-element.161.sum_ref, bf16[768,768]{1,0:T(8,128)(2,1)} %get-tuple-element.156.dq_ref.refs_0_, bf16[768,768]{1,0:T(8,128)(2,1)} %get-tuple-element.157.refs_0_.refs_1_, bf16[768,768]{1,0:T(8,128)(2,1)} %get-tuple-element.158.refs_1_.refs_2_, ...), custom_call_target="tpu_custom_call" | custom-call | flops 1024 | bytes 1024 | tf_op jit(solution)/shard_map/entry_back/pallas_call | solution.py:768
  456.7 11.8 %attn_grads.2 = (bf16[16,576,768]{2,1,0:T(8,128)(2,1)}, f32[8,768]{1,0:T(8,128)}) custom-call(bf16[768,768]{1,0:T(8,128)(2,1)} %get-tuple-element.138.x_ref.refs_0_, bf16[768,768]{1,0:T(8,128)(2,1)} %collective-permute-done.3.x_ref.refs_1_, bf16[768,768]{1,0:T(8,128)(2,1)} %get-tuple-element.165.refs_2_, ...), custom_call_target="tpu_custom_call" | custom-call | flops 1024 | bytes 1024 | tf_op jit(solution)/shard_map/attn_grads/pallas_call | solution.py:810
  468.5 15.1 %collective-permute-done.5.refs_0_ = bf16[768,768]{1,0:T(8,128)(2,1)S(1)} collective-permute-done((bf16[768,768]{1,0:T(8,128)(2,1)}, bf16[768,768]{1,0:T(8,128)(2,1)S(1)}, u32[]{:S(2)}, u32[]{:S(2)}) %collective-permute-start.5) | collective-permute-done | bytes 1179680 | tf_op jit(solution)/shard_map/ppermute | solution.py:989
  484.6 28.7 %feed_back.3 = (f32[768,768]{1,0:T(8,128)}, bf16[768,768]{1,0:T(8,128)(2,1)}, bf16[768,768]{1,0:T(8,128)(2,1)}, f32[8,768]{1,0:T(8,128)}, f32[1,3072]{1,0:T(1,128)}, /*index=5*/bf16[16,576,768]{2,1,0:T(8,128)(2,1)}) custom-call(bf16[16,576,768]{2,1,0:T(8,128)(2,1)} %get-tuple-element.171.refs_0_, ...), custom_call_target="tpu_custom_call", output_to_operand_aliasing={{5}: (0, {})} | custom-call | flops 1024 | bytes 1024 | tf_op jit(solution)/shard_map/feed_back/pallas_call | solution.py:705
  520.7 3.8 all-to-all-start
  537.0 3.9 fusion.41
  544.1 27.8 %attend_back.3 = (bf16[768,768]{1,0:T(8,128)(2,1)}, bf16[768,768]{1,0:T(8,128)(2,1)}, bf16[768,768]{1,0:T(8,128)(2,1)}, bf16[768,768]{1,0:T(8,128)(2,1)}, bf16[768,768]{1,0:T(8,128)(2,1)}) custom-call(bf16[3,768,768]{2,1,0:T(8,128)(2,1)} %project.4.q_ref.refs_0_.refs_1_, bf16[768,768]{1,0:T(8,128)(2,1)} %get-tuple-element.184.d_ref, ...), custom_call_target="tpu_custom_call" | custom-call | flops 1024 | bytes 1024 | tf_op jit(solution)/shard_map/attend_back/pallas_call | solution.py:457
  573.2 11.0 %entry_back.3 = (f32[768,768]{1,0:T(8,128)}, bf16[768,768]{1,0:T(8,128)(2,1)}) custom-call(f32[768,768]{1,0:T(8,128)} %get-tuple-element.197.sum_ref, bf16[768,768]{1,0:T(8,128)(2,1)} %get-tuple-element.192.dq_ref.refs_0_, bf16[768,768]{1,0:T(8,128)(2,1)} %get-tuple-element.193.refs_0_.refs_1_, bf16[768,768]{1,0:T(8,128)(2,1)} %get-tuple-element.194.refs_1_.refs_2_, ...), custom_call_target="tpu_custom_call" | custom-call | flops 1024 | bytes 1024 | tf_op jit(solution)/shard_map/entry_back/pallas_call | solution.py:768
  591.7 2.7 fusion.143
  598.7 11.8 %attn_grads.3 = (bf16[16,192,768]{2,1,0:T(8,128)(2,1)}, f32[8,768]{1,0:T(8,128)}) custom-call(bf16[768,768]{1,0:T(8,128)(2,1)} %get-tuple-element.133.x_ref.refs_0_, bf16[768,768]{1,0:T(8,128)(2,1)} %copy-done.16, bf16[768,768]{1,0:T(8,128)(2,1)} %get-tuple-element.203.refs_2_, bf16[768,768]{1,0:T(8,128)(2,1)} %get-tuple-element.137.mixed_ref.refs_3_, ...), custom_call_target="tpu_custom_call" | custom-call | flops 1024 | bytes 1024 | tf_op jit(solution)/shard_map/attn_grads/pallas_call | solution.py:810
  613.7 3.2 multiply_reduce_fusion.1
  620.9 3.4 collective-permute-start.7
  628.1 4.1 collective-permute-done.8
  634.9 3.2 copy.195
  638.2 2.4 copy-done.3
  641.9 31.0 %conv_weight_grad.1.refs_1_ = bf16[16,768,384]{2,1,0:T(8,128)(2,1)} custom-call(bf16[176,16,1024]{2,1,0:T(8,128)(2,1)} %bitcast.314, bf16[48,16,1024]{2,1,0:T(8,128)(2,1)} %slice.617.d_ref), custom_call_target="tpu_custom_call" | custom-call | flops 35000000512 | bytes 10000000 | tf_op jit(solution)/shard_map/conv_weight_grad/pallas_call | solution.py:201
  673.0 2.3 broadcast_select_fusion.1
  675.3 2.1 pad_maximum_fusion.refs_3_
  677.5 31.6 %conv_input_grad.1.refs_0_ = f32[48,16,1024]{2,1,0:T(8,128)} custom-call(bf16[176,16,1024]{2,1,0:T(8,128)(2,1)} %get-tuple-element.212.d_ref, bf16[16,928,384]{2,1,0:T(8,128)(2,1)} %bitcast.340), custom_call_target="tpu_custom_call" | custom-call | flops 35000000512 | bytes 10000000 | tf_op jit(solution)/shard_map/conv_input_grad/pallas_call | solution.py:157
  710.2 3.8 copy.174
  714.0 2.1 collective-permute-start.11
  716.7 3.0 fusion.107
  719.8 2.4 convert_reduce_fusion.1
  725.2 3.2 fusion.28.refs_0_
  728.5 3.7 pack_grads.1.refs_0_
  734.1 2.6 convert_add_fusion.2.refs_2_
  736.7 17.6 %reduce-scatter.8.cloned.1.call-done = bf16[1,192,768]{2,1,0:T(8,128)(2,1)} async-done(((bf16[16,192,768]{2,1,0:T(8,128)(2,1)}), bf16[1,192,768]{2,1,0:T(8,128)(2,1)}) %reduce-scatter.8.cloned.1.call-update) | async-done | bytes 294928 | tf_op jit(solution)/shard_map/reduce_scatter | solution.py:1232
  756.8 5.4 collective-permute-done.12
  764.2 4.2 all-to-all-start.1
  771.9 12.2 %all-to-all-done.1 = bf16[16,1,48,384]{3,2,1,0:T(8,128)(2,1)} async-done(((bf16[16,1,48,384]{3,2,1,0:T(8,128)(2,1)}), bf16[16,1,48,384]{3,2,1,0:T(8,128)(2,1)}, u32[]{:S(2)}, u32[]{:S(2)}) %all-to-all-start.1) | async-done | bytes 589856 | tf_op jit(solution)/shard_map/all_to_all | solution.py:1236
  784.2 4.2 multiply_subtract_fusion.1
  788.4 2.3 multiply_subtract_fusion
  790.7 2.2 broadcast_select_fusion.3
  792.9 5.7 fusion.37
  798.6 4.9 fusion.32
  806.8 99.9 %reduce_chunks.1 = (f32[160,384]{1,0:T(8,128)}, f32[768,384]{1,0:T(8,128)}, bf16[16,2,48,384]{3,2,1,0:T(8,128)(2,1)}) custom-call(bf16[16,160,384]{2,1,0:T(8,128)(2,1)} %get-tuple-element.226.refs_0_, bf16[16,768,384]{2,1,0:T(8,128)(2,1)} %get-tuple-element.227.refs_1_, bf16[16,2,48,384]{3,2,1,0:T(8,128)(2,1)} %pad_maximum_fusion.5.refs_2_), custom_call_target="tpu_custom_call" | custom-call | flops 1024 | bytes 1024 | tf_op jit(solution)/shard_map/reduce_chunks/pallas_call | solution.py:963
  925.0 5.1 turned_adam.1
  (445 shorter events, 139.4 us)
Async XLA Ops:
  7.2 100.3 %all-gather.5.cloned.1.call-start = ((), (), s32[]{:S(2)}) async-start(), calls=%async_computation.5 | async-start | bytes 12115968 | tf_op jit(solution)/shard_map/all_gather | solution.py:1208
  8.6 31.6 %copy-start.17 = (f32[8,48,768]{2,1,0:T(8,128)S(1)}, f32[8,48,768]{2,1,0:T(8,128)}, u32[]{:S(2)}) copy-start(f32[8,48,768]{2,1,0:T(8,128)} %param.43) | copy-start | bytes 3538948
  11.1 29.1 %copy-start.23 = (f32[2,48,3072]{2,1,0:T(8,128)S(1)}, f32[2,48,3072]{2,1,0:T(8,128)}, u32[]{:S(2)}) copy-start(f32[2,48,3072]{2,1,0:T(8,128)} %param.48) | copy-start | bytes 3538948
  11.2 208.0 %all-gather.7.cloned.1.call-start = ((), (), s32[]{:S(2)}) async-start(), calls=%async_computation.6 | async-start | bytes 15040512 | tf_op jit(solution)/shard_map/all_gather | solution.py:1208
  42.8 252.5 %all-gather.9.cloned.1.call-start = ((), (), s32[]{:S(2)}) async-start(), calls=%async_computation.7 | async-start | bytes 5013504 | tf_op jit(solution)/shard_map/all_gather | solution.py:1208
  42.9 135.1 %copy-start.95 = (pred[768]{0:T(1024)(128)(4,1)}, pred[768]{0:T(1024)(128)(4,1)S(1)}, u32[]{:S(2)}) copy-start(pred[768]{0:T(1024)(128)(4,1)S(1)} %broadcast_in_dim.63) | copy-start | bytes 2308
  42.9 135.1 %copy-start.97 = (pred[768]{0:T(1024)(128)(4,1)}, pred[768]{0:T(1024)(128)(4,1)S(1)}, u32[]{:S(2)}) copy-start(pred[768]{0:T(1024)(128)(4,1)S(1)} %get-tuple-element.384) | copy-start | bytes 2308
  42.9 135.1 %copy-start.99 = (pred[768]{0:T(1024)(128)(4,1)}, pred[768]{0:T(1024)(128)(4,1)S(1)}, u32[]{:S(2)}) copy-start(pred[768]{0:T(1024)(128)(4,1)S(1)} %get-tuple-element.385) | copy-start | bytes 2308
  42.9 135.1 %copy-start.87 = (s32[768]{0:T(1024)}, s32[768]{0:T(1024)S(1)}, u32[]{:S(2)}) copy-start(s32[768]{0:T(1024)S(1)} %get-tuple-element.382) | copy-start | bytes 9220
  42.9 135.1 %copy-start.89 = (s32[768]{0:T(1024)}, s32[768]{0:T(1024)S(1)}, u32[]{:S(2)}) copy-start(s32[768]{0:T(1024)S(1)} %get-tuple-element.383) | copy-start | bytes 9220
  43.0 135.1 %copy-start.91 = (s32[768]{0:T(1024)}, s32[768]{0:T(1024)S(1)}, u32[]{:S(2)}) copy-start(s32[768]{0:T(1024)S(1)} %get-tuple-element.380) | copy-start | bytes 9220
  43.0 135.1 %copy-start.93 = (s32[768]{0:T(1024)}, s32[768]{0:T(1024)S(1)}, u32[]{:S(2)}) copy-start(s32[768]{0:T(1024)S(1)} %get-tuple-element.381) | copy-start | bytes 9220
  44.0 66.0 %copy-start.65 = (f32[2,384]{1,0:T(2,128)}, f32[2,384]{1,0:T(2,128)S(1)}, u32[]{:S(2)}) copy-start(f32[2,384]{1,0:T(2,128)S(1)} %broadcast_multiply_fusion.4) | copy-start | bytes 9220
  44.4 65.9 %copy-start.70 = (f32[2,384]{1,0:T(2,128)}, f32[2,384]{1,0:T(2,128)S(1)}, u32[]{:S(2)}) copy-start(f32[2,384]{1,0:T(2,128)S(1)} %add_rsqrt_fusion.3) | copy-start | bytes 9220
  111.2 7.9 collective-permute-start
  114.6 8.7 collective-permute-start.1
  116.4 65.9 %copy-start.61 = (f32[768]{0:T(1024)}, f32[768]{0:T(1024)S(1)}, u32[]{:S(2)}) copy-start(f32[768]{0:T(1024)S(1)} %get-tuple-element.345) | copy-start | bytes 9220
  184.6 171.8 %all-gather.11.cloned.1.call-start = ((), (), s32[]{:S(2)}) async-start(), calls=%async_computation.8 | async-start | bytes 10027008 | tf_op jit(solution)/shard_map/all_gather | solution.py:1208
  184.6 41.2 %collective-permute-start.2 = (bf16[768,768]{1,0:T(8,128)(2,1)}, bf16[768,768]{1,0:T(8,128)(2,1)S(1)}, u32[]{:S(2)}, u32[]{:S(2)}) collective-permute-start(bf16[768,768]{1,0:T(8,128)(2,1)} %get-tuple-element.133.x_ref.refs_0_), channel_id=1, source_target_pairs={{0,16},{16,0},{1,17},{17,1},{2,18},{18,2},{3,19},{19,3},{4,20},{20... | collective-permute-start | bytes 3538952 | tf_op jit(solution)/shard_map/ppermute | solution.py:984
  250.4 427.0 %reduce-scatter.4.cloned.1.call-start = ((), (), s32[]{:S(2)}) async-start(), calls=%async_computation.9 | async-start | bytes 10027008 | tf_op jit(solution)/shard_map/reduce_scatter | solution.py:1232
  251.1 3.6 collective-permute-start.4
  256.0 34.3 %copy-start.44 = (pred[1536,320]{1,0:T(32,128)(4,1)}, pred[1536,320]{1,0:T(32,128)(4,1)S(1)}, u32[]{:S(2)}) copy-start(pred[1536,320]{1,0:T(32,128)(4,1)S(1)} %get-tuple-element.388) | copy-start | bytes 1474564
  256.0 34.3 %copy-start.46 = (pred[1536,320]{1,0:T(32,128)(4,1)}, pred[1536,320]{1,0:T(32,128)(4,1)S(1)}, u32[]{:S(2)}) copy-start(pred[1536,320]{1,0:T(32,128)(4,1)S(1)} %get-tuple-element.389) | copy-start | bytes 1474564
  287.7 27.9 %collective-permute-start.3 = (bf16[768,768]{1,0:T(8,128)(2,1)}, bf16[768,768]{1,0:T(8,128)(2,1)}, u32[]{:S(2)}, u32[]{:S(2)}) collective-permute-start(bf16[768,768]{1,0:T(8,128)(2,1)} %get-tuple-element.138.x_ref.refs_0_), channel_id=1, source_target_pairs={{0,16},{16,0},{1,17},{17,1},{2,18},{18,2},{3,19},{19,3},{4,20},{20... | collective-permute-start | bytes 3538952 | tf_op jit(solution)/shard_map/ppermute | solution.py:984
  415.6 294.6 %reduce-scatter.6.cloned.1.call-start = ((), (), s32[]{:S(2)}) async-start(), calls=%async_computation.10 | async-start | bytes 15040512 | tf_op jit(solution)/shard_map/reduce_scatter | solution.py:1232
  455.3 28.3 %collective-permute-start.5 = (bf16[768,768]{1,0:T(8,128)(2,1)}, bf16[768,768]{1,0:T(8,128)(2,1)S(1)}, u32[]{:S(2)}, u32[]{:S(2)}) collective-permute-start(bf16[768,768]{1,0:T(8,128)(2,1)} %get-tuple-element.173), channel_id=1, source_target_pairs={{0,16},{16,0},{1,17},{17,1},{2,18},{18,2},{3,19},{19,3},{4,20},{20... | collective-permute-start | bytes 3538952 | tf_op jit(solution)/shard_map/ppermute | solution.py:989
  520.7 5.0 copy-start.66
  520.7 51.3 %all-to-all-start = ((bf16[16,3,48,384]{3,2,1,0:T(8,128)(2,1)}), bf16[16,3,48,384]{3,2,1,0:T(8,128)(2,1)S(1)}, u32[]{:S(2)}, u32[]{:S(2)}) async-start(bf16[16,3,48,384]{3,2,1,0:T(8,128)(2,1)} %bitcast.52), calls=%async_computation | async-start | bytes 3538944 | tf_op jit(solution)/shard_map/all_to_all | solution.py:1236
  524.5 229.7 %reduce-scatter.8.cloned.1.call-start = ((), (), s32[]{:S(2)}) async-start(), calls=%async_computation.11 | async-start | bytes 5013504 | tf_op jit(solution)/shard_map/reduce_scatter | solution.py:1232
  527.8 7.6 copy-start
  537.0 5.8 copy-start.51
  537.0 6.1 copy-start.50
  584.2 6.8 copy-start.77
  584.3 7.4 copy-start.40
  584.3 13.1 %copy-start.6 = (bf16[16,3,48,384]{3,2,1,0:T(8,128)(2,1)S(1)}, bf16[16,3,48,384]{3,2,1,0:T(8,128)(2,1)}, u32[]{:S(2)}) copy-start(bf16[16,3,48,384]{3,2,1,0:T(8,128)(2,1)} %get-tuple-element.215) | copy-start | bytes 5308420
  584.3 28.4 %collective-permute-start.6 = (bf16[768,768]{1,0:T(8,128)(2,1)}, bf16[768,768]{1,0:T(8,128)(2,1)S(1)}, u32[]{:S(2)}, u32[]{:S(2)}) collective-permute-start(bf16[768,768]{1,0:T(8,128)(2,1)} %get-tuple-element.202), channel_id=1, source_target_pairs={{0,16},{16,0},{1,17},{17,1},{2,18},{18,2},{3,19},{19,3},{4,20},{20... | collective-permute-start | bytes 3538952 | tf_op jit(solution)/shard_map/ppermute | solution.py:989
  598.7 74.3 %collective-permute-start.10 = (bf16[3,768,384]{2,1,0:T(8,128)(2,1)}, bf16[3,768,384]{2,1,0:T(8,128)(2,1)}, u32[]{:S(2)}, u32[]{:S(2)}) collective-permute-start(bf16[3,768,384]{2,1,0:T(8,128)(2,1)} %bitcast.71), channel_id=1, source_target_pairs={{0,1},{1,0},{2,3},{3,2},{4,5},{5,4},{6,7},{7,6},{8,9},{9,8},{10,11... | collective-permute-start | bytes 5308424 | tf_op jit(solution)/shard_map/ppermute | solution.py:1325
  613.7 4.6 copy-start.35
  620.2 12.1 %copy-start.88 = (s32[768]{0:T(1024)S(1)}, s32[768]{0:T(1024)}, u32[]{:S(2)}) copy-start(s32[768]{0:T(1024)} %copy-done.87) | copy-start | bytes 9220
  620.2 12.1 %copy-start.90 = (s32[768]{0:T(1024)S(1)}, s32[768]{0:T(1024)}, u32[]{:S(2)}) copy-start(s32[768]{0:T(1024)} %copy-done.89) | copy-start | bytes 9220
  620.2 12.1 %copy-start.92 = (s32[768]{0:T(1024)S(1)}, s32[768]{0:T(1024)}, u32[]{:S(2)}) copy-start(s32[768]{0:T(1024)} %copy-done.91) | copy-start | bytes 9220
  620.2 12.1 %copy-start.94 = (s32[768]{0:T(1024)S(1)}, s32[768]{0:T(1024)}, u32[]{:S(2)}) copy-start(s32[768]{0:T(1024)} %copy-done.93) | copy-start | bytes 9220
  620.2 12.1 %copy-start.98 = (pred[768]{0:T(1024)(128)(4,1)S(1)}, pred[768]{0:T(1024)(128)(4,1)}, u32[]{:S(2)}) copy-start(pred[768]{0:T(1024)(128)(4,1)} %copy-done.97) | copy-start | bytes 2308
  620.3 12.1 %copy-start.100 = (pred[768]{0:T(1024)(128)(4,1)S(1)}, pred[768]{0:T(1024)(128)(4,1)}, u32[]{:S(2)}) copy-start(pred[768]{0:T(1024)(128)(4,1)} %copy-done.99) | copy-start | bytes 2308
  620.9 7.2 collective-permute-start.7
  624.3 8.0 collective-permute-start.8
  677.5 31.6 %collective-permute-start.9 = (bf16[384,768]{1,0:T(8,128)(2,1)}, bf16[384,768]{1,0:T(8,128)(2,1)S(1)}, u32[]{:S(2)}, u32[]{:S(2)}) collective-permute-start(bf16[384,768]{1,0:T(8,128)(2,1)} %get-tuple-element.213), channel_id=1, source_target_pairs={{0,16},{16,0},{1,17},{17,1},{2,18},{18,2},{3,19},{19,3},{4,20},{20... | collective-permute-start | bytes 1769480 | tf_op jit(solution)/shard_map/ppermute | solution.py:995
  677.5 31.6 %copy-start.36 = (bf16[384,768]{1,0:T(8,128)(2,1)S(1)}, bf16[384,768]{1,0:T(8,128)(2,1)}, u32[]{:S(2)}) copy-start(bf16[384,768]{1,0:T(8,128)(2,1)} %get-tuple-element.213) | copy-start | bytes 1769476
  714.0 20.1 %collective-permute-start.11 = (bf16[576,768]{1,0:T(8,128)(2,1)S(1)}, bf16[576,768]{1,0:T(8,128)(2,1)}, u32[]{:S(2)}, u32[]{:S(2)}) collective-permute-start(bf16[576,768]{1,0:T(8,128)(2,1)S(1)} %copy-done.30), channel_id=1, source_target_pairs={{0,16},{16,0},{1,17},{17,1},{2,18},{18,2},{3,19},{19,3},{4,20},{20... | collective-permute-start | bytes 2654216 | tf_op jit(solution)/shard_map/ppermute | solution.py:995
  754.3 7.9 collective-permute-start.12
  763.2 5.3 copy-start.9
  764.2 19.8 %all-to-all-start.1 = ((bf16[16,1,48,384]{3,2,1,0:T(8,128)(2,1)}), bf16[16,1,48,384]{3,2,1,0:T(8,128)(2,1)}, u32[]{:S(2)}, u32[]{:S(2)}) async-start(bf16[16,1,48,384]{3,2,1,0:T(8,128)(2,1)} %bitcast.96), calls=%async_computation.4 | async-start | bytes 1179648 | tf_op jit(solution)/shard_map/all_to_all | solution.py:1236
  771.1 13.1 %copy-start.24 = (f32[2,48,3072]{2,1,0:T(8,128)S(1)}, f32[2,48,3072]{2,1,0:T(8,128)}, u32[]{:S(2)}) copy-start(f32[2,48,3072]{2,1,0:T(8,128)} %param.48) | copy-start | bytes 3538948
  784.1 6.6 collective-permute-start.13
  788.3 4.5 copy-start.8
  918.4 4.5 copy-start.54
  918.4 6.0 copy-start.69
  918.4 5.9 copy-start.82
  918.5 5.9 copy-start.83
  925.0 5.2 copy-start.48
  925.0 5.2 copy-start.52
  925.0 5.2 copy-start.53
  925.0 5.2 copy-start.58
  925.0 5.2 copy-start.59
  (61 other events, 150.6 us)
Sparse Core Ops, SparseCore 0:
  11.3 96.2 all-gather.4
  110.4 108.7 all-gather.6
  222.1 51.5 all-gather.8
  276.4 79.9 all-gather.10
  415.8 109.4 reduce-scatter.3
  529.9 145.3 reduce-scatter.5
  679.6 74.6 reduce-scatter.7

commit v4 on v3

--- a/solution.py
+++ b/solution.py
@@ -829,20 +829,23 @@
 MESH = pl.DeviceIdType.MESH
 AHEAD = 3
 OTHER = 2
-
-
-def reduce_kernel(count, seqs, sizes, trades, *refs):
+GATHER_AT = 5
+
+
+def reduce_kernel(count, seqs, sizes, parts, rule, *refs):
     number = len(sizes)
-    if trades:
-        give_ref, take_ref = refs[number], refs[2 * number + 1]
-        refs = refs[:number] + refs[number + 1 : 2 * number + 1] + refs[2 * number + 2 :]
+    extra = 5 if parts else 1
+    give_ref, basis = refs[number], refs[number + 1 : number + extra]
+    take_ref = refs[2 * number + extra]
+    refs = refs[:number] + refs[number + extra : 2 * number + extra] + refs[2 * number + extra + 1 :]
     sources = refs[:number]
     outs = refs[number : 2 * number]
     bits = count.bit_length() - 1
     turns = seqs.bit_length() - 1
     levels = bits + turns
     held = refs[2 * number : 2 * number + levels]
-    send_sem, recv_sem, give_sem, take_sem = refs[2 * number + levels :]
+    send_sem, recv_sem, give_sem, take_sem = refs[2 * number + levels : 2 * number + levels + 4]
+    rest = refs[2 * number + levels + 4 :]
     me = lax.axis_index("shard")
     place = lax.axis_index("seq")
 
@@ -851,7 +854,7 @@
 
     partners = [{"shard": across(me, b)} for b in range(bits)] + [{"seq": across(place, t)} for t in range(turns)]
     others = [{"shard": lax.rem(me + k, count)} for k in range(1, count)]
-    greeted = others + partners[bits:] if trades else partners
+    greeted = others + partners[bits:]
     barrier = pltpu.get_barrier_semaphore()
     for partner in greeted:
         pl.semaphore_signal(barrier, inc=1, device_id=partner, device_id_type=MESH)
@@ -918,26 +921,78 @@
             else:
                 held[level][j, pl.ds(spot, cut)] = mine + other
 
-    swaps = []
-    if trades:
+    def trade_all(source, target_ref, send, recv):
+        copies = [pltpu.make_async_copy(source.at[me], target_ref.at[me], send.at[0])]
         for k in range(1, count):
             target = lax.rem(me + k, count)
-            swaps.append(
+            copies.append(
                 pltpu.make_async_remote_copy(
-                    src_ref=give_ref.at[target],
-                    dst_ref=take_ref.at[me],
-                    send_sem=give_sem.at[k],
-                    recv_sem=take_sem.at[k],
+                    src_ref=source.at[target],
+                    dst_ref=target_ref.at[me],
+                    send_sem=send.at[k],
+                    recv_sem=recv.at[k],
                     device_id={"shard": target},
                     device_id_type=MESH,
                 )
             )
-        own = pltpu.make_async_copy(give_ref.at[me], take_ref.at[me], give_sem.at[0])
-        own.start()
-        for swap in swaps:
-            swap.start()
+        for copy in copies:
+            copy.start()
+        return copies
+
+    def wait_all(copies):
+        for copy in copies:
+            copy.wait()
+
+    if parts:
+        left_ref, first_ref, second_ref, right_ref = basis
+        held_rows, whole, turned_rows, near_send, near_recv, back_send, back_recv = rest
+        part = lax.rem(me, parts)
+        columns = give_ref.shape[2]
+
+        def gather_near():
+            wait_all(away[0])
+            whole[part] = held_rows[...].reshape(D, columns)
+            copies = []
+            for j in range(1, parts):
+                copies.append(
+                    pltpu.make_async_remote_copy(
+                        src_ref=whole.at[part],
+                        dst_ref=whole.at[part],
+                        send_sem=near_send.at[j],
+                        recv_sem=near_recv.at[j],
+                        device_id={"shard": me - part + lax.rem(part + j, parts)},
+                        device_id_type=MESH,
+                    )
+                )
+                copies[-1].start()
+            away.append(copies)
+
+        def own_columns(values):
+            kept = values[:, 0:columns]
+            for j in range(1, parts):
+                kept = jnp.where(part == j, values[:, j * columns : (j + 1) * columns], kept)
+            return kept.astype(jnp.bfloat16)
+
+        def turn():
+            wait_all(away[1])
+            grad = jnp.concatenate([whole[j] for j in range(parts)], 1)
+            left, right = left_ref[...], right_ref[...]
+            rotated = mm(mm(left, grad).astype(jnp.bfloat16), right)
+            share = rule(first_ref[...].astype(jnp.float32), second_ref[...].astype(jnp.float32), rotated)[0]
+            back = own_columns(mm(share.astype(jnp.bfloat16), right, NT))
+            turned_rows[:, 0] = own_columns(rotated).reshape(count, -1, columns)
+            turned_rows[:, 1] = mm(turned(left), back).astype(jnp.bfloat16).reshape(count, -1, columns)
+            away.append(trade_all(turned_rows, take_ref, back_send, back_recv))
+
+        away = [trade_all(give_ref, held_rows, give_sem, take_sem)]
+        between = {GATHER_AT: gather_near, GATHER_AT + 2: turn}
+    else:
+        away = [trade_all(give_ref, take_ref, give_sem, take_sem)]
+        between = {}
     delay = [0, 1] + [1 + AHEAD * level for level in range(1, levels)]
     for wave in range(len(pieces) + delay[-1]):
+        if wave in between:
+            between[wave]()
         for level in range(levels, -1, -1):
             piece = wave - delay[level]
             if 0 <= piece < len(pieces):
@@ -945,13 +1000,10 @@
                     absorb(piece, level - 1)
                 if level < levels:
                     launch(piece, level)
-    if trades:
-        own.wait()
-        for swap in swaps:
-            swap.wait()
-
-
-def reduce_chunks(mesh_sizes, cuts, chunks, give):
+    wait_all(away[-1])
+
+
+def reduce_chunks(mesh_sizes, cuts, chunks, give, parts, rule, basis):
     count, seqs = mesh_sizes
     bits, turns = count.bit_length() - 1, seqs.bit_length() - 1
     lanes = chunks[0].shape[2]
@@ -960,19 +1012,78 @@
     number = sum(rows // cut for rows, cut in sizes)
     slots = [2 ** (bits - 1 - level) for level in range(bits)] + [1] * turns
     spec = pl.BlockSpec(memory_space=pltpu.VMEM)
+    scratch = [pltpu.VMEM((n, total, lanes), jnp.bfloat16) for n in slots]
+    scratch += [pltpu.SemaphoreType.DMA((number, bits + turns, count // 2))] * 2
+    scratch += [pltpu.SemaphoreType.DMA((count,))] * 2
+    taken = give.shape
+    if parts:
+        _, depth, columns = give.shape
+        taken = (count, 2, depth, columns)
+        scratch += [
+            pltpu.VMEM(give.shape, jnp.bfloat16),
+            pltpu.VMEM((parts, D, columns), jnp.bfloat16),
+            pltpu.VMEM(taken, jnp.bfloat16),
+        ]
+        scratch += [pltpu.SemaphoreType.DMA((parts,))] * 2 + [pltpu.SemaphoreType.DMA((count,))] * 2
     return pl.pallas_call(
-        functools.partial(reduce_kernel, count, seqs, sizes, True),
-        in_specs=[spec] * (len(chunks) + 1),
+        functools.partial(reduce_kernel, count, seqs, sizes, parts, rule),
+        in_specs=[spec] * (len(chunks) + 1 + len(basis)),
         out_specs=[spec] * (len(chunks) + 1),
         out_shape=[jax.ShapeDtypeStruct(c.shape[1:], jnp.float32) for c in chunks]
-        + [jax.ShapeDtypeStruct(give.shape, give.dtype)],
-        scratch_shapes=[pltpu.VMEM((n, total, lanes), jnp.bfloat16) for n in slots]
-        + [pltpu.SemaphoreType.DMA((number, bits + turns, count // 2))] * 2
-        + [pltpu.SemaphoreType.DMA((count,))] * 2,
+        + [jax.ShapeDtypeStruct(taken, give.dtype)],
+        scratch_shapes=scratch,
         cost_estimate=SMALL_COST,
         compiler_params=pltpu.CompilerParams(collective_id=0, has_side_effects=True, vmem_limit_bytes=VMEM),
         name="reduce_chunks",
-    )(*chunks, give)
+    )(*chunks, give, *basis)
+
+
+def finish_kernel(rules, parts, shapes, *refs):
+    number = len(shapes)
+    small_ref, conv_sum_ref, take_ref = refs[:3]
+    ins = [refs[3 + 3 * i : 6 + 3 * i] for i in range(number + 3)]
+    outs = [refs[3 * number + 12 + 3 * i : 3 * number + 15 + 3 * i] for i in range(number + 3)]
+    conv_rule, turned_rule, vector_rule, small_rules = rules
+
+    def put(at, values):
+        for ref, value in zip(outs[at], values):
+            ref[...] = value
+
+    put(0, conv_rule(ins[0][0][...], conv_sum_ref[...].T, ins[0][1][...], ins[0][2][...]))
+    for m in range(ins[1][0].shape[0]):
+        rotated = jnp.concatenate([take_ref[m * parts + j, 0] for j in range(parts)], 1).astype(jnp.float32)
+        update = jnp.concatenate([take_ref[m * parts + j, 1] for j in range(parts)], 1).astype(jnp.float32)
+        weight, first, second = turned_rule(ins[1][0][m], update, ins[1][1][m], ins[1][2][m], rotated)
+        outs[1][0][m] = weight
+        outs[1][1][m] = first
+        outs[1][2][m] = second
+    taps = small_ref.shape[1]
+    start = 0
+    for i, (depth, width) in enumerate(shapes):
+        count = -(-width // taps)
+        grad = jnp.concatenate([small_ref[start + j * depth : start + (j + 1) * depth, :] for j in range(count)], 1)
+        start += count * depth
+        put(3 + i, small_rules[i](ins[3 + i][0][...], grad[:, :width], ins[3 + i][1][...], ins[3 + i][2][...]))
+    size = ins[2][0].shape[1]
+    count = -(-size // taps)
+    grad = jnp.concatenate([small_ref[start + j : start + j + 1, :] for j in range(count)], 1)[:, :size]
+    put(2, vector_rule(ins[2][0][...], grad, ins[2][1][...], ins[2][2][...]))
+
+
+def finish(rules, parts, small_sum, conv_sum, take, conv, attention, vector, small):
+    vector = tuple(v.reshape(1, -1) for v in vector)
+    operands = list(conv) + list(attention) + list(vector) + [item for triple in small for item in triple]
+    shapes = [triple[0].shape for triple in small]
+    results = pl.pallas_call(
+        functools.partial(finish_kernel, rules, parts, shapes),
+        out_shape=[jax.ShapeDtypeStruct(item.shape, jnp.float32) for item in operands],
+        cost_estimate=SMALL_COST,
+        compiler_params=pltpu.CompilerParams(vmem_limit_bytes=VMEM),
+        name="finish",
+    )(small_sum, conv_sum, take, *operands)
+    triples = [tuple(results[3 * i : 3 * i + 3]) for i in range(len(results) // 3)]
+    triples[2] = tuple(v.reshape(-1) for v in triples[2])
+    return triples
 
 
 def swap_moves(count, step):
@@ -1202,6 +1313,30 @@
 
 def matrix_rule(weight, grad, first, second):
     return adam_update(weight, grad, first, second, rate_matrix, decay_rate)
+
+
+def target_rule(weight, grad, first, second):
+    return adam_update(weight, grad, first, second, rate_target, decay_rate)
+
+
+def codebook_rule(weight, grad, first, second):
+    return adam_update(weight, grad, first, second, rate_codebook, decay_rate)
+
+
+def vector_rule(weight, grad, first, second):
+    return adam_update(weight, grad, first, second, rate_vector, 0.0)
+
+
+def rotated_adam(first, second, grad):
+    first = beta_rotated * first + (1 - beta_rotated) * grad
+    second = beta_rotated * second + (1 - beta_rotated) * grad * grad
+    share = first / (1 - beta_rotated**STEP) / (jnp.sqrt(second / (1 - beta_rotated**STEP)) + adam_epsilon)
+    return share, first, second
+
+
+def attention_rule(weight, update, first, second, rotated):
+    _, first, second = rotated_adam(first, second, rotated)
+    return weight - rate_rotated * update, first, second
 
 
 def gather_rows(block):
@@ -1310,11 +1445,13 @@
     blocks, vector_low, _ = split_small(first_all[:, D:])
     feat_w, final_w, target_w, code_w = [block.reshape(-1, block.shape[-1]) for block in blocks]
 
+    def cut_halves(block):
+        number = block.shape[1]
+        cut = block.reshape(4 * LAYERS, number, rows, parts, D // parts).transpose(0, 3, 1, 2, 4)
+        return cut.reshape(shards, number, rows, D // parts)
+
     def spread_halves(block):
-        number = block.shape[1]
-        columns = D // parts
-        cut = block.reshape(4 * LAYERS, number, rows, parts, columns).transpose(0, 3, 1, 2, 4)
-        return trade(cut.reshape(shards, number, rows, columns))
+        return trade(cut_halves(block))
 
     def join_halves(got):
         number = got.shape[1]
@@ -1422,16 +1559,11 @@
     grad_hidden = turned_dot(grad_context_low, final_w)
 
     columns = D // parts
-    def rotated_adam(first, second, grad):
-        first = beta_rotated * first + (1 - beta_rotated) * grad
-        second = beta_rotated * second + (1 - beta_rotated) * grad * grad
-        share = first / (1 - beta_rotated**STEP) / (jnp.sqrt(second / (1 - beta_rotated**STEP)) + adam_epsilon)
-        return share, first, second
+    group = lax.axis_index("shard") // parts
+    right_low = lowered(lax.dynamic_index_in_dim(right_orthogonal_basis, group, 0, keepdims=False))
 
     def rotate(whole_grad):
         left_low, first_low, second_low = traded[0], traded[1], traded[2]
-        group = lax.axis_index("shard") // parts
-        right_low = lowered(lax.dynamic_index_in_dim(right_orthogonal_basis, group, 0, keepdims=False))
         rotated = bdot(lowered(bdot(left_low, whole_grad)), right_low)
         direction = rotated_adam(first_low.astype(jnp.float32), second_low.astype(jnp.float32), rotated)[0]
         half_back = lowered(turned_dot(lowered(direction), right_low))
@@ -1488,34 +1620,50 @@
     sum_feed_0 = seq_sum(sum_feed_0)
     small_chunks, sum_attn, sum_feed_0 = fence(small_chunks, sum_attn, sum_feed_0)
     attn_rows = jnp.concatenate([seq_sum(sum_attn), sum_feed_0[: 4 * rows]]).reshape(4 * LAYERS, 1, rows, D)
-    whole_grad = join_halves(spread_halves(lowered(attn_rows)))[0]
-    sent = rotate(whole_grad)
-    small_sum, sum_conv, rotation = reduce_chunks(
-        (shards, seq_count), (SMALL_ROWS, 96), [small_chunks, conv_chunks], sent
-    )
-    arrived = rotation.reshape(4 * LAYERS, parts, 2, rows, columns).transpose(2, 0, 3, 1, 4)
-    arrived = arrived.reshape(2, 4 * LAYERS, rows, D).astype(jnp.float32)
-    _, rot_first, rot_second = rotated_adam(attention_first, attention_second, arrived[0])
-    new_attention = attention_weight - rate_rotated * arrived[1]
+    mesh_sizes, cuts, last_chunks = (shards, seq_count), (SMALL_ROWS, 128), [small_chunks, conv_chunks]
+    if fused:
+        give = cut_halves(lowered(attn_rows)).reshape(shards, rows, columns)
+        basis = [traded[0], traded[1], traded[2], right_low]
+        small_sum, sum_conv, rotation = reduce_chunks(mesh_sizes, cuts, last_chunks, give, parts, rotated_adam, basis)
+    else:
+        sent = rotate(join_halves(spread_halves(lowered(attn_rows)))[0])
+        small_sum, sum_conv, rotation = reduce_chunks(mesh_sizes, cuts, last_chunks, sent, 0, None, [])
     feed_sums = [sum_feed_0[4 * rows :], sum_feed_1]
-    (sum_feat, sum_final, sum_target, sum_code), sum_vector, sum_loss = split_small(small_sum)
+    small_sums, sum_vector, sum_loss = split_small(small_sum)
     sum_expand = jnp.stack(
         [s[: -shrink_weight.shape[1]].reshape(FF // D, -1, D).transpose(1, 0, 2).reshape(-1, FF) for s in feed_sums]
     )
     sum_shrink = jnp.stack([s[-shrink_weight.shape[1] :] for s in feed_sums])
-    feature_new = adam_update(feature_weight, sum_feat, feature_first, feature_second, rate_matrix, decay_rate)
-    conv_new = turned_adam(matrix_rule, conv_weight, sum_conv, conv_first, conv_second)
     expand_new = adam_update(expand_weight, sum_expand, expand_first, expand_second, rate_matrix, decay_rate)
     shrink_new = adam_update(shrink_weight, sum_shrink, shrink_first, shrink_second, rate_matrix, decay_rate)
-    final_new = adam_update(final_weight, sum_final, final_first, final_second, rate_matrix, decay_rate)
-    target_new = adam_update(target_weight, sum_target, target_first, target_second, rate_target, decay_rate)
-    codebook_new = adam_update(codebook_weight, sum_code, codebook_first, codebook_second, rate_codebook, decay_rate)
-    vector_new = adam_update(vector_params, sum_vector, vector_first, vector_second, rate_vector, 0.0)
+    conv_all = (conv_weight, conv_first, conv_second)
+    attention_all = (attention_weight, attention_first, attention_second)
+    vector_all = (vector_params, vector_first, vector_second)
+    small_all = [
+        (feature_weight, feature_first, feature_second),
+        (final_weight, final_first, final_second),
+        (target_weight, target_first, target_second),
+        (codebook_weight, codebook_first, codebook_second),
+    ]
+    small_rules = [matrix_rule, matrix_rule, target_rule, codebook_rule]
+    if fused:
+        rules = (matrix_rule, attention_rule, vector_rule, small_rules)
+        results = finish(rules, parts, small_sum, sum_conv, rotation, conv_all, attention_all, vector_all, small_all)
+        conv_new, attention_new, vector_new, feature_new, final_new, target_new, codebook_new = results
+    else:
+        arrived = rotation.reshape(4 * LAYERS, parts, 2, rows, columns).transpose(2, 0, 3, 1, 4)
+        arrived = arrived.reshape(2, 4 * LAYERS, rows, D).astype(jnp.float32)
+        attention_new = attention_rule(attention_weight, arrived[1], attention_first, attention_second, arrived[0])
+        conv_new = turned_adam(matrix_rule, conv_weight, sum_conv, conv_first, conv_second)
+        vector_new = vector_rule(vector_params, sum_vector, vector_first, vector_second)
+        feature_new, final_new, target_new, codebook_new = [
+            rule(triple[0], grad, triple[1], triple[2]) for rule, grad, triple in zip(small_rules, small_sums, small_all)
+        ]
     return (
         (sum_loss,)
         + feature_new
         + conv_new
-        + (new_attention, rot_first, rot_second)
+        + attention_new
         + expand_new
         + shrink_new
         + final_new

time: 946 us -> 907 us (0.959)
  waiting for transfers between devices: 193 us -> 165 us
  Pallas kernels: 502 us -> 517 us
  other arithmetic: 62.4 us -> 49.7 us
  matrix products: 54.2 us -> 43.1 us
    pallas_call x2, Pallas kernels: 105 us -> 120 us  [the longest x1 112 us: reduce_chunks(): pl.pallas_call(functools.partial(reduce_kernel, count, seqs, sizes, parts...]
    all_to_all x2 -> x1, waiting for transfers between devices: 12.2 us -> 0.01 us  [trade(): lax.all_to_all(chunks, 'shard', split_axis=0, concat_axis=0, tiled=True)]
  transfers between devices with their start and end apart: 23 -> 21, of which waited for: 15 -> 13; matrix products, arithmetic and copies ran while one was open for 15% -> 16% of each run, Pallas kernels for 37% -> 38%
where the time goes in v4:
time: 907 us; the launch traced here: 899 us
  Pallas kernels  517 us (57%)
  waiting for transfers between devices  165 us (18%)
  local copies, waits for them, and re-layouts  83.6 us (9%)
  other arithmetic  49.7 us (5%)
  matrix products  43.1 us (5%)
  starting transfers between devices  24.6 us (3%)
  between operations  16.1 us (2%)
    pallas_call x1, Pallas kernels, reduce_chunks(): pl.pallas_call(functools.partial(reduce_kernel, count, seqs, sizes, parts...  112 us
    all_gather x4, waiting for transfers between devices, gather_rows(): whole = lax.all_gather(block, 'shard', axis=0, tiled=True)  111 us
    pallas_call x2, Pallas kernels, feed_back(): pl.pallas_call(functools.partial(feed_back_kernel, len(grads) - 1, 0 if c...  56.5 us
    pallas_call x2, Pallas kernels, attend_back(): pl.pallas_call(functools.partial(attend_back_kernel, blocks), grid=(clips...  55.6 us
    pallas_call x2, Pallas kernels, feed_forward(): pl.pallas_call(feed_kernel, grid=(parts,), in_specs=[flat, flat, pl.Block...  42.3 us
    pallas_call x1, Pallas kernels, conv_forward(): pl.pallas_call(functools.partial(conv_forward_kernel, rows, shards), grid...  39.2 us
    pallas_call x2, Pallas kernels, attend(): pl.pallas_call(functools.partial(attend_kernel, blocks), grid=(clips, HEA...  37.1 us
    pallas_call x1, Pallas kernels, conv_input_grad(): pl.pallas_call(functools.partial(conv_input_kernel, rows, shards), grid=(...  31.6 us
  transfers between devices with their start and end apart: 21, of which 13 were waited for; matrix products, arithmetic and copies ran while one was open for 16% of the time, Pallas kernels for 38%

profile of v4, /device:TPU:0, one launch (start us, length us, event | category | flops | bytes accessed | tf_op | source)
XLA Modules:
  0.0 899.2 jit_solution(2585224032784252490)
XLA Ops:
  8.6 2.5 pack_weights.1
  12.1 28.1 %count_draws.1.refs_0_ = bf16[2,768,384]{2,1,0:T(8,128)(2,1)} custom-call(s32[2,100,384]{2,1,0:T(8,128)} %fusion.43.n_ref), custom_call_target="tpu_custom_call" | custom-call | flops 1024 | bytes 1024 | tf_op jit(solution)/shard_map/count_draws/pallas_call | solution.py:484
  44.4 63.1 %all-gather.5.cloned.1.call-done = bf16[14848,384]{1,0:T(8,128)(2,1)} async-done(((bf16[928,384]{1,0:T(8,128)(2,1)}), bf16[14848,384]{1,0:T(8,128)(2,1)}) %all-gather.5.cloned.1.call-update) | async-done | bytes 11403280 | tf_op jit(solution)/shard_map/all_gather | solution.py:1343
  111.2 3.4 collective-permute-start
  116.4 2.7 collective-permute-done
  119.1 4.1 collective-permute-done.1
  123.4 2.1 convolution_convert_fusion.1
  125.9 5.7 copy.171
  131.6 39.2 %conv_forward.1 = f32[48,16,1024]{2,1,0:T(8,128)} custom-call(bf16[176,16,1024]{2,1,0:T(8,128)(2,1)} %bitcast.284, bf16[16,928,384]{2,1,0:T(8,128)(2,1)} %bitcast.305), custom_call_target="tpu_custom_call" | custom-call | flops 1024 | bytes 1024 | tf_op jit(solution)/shard_map/conv_forward/pallas_call | solution.py:121
  170.8 3.7 copy.143
  175.2 2.8 fusion.74
  178.1 3.7 fusion.83
  182.2 2.4 fusion.82
  186.2 33.0 %all-gather.7.cloned.1.call-done = bf16[9216,768]{1,0:T(8,128)(2,1)} async-done(((bf16[576,768]{1,0:T(8,128)(2,1)}), bf16[9216,768]{1,0:T(8,128)(2,1)}) %all-gather.7.cloned.1.call-update) | async-done | bytes 14155792 | tf_op jit(solution)/shard_map/all_gather | solution.py:1343
  219.2 6.6 project.4.q_ref.refs_0_.refs_1_
  226.8 5.0 project.5.refs_2_.refs_3_
  231.8 18.6 %attend.2 = (bf16[768,768]{1,0:T(8,128)(2,1)}, f32[2,6,2,384]{3,2,1,0:T(2,128)}) custom-call(bf16[3,768,768]{2,1,0:T(8,128)(2,1)} %project.4.q_ref.refs_0_.refs_1_, bf16[3,768,768]{2,1,0:T(8,128)(2,1)} %project.4.q_ref.refs_0_.refs_1_, bf16[3,768,768]{2,1,0:T(8,128)(2,1)} %project.4.q_ref.refs_0_.refs_1_, bf16[2,768,768]{2,1,0:T(8,128)(2,1)} %project.5.refs_2_.refs_3_, ...), custom_call_target="tpu_custom_call" | custom-call | flops 1024 | bytes 1024 | tf_op jit(solution)/shard_map/attend/pallas_call | solution.py:385
  252.7 2.0 collective-permute-done.4
  266.7 21.0 %feed_forward.2 = (bf16[768,768]{1,0:T(8,128)(2,1)}, f32[768,768]{1,0:T(8,128)}, f32[768,1]{1,0:T(8,128)}, bf16[768,3072]{1,0:T(8,128)(2,1)}, bf16[768,3072]{1,0...) custom-call(f32[768,768]{1,0:T(8,128)} %get-tuple-element.153.hidden_ref,, ...), custom_call_target="tpu_custom_call" | custom-call | flops 1024 | bytes 1024 | tf_op jit(solution)/shard_map/feed_forward/pallas_call | solution.py:591
  290.4 2.3 multiply_reduce_fusion.6
  295.4 6.6 project.6.q_ref.refs_0_.refs_1_
  301.9 13.6 %collective-permute-done.3.x_ref.refs_1_ = bf16[768,768]{1,0:T(8,128)(2,1)} collective-permute-done((bf16[768,768]{1,0:T(8,128)(2,1)}, bf16[768,768]{1,0:T(8,128)(2,1)}, u32[]{:S(2)}, u32[]{:S(2)}) %collective-permute-start.3) | collective-permute-done | bytes 1179680 | tf_op jit(solution)/shard_map/ppermute | solution.py:1095
  315.6 5.0 project.7.refs_2_.refs_3_
  321.1 18.5 %attend.3 = (bf16[768,768]{1,0:T(8,128)(2,1)}, f32[2,6,2,384]{3,2,1,0:T(2,128)}) custom-call(bf16[3,768,768]{2,1,0:T(8,128)(2,1)} %project.6.q_ref.refs_0_.refs_1_, bf16[3,768,768]{2,1,0:T(8,128)(2,1)} %project.6.q_ref.refs_0_.refs_1_, bf16[3,768,768]{2,1,0:T(8,128)(2,1)} %project.6.q_ref.refs_0_.refs_1_, bf16[2,768,768]{2,1,0:T(8,128)(2,1)} %project.7.refs_2_.refs_3_, ...), custom_call_target="tpu_custom_call" | custom-call | flops 1024 | bytes 1024 | tf_op jit(solution)/shard_map/attend/pallas_call | solution.py:385
  341.2 15.2 %all-gather.11.cloned.1.call-done = bf16[6144,768]{1,0:T(8,128)(2,1)} async-done(((bf16[384,768]{1,0:T(8,128)(2,1)}), bf16[6144,768]{1,0:T(8,128)(2,1)}) %all-gather.11.cloned.1.call-update) | async-done | bytes 9437200 | tf_op jit(solution)/shard_map/all_gather | solution.py:1343
  356.4 21.3 %feed_forward.3 = (bf16[768,768]{1,0:T(8,128)(2,1)}, f32[768,768]{1,0:T(8,128)}, f32[768,1]{1,0:T(8,128)}, bf16[768,3072]{1,0:T(8,128)(2,1)}, bf16[768,3072]{1,0...) custom-call(f32[768,768]{1,0:T(8,128)} %get-tuple-element.161.hidden_ref,, ...), custom_call_target="tpu_custom_call" | custom-call | flops 1024 | bytes 1024 | tf_op jit(solution)/shard_map/feed_forward/pallas_call | solution.py:591
  387.7 27.8 %feed_back.2 = (f32[768,768]{1,0:T(8,128)}, bf16[768,768]{1,0:T(8,128)(2,1)}, bf16[768,768]{1,0:T(8,128)(2,1)}, f32[8,768]{1,0:T(8,128)}, f32[1,3072]{1,0:T(1,128)}, /*index=5*/bf16[16,384,768]{2,1,0:T(8,128)(2,1)}) custom-call(f32[768,768]{1,0:T(8,128)} %fusion.100.refs_0_, f32[768,768]{1,0:T(8,128)} %get-tuple-element.165.refs_1_, ...), custom_call_target="tpu_custom_call" | custom-call | flops 1024 | bytes 1024 | tf_op jit(solution)/shard_map/feed_back/pallas_call | solution.py:705
  415.6 27.7 %attend_back.2 = (bf16[768,768]{1,0:T(8,128)(2,1)}, bf16[768,768]{1,0:T(8,128)(2,1)}, bf16[768,768]{1,0:T(8,128)(2,1)}, bf16[768,768]{1,0:T(8,128)(2,1)}, bf16[768,768]{1,0:T(8,128)(2,1)}) custom-call(bf16[3,768,768]{2,1,0:T(8,128)(2,1)} %project.6.q_ref.refs_0_.refs_1_, bf16[768,768]{1,0:T(8,128)(2,1)} %get-tuple-element.172.d_ref, ...), custom_call_target="tpu_custom_call" | custom-call | flops 1024 | bytes 1024 | tf_op jit(solution)/shard_map/attend_back/pallas_call | solution.py:457
  443.4 11.8 %entry_back.2 = (f32[768,768]{1,0:T(8,128)}, bf16[768,768]{1,0:T(8,128)(2,1)}) custom-call(f32[768,768]{1,0:T(8,128)} %get-tuple-element.179.sum_ref, bf16[768,768]{1,0:T(8,128)(2,1)} %get-tuple-element.174.dq_ref.refs_0_, bf16[768,768]{1,0:T(8,128)(2,1)} %get-tuple-element.175.refs_0_.refs_1_, bf16[768,768]{1,0:T(8,128)(2,1)} %get-tuple-element.176.refs_1_.refs_2_, ...), custom_call_target="tpu_custom_call" | custom-call | flops 1024 | bytes 1024 | tf_op jit(solution)/shard_map/entry_back/pallas_call | solution.py:768
  456.6 11.8 %attn_grads.2 = (bf16[16,576,768]{2,1,0:T(8,128)(2,1)}, f32[8,768]{1,0:T(8,128)}) custom-call(bf16[768,768]{1,0:T(8,128)(2,1)} %get-tuple-element.156.x_ref.refs_0_, bf16[768,768]{1,0:T(8,128)(2,1)} %collective-permute-done.3.x_ref.refs_1_, bf16[768,768]{1,0:T(8,128)(2,1)} %get-tuple-element.183.refs_2_, ...), custom_call_target="tpu_custom_call" | custom-call | flops 1024 | bytes 1024 | tf_op jit(solution)/shard_map/attn_grads/pallas_call | solution.py:810
  468.4 15.1 %collective-permute-done.5.refs_0_ = bf16[768,768]{1,0:T(8,128)(2,1)S(1)} collective-permute-done((bf16[768,768]{1,0:T(8,128)(2,1)}, bf16[768,768]{1,0:T(8,128)(2,1)S(1)}, u32[]{:S(2)}, u32[]{:S(2)}) %collective-permute-start.5) | collective-permute-done | bytes 1179680 | tf_op jit(solution)/shard_map/ppermute | solution.py:1100
  484.5 28.7 %feed_back.3 = (f32[768,768]{1,0:T(8,128)}, bf16[768,768]{1,0:T(8,128)(2,1)}, bf16[768,768]{1,0:T(8,128)(2,1)}, f32[8,768]{1,0:T(8,128)}, f32[1,3072]{1,0:T(1,128)}, /*index=5*/bf16[16,576,768]{2,1,0:T(8,128)(2,1)}) custom-call(bf16[16,576,768]{2,1,0:T(8,128)(2,1)} %get-tuple-element.189.refs_0_, ...), custom_call_target="tpu_custom_call", output_to_operand_aliasing={{5}: (0, {})} | custom-call | flops 1024 | bytes 1024 | tf_op jit(solution)/shard_map/feed_back/pallas_call | solution.py:705
  520.5 3.9 all-to-all-start
  527.3 2.8 fusion.15.refs_6_
  537.4 2.2 fusion.102
  541.4 3.9 fusion.22
  548.5 27.8 %attend_back.3 = (bf16[768,768]{1,0:T(8,128)(2,1)}, bf16[768,768]{1,0:T(8,128)(2,1)}, bf16[768,768]{1,0:T(8,128)(2,1)}, bf16[768,768]{1,0:T(8,128)(2,1)}, bf16[768,768]{1,0:T(8,128)(2,1)}) custom-call(bf16[3,768,768]{2,1,0:T(8,128)(2,1)} %project.4.q_ref.refs_0_.refs_1_, bf16[768,768]{1,0:T(8,128)(2,1)} %get-tuple-element.202.d_ref, ...), custom_call_target="tpu_custom_call" | custom-call | flops 1024 | bytes 1024 | tf_op jit(solution)/shard_map/attend_back/pallas_call | solution.py:457
  577.5 11.0 %entry_back.3 = (f32[768,768]{1,0:T(8,128)}, bf16[768,768]{1,0:T(8,128)(2,1)}) custom-call(f32[768,768]{1,0:T(8,128)} %get-tuple-element.215.sum_ref, bf16[768,768]{1,0:T(8,128)(2,1)} %get-tuple-element.210.dq_ref.refs_0_, bf16[768,768]{1,0:T(8,128)(2,1)} %get-tuple-element.211.refs_0_.refs_1_, bf16[768,768]{1,0:T(8,128)(2,1)} %get-tuple-element.212.refs_1_.refs_2_, ...), custom_call_target="tpu_custom_call" | custom-call | flops 1024 | bytes 1024 | tf_op jit(solution)/shard_map/entry_back/pallas_call | solution.py:768
  596.0 2.7 fusion.101
  603.1 11.8 %attn_grads.3 = (bf16[16,192,768]{2,1,0:T(8,128)(2,1)}, f32[8,768]{1,0:T(8,128)}) custom-call(bf16[768,768]{1,0:T(8,128)(2,1)} %get-tuple-element.151.x_ref.refs_0_, bf16[768,768]{1,0:T(8,128)(2,1)} %copy-done.18, bf16[768,768]{1,0:T(8,128)(2,1)} %get-tuple-element.221.refs_2_, bf16[768,768]{1,0:T(8,128)(2,1)} %get-tuple-element.155.mixed_ref.refs_3_, ...), custom_call_target="tpu_custom_call" | custom-call | flops 1024 | bytes 1024 | tf_op jit(solution)/shard_map/attn_grads/pallas_call | solution.py:810
  614.9 2.0 collective-permute-done.6.refs_0_
  618.0 3.2 multiply_reduce_fusion.1
  625.2 3.5 collective-permute-start.7
  632.6 4.1 collective-permute-done.8
  636.9 2.1 convolution_convert_fusion
  639.4 3.2 copy.170
  642.6 2.4 copy-done.4
  646.4 30.7 %conv_weight_grad.1.refs_1_ = bf16[16,768,384]{2,1,0:T(8,128)(2,1)} custom-call(bf16[176,16,1024]{2,1,0:T(8,128)(2,1)} %bitcast.285, bf16[48,16,1024]{2,1,0:T(8,128)(2,1)} %slice.565.d_ref), custom_call_target="tpu_custom_call" | custom-call | flops 35000000512 | bytes 10000000 | tf_op jit(solution)/shard_map/conv_weight_grad/pallas_call | solution.py:201
  677.2 2.3 broadcast_select_fusion.1
  679.5 2.1 pad_maximum_fusion.refs_3_
  681.6 31.6 %conv_input_grad.1.refs_0_ = f32[48,16,1024]{2,1,0:T(8,128)} custom-call(bf16[176,16,1024]{2,1,0:T(8,128)(2,1)} %get-tuple-element.230.d_ref, bf16[16,928,384]{2,1,0:T(8,128)(2,1)} %bitcast.311), custom_call_target="tpu_custom_call" | custom-call | flops 35000000512 | bytes 10000000 | tf_op jit(solution)/shard_map/conv_input_grad/pallas_call | solution.py:157
  714.4 3.7 copy.153
  718.1 2.1 collective-permute-start.11
  720.8 3.0 fusion.73
  723.9 2.4 convert_reduce_fusion.1
  729.3 3.2 fusion.16.refs_0_
  732.6 3.8 pack_grads.1.refs_0_
  738.5 2.3 stack_reshape.7
  742.6 2.9 convert_add_fusion.2.refs_2_
  745.5 8.7 reduce-scatter.8.cloned.1.call-done
  759.8 2.4 multiply_subtract_fusion.1
  763.2 2.3 multiply_subtract_fusion
  767.3 111.7 %reduce_chunks.1 = (f32[160,384]{1,0:T(8,128)}, f32[768,384]{1,0:T(8,128)}, bf16[16,2,48,384]{3,2,1,0:T(8,128)(2,1)}) custom-call(bf16[16,160,384]{2,1,0:T(8,128)(2,1)} %get-tuple-element.244.refs_0_, bf16[16,768,384]{2,1,0:T(8,128)(2,1)} %get-tuple-element.245.refs_1_, bf16[16,48,384]{2,1,0:T(8,128)(2,1)} %bitcast.325, ...), custom_call_target="tpu_custom_call" | custom-call | flops 1024 | bytes 1024 | tf_op jit(solution)/shard_map/reduce_chunks/pallas_call | solution.py:1028
  880.2 8.0 finish.1
  (392 shorter events, 118.0 us)
Async XLA Ops:
  7.2 4.0 copy-start.46
  7.2 100.3 %all-gather.5.cloned.1.call-start = ((), (), s32[]{:S(2)}) async-start(), calls=%async_computation.4 | async-start | bytes 12115968 | tf_op jit(solution)/shard_map/all_gather | solution.py:1343
  8.6 31.6 %copy-start.16 = (f32[8,48,768]{2,1,0:T(8,128)S(1)}, f32[8,48,768]{2,1,0:T(8,128)}, u32[]{:S(2)}) copy-start(f32[8,48,768]{2,1,0:T(8,128)} %refs_6_.1) | copy-start | bytes 3538948
  11.1 29.1 %copy-start.19 = (f32[2,48,3072]{2,1,0:T(8,128)S(1)}, f32[2,48,3072]{2,1,0:T(8,128)}, u32[]{:S(2)}) copy-start(f32[2,48,3072]{2,1,0:T(8,128)} %param.48) | copy-start | bytes 3538948
  11.2 208.0 %all-gather.7.cloned.1.call-start = ((), (), s32[]{:S(2)}) async-start(), calls=%async_computation.5 | async-start | bytes 15040512 | tf_op jit(solution)/shard_map/all_gather | solution.py:1343
  42.8 252.6 %all-gather.9.cloned.1.call-start = ((), (), s32[]{:S(2)}) async-start(), calls=%async_computation.6 | async-start | bytes 5013504 | tf_op jit(solution)/shard_map/all_gather | solution.py:1343
  42.9 135.1 %copy-start.78 = (pred[768]{0:T(1024)(128)(4,1)}, pred[768]{0:T(1024)(128)(4,1)S(1)}, u32[]{:S(2)}) copy-start(pred[768]{0:T(1024)(128)(4,1)S(1)} %broadcast_in_dim.63) | copy-start | bytes 2308
  42.9 135.1 %copy-start.80 = (pred[768]{0:T(1024)(128)(4,1)}, pred[768]{0:T(1024)(128)(4,1)S(1)}, u32[]{:S(2)}) copy-start(pred[768]{0:T(1024)(128)(4,1)S(1)} %get-tuple-element.398) | copy-start | bytes 2308
  42.9 135.1 %copy-start.82 = (pred[768]{0:T(1024)(128)(4,1)}, pred[768]{0:T(1024)(128)(4,1)S(1)}, u32[]{:S(2)}) copy-start(pred[768]{0:T(1024)(128)(4,1)S(1)} %get-tuple-element.399) | copy-start | bytes 2308
  42.9 135.1 %copy-start.70 = (s32[768]{0:T(1024)}, s32[768]{0:T(1024)S(1)}, u32[]{:S(2)}) copy-start(s32[768]{0:T(1024)S(1)} %get-tuple-element.396) | copy-start | bytes 9220
  42.9 135.1 %copy-start.72 = (s32[768]{0:T(1024)}, s32[768]{0:T(1024)S(1)}, u32[]{:S(2)}) copy-start(s32[768]{0:T(1024)S(1)} %get-tuple-element.397) | copy-start | bytes 9220
  43.0 135.1 %copy-start.74 = (s32[768]{0:T(1024)}, s32[768]{0:T(1024)S(1)}, u32[]{:S(2)}) copy-start(s32[768]{0:T(1024)S(1)} %get-tuple-element.394) | copy-start | bytes 9220
  43.0 135.1 %copy-start.76 = (s32[768]{0:T(1024)}, s32[768]{0:T(1024)S(1)}, u32[]{:S(2)}) copy-start(s32[768]{0:T(1024)S(1)} %get-tuple-element.395) | copy-start | bytes 9220
  44.0 66.0 %copy-start.55 = (f32[2,384]{1,0:T(2,128)}, f32[2,384]{1,0:T(2,128)S(1)}, u32[]{:S(2)}) copy-start(f32[2,384]{1,0:T(2,128)S(1)} %broadcast_multiply_fusion.4) | copy-start | bytes 9220
  44.4 65.9 %copy-start.57 = (f32[2,384]{1,0:T(2,128)}, f32[2,384]{1,0:T(2,128)S(1)}, u32[]{:S(2)}) copy-start(f32[2,384]{1,0:T(2,128)S(1)} %add_rsqrt_fusion.3) | copy-start | bytes 9220
  111.2 7.9 collective-permute-start
  114.6 8.7 collective-permute-start.1
  116.4 65.8 %copy-start.51 = (f32[768]{0:T(1024)}, f32[768]{0:T(1024)S(1)}, u32[]{:S(2)}) copy-start(f32[768]{0:T(1024)S(1)} %get-tuple-element.359) | copy-start | bytes 9220
  184.7 171.8 %all-gather.11.cloned.1.call-start = ((), (), s32[]{:S(2)}) async-start(), calls=%async_computation.7 | async-start | bytes 10027008 | tf_op jit(solution)/shard_map/all_gather | solution.py:1343
  184.7 41.1 %collective-permute-start.2 = (bf16[768,768]{1,0:T(8,128)(2,1)}, bf16[768,768]{1,0:T(8,128)(2,1)S(1)}, u32[]{:S(2)}, u32[]{:S(2)}) collective-permute-start(bf16[768,768]{1,0:T(8,128)(2,1)} %get-tuple-element.151.x_ref.refs_0_), channel_id=1, source_target_pairs={{0,16},{16,0},{1,17},{17,1},{2,18},{18,2},{3,19},{19,3},{4,20},{20... | collective-permute-start | bytes 3538952 | tf_op jit(solution)/shard_map/ppermute | solution.py:1095
  250.4 431.2 %reduce-scatter.4.cloned.1.call-start = ((), (), s32[]{:S(2)}) async-start(), calls=%async_computation.8 | async-start | bytes 10027008 | tf_op jit(solution)/shard_map/reduce_scatter | solution.py:1367
  251.1 3.6 collective-permute-start.4
  256.0 34.4 %copy-start.42 = (pred[1536,320]{1,0:T(32,128)(4,1)}, pred[1536,320]{1,0:T(32,128)(4,1)S(1)}, u32[]{:S(2)}) copy-start(pred[1536,320]{1,0:T(32,128)(4,1)S(1)} %get-tuple-element.402) | copy-start | bytes 1474564
  256.0 34.4 %copy-start.44 = (pred[1536,320]{1,0:T(32,128)(4,1)}, pred[1536,320]{1,0:T(32,128)(4,1)S(1)}, u32[]{:S(2)}) copy-start(pred[1536,320]{1,0:T(32,128)(4,1)S(1)} %get-tuple-element.403) | copy-start | bytes 1474564
  287.8 27.8 %collective-permute-start.3 = (bf16[768,768]{1,0:T(8,128)(2,1)}, bf16[768,768]{1,0:T(8,128)(2,1)}, u32[]{:S(2)}, u32[]{:S(2)}) collective-permute-start(bf16[768,768]{1,0:T(8,128)(2,1)} %get-tuple-element.156.x_ref.refs_0_), channel_id=1, source_target_pairs={{0,16},{16,0},{1,17},{17,1},{2,18},{18,2},{3,19},{19,3},{4,20},{20... | collective-permute-start | bytes 3538952 | tf_op jit(solution)/shard_map/ppermute | solution.py:1095
  415.6 298.8 %reduce-scatter.6.cloned.1.call-start = ((), (), s32[]{:S(2)}) async-start(), calls=%async_computation.9 | async-start | bytes 15040512 | tf_op jit(solution)/shard_map/reduce_scatter | solution.py:1367
  455.1 28.3 %collective-permute-start.5 = (bf16[768,768]{1,0:T(8,128)(2,1)}, bf16[768,768]{1,0:T(8,128)(2,1)S(1)}, u32[]{:S(2)}, u32[]{:S(2)}) collective-permute-start(bf16[768,768]{1,0:T(8,128)(2,1)} %get-tuple-element.191), channel_id=1, source_target_pairs={{0,16},{16,0},{1,17},{17,1},{2,18},{18,2},{3,19},{19,3},{4,20},{20... | collective-permute-start | bytes 3538952 | tf_op jit(solution)/shard_map/ppermute | solution.py:1100
  520.5 4.4 copy-start.58
  520.5 5.0 copy-start.56
  520.5 5.6 copy-start.65
  520.5 6.2 copy-start.66
  520.5 55.8 %all-to-all-start = ((bf16[16,3,48,384]{3,2,1,0:T(8,128)(2,1)}), bf16[16,3,48,384]{3,2,1,0:T(8,128)(2,1)S(1)}, u32[]{:S(2)}, u32[]{:S(2)}) async-start(bf16[16,3,48,384]{3,2,1,0:T(8,128)(2,1)} %bitcast.52), calls=%async_computation | async-start | bytes 3538944 | tf_op jit(solution)/shard_map/all_to_all | solution.py:1371
  524.4 229.8 %reduce-scatter.8.cloned.1.call-start = ((), (), s32[]{:S(2)}) async-start(), calls=%async_computation.10 | async-start | bytes 5013504 | tf_op jit(solution)/shard_map/reduce_scatter | solution.py:1367
  531.7 7.9 copy-start
  541.4 5.8 copy-start.48
  541.4 6.1 copy-start.47
  588.6 6.8 copy-start.60
  588.6 7.4 copy-start.34
  588.6 13.1 %copy-start.7 = (bf16[16,3,48,384]{3,2,1,0:T(8,128)(2,1)S(1)}, bf16[16,3,48,384]{3,2,1,0:T(8,128)(2,1)}, u32[]{:S(2)}) copy-start(bf16[16,3,48,384]{3,2,1,0:T(8,128)(2,1)} %get-tuple-element.233) | copy-start | bytes 5308420
  588.6 28.4 %collective-permute-start.6 = (bf16[768,768]{1,0:T(8,128)(2,1)}, bf16[768,768]{1,0:T(8,128)(2,1)S(1)}, u32[]{:S(2)}, u32[]{:S(2)}) collective-permute-start(bf16[768,768]{1,0:T(8,128)(2,1)} %get-tuple-element.220), channel_id=1, source_target_pairs={{0,16},{16,0},{1,17},{17,1},{2,18},{18,2},{3,19},{19,3},{4,20},{20... | collective-permute-start | bytes 3538952 | tf_op jit(solution)/shard_map/ppermute | solution.py:1100
  603.1 74.1 %collective-permute-start.10 = (bf16[3,768,384]{2,1,0:T(8,128)(2,1)}, bf16[3,768,384]{2,1,0:T(8,128)(2,1)}, u32[]{:S(2)}, u32[]{:S(2)}) collective-permute-start(bf16[3,768,384]{2,1,0:T(8,128)(2,1)} %bitcast.71), channel_id=1, source_target_pairs={{0,1},{1,0},{2,3},{3,2},{4,5},{5,4},{6,7},{7,6},{8,9},{9,8},{10,11... | collective-permute-start | bytes 5308424 | tf_op jit(solution)/shard_map/ppermute | solution.py:1462
  618.0 4.6 copy-start.29
  621.3 3.3 copy-start.10
  624.6 12.3 %copy-start.71 = (s32[768]{0:T(1024)S(1)}, s32[768]{0:T(1024)}, u32[]{:S(2)}) copy-start(s32[768]{0:T(1024)} %copy-done.70) | copy-start | bytes 9220
  624.6 12.3 %copy-start.73 = (s32[768]{0:T(1024)S(1)}, s32[768]{0:T(1024)}, u32[]{:S(2)}) copy-start(s32[768]{0:T(1024)} %copy-done.72) | copy-start | bytes 9220
  624.6 12.3 %copy-start.75 = (s32[768]{0:T(1024)S(1)}, s32[768]{0:T(1024)}, u32[]{:S(2)}) copy-start(s32[768]{0:T(1024)} %copy-done.74) | copy-start | bytes 9220
  624.6 12.3 %copy-start.77 = (s32[768]{0:T(1024)S(1)}, s32[768]{0:T(1024)}, u32[]{:S(2)}) copy-start(s32[768]{0:T(1024)} %copy-done.76) | copy-start | bytes 9220
  624.6 12.3 %copy-start.81 = (pred[768]{0:T(1024)(128)(4,1)S(1)}, pred[768]{0:T(1024)(128)(4,1)}, u32[]{:S(2)}) copy-start(pred[768]{0:T(1024)(128)(4,1)} %copy-done.80) | copy-start | bytes 2308
  624.6 12.3 %copy-start.83 = (pred[768]{0:T(1024)(128)(4,1)S(1)}, pred[768]{0:T(1024)(128)(4,1)}, u32[]{:S(2)}) copy-start(pred[768]{0:T(1024)(128)(4,1)} %copy-done.82) | copy-start | bytes 2308
  625.2 7.3 collective-permute-start.7
  628.7 8.0 collective-permute-start.8
  681.6 31.6 %collective-permute-start.9 = (bf16[384,768]{1,0:T(8,128)(2,1)}, bf16[384,768]{1,0:T(8,128)(2,1)S(1)}, u32[]{:S(2)}, u32[]{:S(2)}) collective-permute-start(bf16[384,768]{1,0:T(8,128)(2,1)} %get-tuple-element.231), channel_id=1, source_target_pairs={{0,16},{16,0},{1,17},{17,1},{2,18},{18,2},{3,19},{19,3},{4,20},{20... | collective-permute-start | bytes 1769480 | tf_op jit(solution)/shard_map/ppermute | solution.py:1106
  681.6 31.6 %copy-start.30 = (bf16[384,768]{1,0:T(8,128)(2,1)S(1)}, bf16[384,768]{1,0:T(8,128)(2,1)}, u32[]{:S(2)}) copy-start(bf16[384,768]{1,0:T(8,128)(2,1)} %get-tuple-element.231) | copy-start | bytes 1769476
  718.1 24.5 %collective-permute-start.11 = (bf16[576,768]{1,0:T(8,128)(2,1)}, bf16[576,768]{1,0:T(8,128)(2,1)}, u32[]{:S(2)}, u32[]{:S(2)}) collective-permute-start(bf16[576,768]{1,0:T(8,128)(2,1)} %get-tuple-element.243), channel_id=1, source_target_pairs={{0,16},{16,0},{1,17},{17,1},{2,18},{18,2},{3,19},{19,3},{4,20},{20... | collective-permute-start | bytes 2654216 | tf_op jit(solution)/shard_map/ppermute | solution.py:1106
  723.8 3.7 copy-start.13
  723.8 3.6 copy-start.27
  723.8 3.6 copy-start.62
  723.8 3.6 copy-start.64
  723.8 3.6 copy-start.68
  723.8 3.6 copy-start.69
  732.6 3.8 copy-start.8
  736.4 4.4 copy-start.3
  758.0 8.1 collective-permute-start.12
  759.8 3.4 copy-start.40
  (42 other events, 81.0 us)
Sparse Core Ops, SparseCore 0:
  11.3 96.2 all-gather.4
  110.4 108.7 all-gather.6
  222.1 51.5 all-gather.8
  276.4 79.9 all-gather.10
  415.7 109.4 reduce-scatter.3
  529.8 145.3 reduce-scatter.5
  679.5 74.5 reduce-scatter.7

commit v5 on v4

--- a/solution.py
+++ b/solution.py
@@ -829,7 +829,7 @@
 MESH = pl.DeviceIdType.MESH
 AHEAD = 3
 OTHER = 2
-GATHER_AT = 5
+GATHER_AT = 3
 
 
 def reduce_kernel(count, seqs, sizes, parts, rule, *refs):
@@ -945,13 +945,27 @@
 
     if parts:
         left_ref, first_ref, second_ref, right_ref = basis
-        held_rows, whole, turned_rows, near_send, near_recv, back_send, back_recv = rest
+        held_rows, whole, turned_rows, near_send, near_recv, back_send, back_recv, other_rows, far_send, far_recv = rest
         part = lax.rem(me, parts)
         columns = give_ref.shape[2]
 
+        def ask_far():
+            wait_all(away[0])
+            copy = pltpu.make_async_remote_copy(
+                src_ref=held_rows,
+                dst_ref=other_rows,
+                send_sem=far_send,
+                recv_sem=far_recv,
+                device_id=partners[bits],
+                device_id_type=MESH,
+            )
+            copy.start()
+            away.append([copy])
+
         def gather_near():
-            wait_all(away[0])
-            whole[part] = held_rows[...].reshape(D, columns)
+            wait_all(away[1])
+            total = held_rows[...].astype(jnp.float32) + other_rows[...].astype(jnp.float32)
+            whole[part] = total.astype(jnp.bfloat16).reshape(D, columns)
             copies = []
             for j in range(1, parts):
                 copies.append(
@@ -974,7 +988,7 @@
             return kept.astype(jnp.bfloat16)
 
         def turn():
-            wait_all(away[1])
+            wait_all(away[2])
             grad = jnp.concatenate([whole[j] for j in range(parts)], 1)
             left, right = left_ref[...], right_ref[...]
             rotated = mm(mm(left, grad).astype(jnp.bfloat16), right)
@@ -985,7 +999,7 @@
             away.append(trade_all(turned_rows, take_ref, back_send, back_recv))
 
         away = [trade_all(give_ref, held_rows, give_sem, take_sem)]
-        between = {GATHER_AT: gather_near, GATHER_AT + 2: turn}
+        between = {GATHER_AT: ask_far, GATHER_AT + 2: gather_near, GATHER_AT + 3: turn}
     else:
         away = [trade_all(give_ref, take_ref, give_sem, take_sem)]
         between = {}
@@ -1025,6 +1039,7 @@
             pltpu.VMEM(taken, jnp.bfloat16),
         ]
         scratch += [pltpu.SemaphoreType.DMA((parts,))] * 2 + [pltpu.SemaphoreType.DMA((count,))] * 2
+        scratch += [pltpu.VMEM(give.shape, jnp.bfloat16)] + [pltpu.SemaphoreType.DMA] * 2
     return pl.pallas_call(
         functools.partial(reduce_kernel, count, seqs, sizes, parts, rule),
         in_specs=[spec] * (len(chunks) + 1 + len(basis)),
@@ -1617,11 +1632,16 @@
     extra = jnp.pad(jnp.stack([loss_sum, mask_count])[None], ((0, 0), (0, 126)))
     small_grads = [grad_feat_w, grad_final_w, grad_target_w, grad_codebook]
     small_chunks = pack_grads(small_grads, vector_grads, extra, shards, SMALL_ROWS, taps)
+    inside = fused and seq_count == 2
+    attn_1 = sum_feed_0[: 4 * rows]
     sum_feed_0 = seq_sum(sum_feed_0)
-    small_chunks, sum_attn, sum_feed_0 = fence(small_chunks, sum_attn, sum_feed_0)
-    attn_rows = jnp.concatenate([seq_sum(sum_attn), sum_feed_0[: 4 * rows]]).reshape(4 * LAYERS, 1, rows, D)
+    small_chunks, sum_attn, sum_feed_0, attn_1 = fence(small_chunks, sum_attn, sum_feed_0, attn_1)
+    if inside:
+        attn_rows = jnp.concatenate([sum_attn, attn_1]).reshape(4 * LAYERS, 1, rows, D)
+    else:
+        attn_rows = jnp.concatenate([seq_sum(sum_attn), sum_feed_0[: 4 * rows]]).reshape(4 * LAYERS, 1, rows, D)
     mesh_sizes, cuts, last_chunks = (shards, seq_count), (SMALL_ROWS, 128), [small_chunks, conv_chunks]
-    if fused:
+    if inside:
         give = cut_halves(lowered(attn_rows)).reshape(shards, rows, columns)
         basis = [traded[0], traded[1], traded[2], right_low]
         small_sum, sum_conv, rotation = reduce_chunks(mesh_sizes, cuts, last_chunks, give, parts, rotated_adam, basis)

time: 907 us -> 914 us (level)
  Pallas kernels: 517 us -> 527 us
    pallas_call x1, Pallas kernels: 112 us -> 122 us  [reduce_chunks(): pl.pallas_call(functools.partial(reduce_kernel, count, seqs, sizes, parts...]
  transfers between devices with their start and end apart: 21 -> 20, of which waited for: 13 -> 12; matrix products, arithmetic and copies ran while one was open for 16% -> 15% of each run, Pallas kernels for 38% -> 38%
where the time goes in v5:
time: 914 us; the launch traced here: 906 us
  Pallas kernels  527 us (58%)
  waiting for transfers between devices  163 us (18%)
  local copies, waits for them, and re-layouts  81.2 us (9%)
  other arithmetic  52.5 us (6%)
  matrix products  43.3 us (5%)
  starting transfers between devices  22.8 us (2%)
  between operations  16.1 us (2%)
    pallas_call x1, Pallas kernels, reduce_chunks(): pl.pallas_call(functools.partial(reduce_kernel, count, seqs, sizes, parts...  122 us
    all_gather x4, waiting for transfers between devices, gather_rows(): whole = lax.all_gather(block, 'shard', axis=0, tiled=True)  111 us
    pallas_call x2, Pallas kernels, feed_back(): pl.pallas_call(functools.partial(feed_back_kernel, len(grads) - 1, 0 if c...  56.5 us
    pallas_call x2, Pallas kernels, attend_back(): pl.pallas_call(functools.partial(attend_back_kernel, blocks), grid=(clips...  55.6 us
    pallas_call x2, Pallas kernels, feed_forward(): pl.pallas_call(feed_kernel, grid=(parts,), in_specs=[flat, flat, pl.Block...  42.3 us
    pallas_call x1, Pallas kernels, conv_forward(): pl.pallas_call(functools.partial(conv_forward_kernel, rows, shards), grid...  39.2 us
    pallas_call x2, Pallas kernels, attend(): pl.pallas_call(functools.partial(attend_kernel, blocks), grid=(clips, HEA...  37.1 us
    pallas_call x1, Pallas kernels, conv_input_grad(): pl.pallas_call(functools.partial(conv_input_kernel, rows, shards), grid=(...  31.6 us
  transfers between devices with their start and end apart: 20, of which 12 were waited for; matrix products, arithmetic and copies ran while one was open for 15% of the time, Pallas kernels for 38%

profile of v5, /device:TPU:0, one launch (start us, length us, event | category | flops | bytes accessed | tf_op | source)
XLA Modules:
  0.0 906.3 jit_solution(14477060178674593088)
XLA Ops:
  8.6 2.5 pack_weights.1
  12.1 28.1 %count_draws.1.refs_0_ = bf16[2,768,384]{2,1,0:T(8,128)(2,1)} custom-call(s32[2,100,384]{2,1,0:T(8,128)} %fusion.43.n_ref), custom_call_target="tpu_custom_call" | custom-call | flops 1024 | bytes 1024 | tf_op jit(solution)/shard_map/count_draws/pallas_call | solution.py:484
  44.4 63.1 %all-gather.5.cloned.1.call-done = bf16[14848,384]{1,0:T(8,128)(2,1)} async-done(((bf16[928,384]{1,0:T(8,128)(2,1)}), bf16[14848,384]{1,0:T(8,128)(2,1)}) %all-gather.5.cloned.1.call-update) | async-done | bytes 11403280 | tf_op jit(solution)/shard_map/all_gather | solution.py:1358
  111.2 3.4 collective-permute-start
  116.4 2.7 collective-permute-done
  119.1 4.1 collective-permute-done.1
  123.4 2.1 convolution_convert_fusion.1
  125.9 5.7 copy.172
  131.6 39.2 %conv_forward.1 = f32[48,16,1024]{2,1,0:T(8,128)} custom-call(bf16[176,16,1024]{2,1,0:T(8,128)(2,1)} %bitcast.284, bf16[16,928,384]{2,1,0:T(8,128)(2,1)} %bitcast.305), custom_call_target="tpu_custom_call" | custom-call | flops 1024 | bytes 1024 | tf_op jit(solution)/shard_map/conv_forward/pallas_call | solution.py:121
  170.8 3.7 copy.144
  175.2 2.8 fusion.74
  178.1 3.7 fusion.83
  182.3 2.4 fusion.82
  186.2 33.0 %all-gather.7.cloned.1.call-done = bf16[9216,768]{1,0:T(8,128)(2,1)} async-done(((bf16[576,768]{1,0:T(8,128)(2,1)}), bf16[9216,768]{1,0:T(8,128)(2,1)}) %all-gather.7.cloned.1.call-update) | async-done | bytes 14155792 | tf_op jit(solution)/shard_map/all_gather | solution.py:1358
  219.3 6.6 project.4.q_ref.refs_0_.refs_1_
  226.8 5.0 project.5.refs_2_.refs_3_
  231.8 18.6 %attend.2 = (bf16[768,768]{1,0:T(8,128)(2,1)}, f32[2,6,2,384]{3,2,1,0:T(2,128)}) custom-call(bf16[3,768,768]{2,1,0:T(8,128)(2,1)} %project.4.q_ref.refs_0_.refs_1_, bf16[3,768,768]{2,1,0:T(8,128)(2,1)} %project.4.q_ref.refs_0_.refs_1_, bf16[3,768,768]{2,1,0:T(8,128)(2,1)} %project.4.q_ref.refs_0_.refs_1_, bf16[2,768,768]{2,1,0:T(8,128)(2,1)} %project.5.refs_2_.refs_3_, ...), custom_call_target="tpu_custom_call" | custom-call | flops 1024 | bytes 1024 | tf_op jit(solution)/shard_map/attend/pallas_call | solution.py:385
  252.7 2.0 collective-permute-done.4
  266.7 21.0 %feed_forward.2 = (bf16[768,768]{1,0:T(8,128)(2,1)}, f32[768,768]{1,0:T(8,128)}, f32[768,1]{1,0:T(8,128)}, bf16[768,3072]{1,0:T(8,128)(2,1)}, bf16[768,3072]{1,0...) custom-call(f32[768,768]{1,0:T(8,128)} %get-tuple-element.154.hidden_ref,, ...), custom_call_target="tpu_custom_call" | custom-call | flops 1024 | bytes 1024 | tf_op jit(solution)/shard_map/feed_forward/pallas_call | solution.py:591
  290.4 2.3 multiply_reduce_fusion.6
  295.2 6.6 project.6.q_ref.refs_0_.refs_1_
  301.8 13.8 %collective-permute-done.3.x_ref.refs_1_ = bf16[768,768]{1,0:T(8,128)(2,1)} collective-permute-done((bf16[768,768]{1,0:T(8,128)(2,1)}, bf16[768,768]{1,0:T(8,128)(2,1)}, u32[]{:S(2)}, u32[]{:S(2)}) %collective-permute-start.3) | collective-permute-done | bytes 1179680 | tf_op jit(solution)/shard_map/ppermute | solution.py:1110
  315.6 5.0 project.7.refs_2_.refs_3_
  321.1 18.5 %attend.3 = (bf16[768,768]{1,0:T(8,128)(2,1)}, f32[2,6,2,384]{3,2,1,0:T(2,128)}) custom-call(bf16[3,768,768]{2,1,0:T(8,128)(2,1)} %project.6.q_ref.refs_0_.refs_1_, bf16[3,768,768]{2,1,0:T(8,128)(2,1)} %project.6.q_ref.refs_0_.refs_1_, bf16[3,768,768]{2,1,0:T(8,128)(2,1)} %project.6.q_ref.refs_0_.refs_1_, bf16[2,768,768]{2,1,0:T(8,128)(2,1)} %project.7.refs_2_.refs_3_, ...), custom_call_target="tpu_custom_call" | custom-call | flops 1024 | bytes 1024 | tf_op jit(solution)/shard_map/attend/pallas_call | solution.py:385
  341.2 15.1 %all-gather.11.cloned.1.call-done = bf16[6144,768]{1,0:T(8,128)(2,1)} async-done(((bf16[384,768]{1,0:T(8,128)(2,1)}), bf16[6144,768]{1,0:T(8,128)(2,1)}) %all-gather.11.cloned.1.call-update) | async-done | bytes 9437200 | tf_op jit(solution)/shard_map/all_gather | solution.py:1358
  356.3 21.3 %feed_forward.3 = (bf16[768,768]{1,0:T(8,128)(2,1)}, f32[768,768]{1,0:T(8,128)}, f32[768,1]{1,0:T(8,128)}, bf16[768,3072]{1,0:T(8,128)(2,1)}, bf16[768,3072]{1,0...) custom-call(f32[768,768]{1,0:T(8,128)} %get-tuple-element.162.hidden_ref,, ...), custom_call_target="tpu_custom_call" | custom-call | flops 1024 | bytes 1024 | tf_op jit(solution)/shard_map/feed_forward/pallas_call | solution.py:591
  387.7 27.8 %feed_back.2 = (f32[768,768]{1,0:T(8,128)}, bf16[768,768]{1,0:T(8,128)(2,1)}, bf16[768,768]{1,0:T(8,128)(2,1)}, f32[8,768]{1,0:T(8,128)}, f32[1,3072]{1,0:T(1,128)}, /*index=5*/bf16[16,384,768]{2,1,0:T(8,128)(2,1)}) custom-call(f32[768,768]{1,0:T(8,128)} %fusion.100.refs_0_, f32[768,768]{1,0:T(8,128)} %get-tuple-element.166.refs_1_, ...), custom_call_target="tpu_custom_call" | custom-call | flops 1024 | bytes 1024 | tf_op jit(solution)/shard_map/feed_back/pallas_call | solution.py:705
  415.5 27.7 %attend_back.2 = (bf16[768,768]{1,0:T(8,128)(2,1)}, bf16[768,768]{1,0:T(8,128)(2,1)}, bf16[768,768]{1,0:T(8,128)(2,1)}, bf16[768,768]{1,0:T(8,128)(2,1)}, bf16[768,768]{1,0:T(8,128)(2,1)}) custom-call(bf16[3,768,768]{2,1,0:T(8,128)(2,1)} %project.6.q_ref.refs_0_.refs_1_, bf16[768,768]{1,0:T(8,128)(2,1)} %get-tuple-element.173.d_ref, ...), custom_call_target="tpu_custom_call" | custom-call | flops 1024 | bytes 1024 | tf_op jit(solution)/shard_map/attend_back/pallas_call | solution.py:457
  443.3 11.8 %entry_back.2 = (f32[768,768]{1,0:T(8,128)}, bf16[768,768]{1,0:T(8,128)(2,1)}) custom-call(f32[768,768]{1,0:T(8,128)} %get-tuple-element.180.sum_ref, bf16[768,768]{1,0:T(8,128)(2,1)} %get-tuple-element.175.dq_ref.refs_0_, bf16[768,768]{1,0:T(8,128)(2,1)} %get-tuple-element.176.refs_0_.refs_1_, bf16[768,768]{1,0:T(8,128)(2,1)} %get-tuple-element.177.refs_1_.refs_2_, ...), custom_call_target="tpu_custom_call" | custom-call | flops 1024 | bytes 1024 | tf_op jit(solution)/shard_map/entry_back/pallas_call | solution.py:768
  456.5 11.8 %attn_grads.2 = (bf16[16,576,768]{2,1,0:T(8,128)(2,1)}, f32[8,768]{1,0:T(8,128)}) custom-call(bf16[768,768]{1,0:T(8,128)(2,1)} %get-tuple-element.157.x_ref.refs_0_, bf16[768,768]{1,0:T(8,128)(2,1)} %collective-permute-done.3.x_ref.refs_1_, bf16[768,768]{1,0:T(8,128)(2,1)} %get-tuple-element.184.refs_2_, ...), custom_call_target="tpu_custom_call" | custom-call | flops 1024 | bytes 1024 | tf_op jit(solution)/shard_map/attn_grads/pallas_call | solution.py:810
  468.3 15.1 %collective-permute-done.5.refs_0_ = bf16[768,768]{1,0:T(8,128)(2,1)S(1)} collective-permute-done((bf16[768,768]{1,0:T(8,128)(2,1)}, bf16[768,768]{1,0:T(8,128)(2,1)S(1)}, u32[]{:S(2)}, u32[]{:S(2)}) %collective-permute-start.5) | collective-permute-done | bytes 1179680 | tf_op jit(solution)/shard_map/ppermute | solution.py:1115
  484.4 28.7 %feed_back.3 = (f32[768,768]{1,0:T(8,128)}, bf16[768,768]{1,0:T(8,128)(2,1)}, bf16[768,768]{1,0:T(8,128)(2,1)}, f32[8,768]{1,0:T(8,128)}, f32[1,3072]{1,0:T(1,128)}, /*index=5*/bf16[16,576,768]{2,1,0:T(8,128)(2,1)}) custom-call(bf16[16,576,768]{2,1,0:T(8,128)(2,1)} %get-tuple-element.190.refs_0_, ...), custom_call_target="tpu_custom_call", output_to_operand_aliasing={{5}: (0, {})} | custom-call | flops 1024 | bytes 1024 | tf_op jit(solution)/shard_map/feed_back/pallas_call | solution.py:705
  520.5 3.9 all-to-all-start
  527.3 2.8 fusion.15.refs_6_
  537.3 2.2 fusion.102
  541.3 3.9 fusion.22
  548.4 27.9 %attend_back.3 = (bf16[768,768]{1,0:T(8,128)(2,1)}, bf16[768,768]{1,0:T(8,128)(2,1)}, bf16[768,768]{1,0:T(8,128)(2,1)}, bf16[768,768]{1,0:T(8,128)(2,1)}, bf16[768,768]{1,0:T(8,128)(2,1)}) custom-call(bf16[3,768,768]{2,1,0:T(8,128)(2,1)} %project.4.q_ref.refs_0_.refs_1_, bf16[768,768]{1,0:T(8,128)(2,1)} %get-tuple-element.203.d_ref, ...), custom_call_target="tpu_custom_call" | custom-call | flops 1024 | bytes 1024 | tf_op jit(solution)/shard_map/attend_back/pallas_call | solution.py:457
  577.5 11.0 %entry_back.3 = (f32[768,768]{1,0:T(8,128)}, bf16[768,768]{1,0:T(8,128)(2,1)}) custom-call(f32[768,768]{1,0:T(8,128)} %get-tuple-element.216.sum_ref, bf16[768,768]{1,0:T(8,128)(2,1)} %get-tuple-element.211.dq_ref.refs_0_, bf16[768,768]{1,0:T(8,128)(2,1)} %get-tuple-element.212.refs_0_.refs_1_, bf16[768,768]{1,0:T(8,128)(2,1)} %get-tuple-element.213.refs_1_.refs_2_, ...), custom_call_target="tpu_custom_call" | custom-call | flops 1024 | bytes 1024 | tf_op jit(solution)/shard_map/entry_back/pallas_call | solution.py:768
  595.9 2.7 fusion.101
  603.0 11.8 %attn_grads.3 = (bf16[16,192,768]{2,1,0:T(8,128)(2,1)}, f32[8,768]{1,0:T(8,128)}) custom-call(bf16[768,768]{1,0:T(8,128)(2,1)} %get-tuple-element.152.x_ref.refs_0_, bf16[768,768]{1,0:T(8,128)(2,1)} %copy-done.19, bf16[768,768]{1,0:T(8,128)(2,1)} %get-tuple-element.222.refs_2_, bf16[768,768]{1,0:T(8,128)(2,1)} %get-tuple-element.156.mixed_ref.refs_3_, ...), custom_call_target="tpu_custom_call" | custom-call | flops 1024 | bytes 1024 | tf_op jit(solution)/shard_map/attn_grads/pallas_call | solution.py:810
  614.9 2.0 collective-permute-done.6.refs_0_
  618.0 3.2 multiply_reduce_fusion.1
  625.2 3.4 collective-permute-start.7
  632.5 4.1 collective-permute-done.8
  636.7 2.1 convolution_convert_fusion
  639.3 3.2 copy.171
  642.5 2.4 copy-done.4
  646.3 30.7 %conv_weight_grad.1.refs_1_ = bf16[16,768,384]{2,1,0:T(8,128)(2,1)} custom-call(bf16[176,16,1024]{2,1,0:T(8,128)(2,1)} %bitcast.285, bf16[48,16,1024]{2,1,0:T(8,128)(2,1)} %slice.564.d_ref), custom_call_target="tpu_custom_call" | custom-call | flops 35000000512 | bytes 10000000 | tf_op jit(solution)/shard_map/conv_weight_grad/pallas_call | solution.py:201
  677.1 2.3 broadcast_select_fusion.1
  679.4 2.1 pad_maximum_fusion.refs_3_
  681.5 31.6 %conv_input_grad.1.refs_0_ = f32[48,16,1024]{2,1,0:T(8,128)} custom-call(bf16[176,16,1024]{2,1,0:T(8,128)(2,1)} %get-tuple-element.231.d_ref, bf16[16,928,384]{2,1,0:T(8,128)(2,1)} %bitcast.311), custom_call_target="tpu_custom_call" | custom-call | flops 35000000512 | bytes 10000000 | tf_op jit(solution)/shard_map/conv_input_grad/pallas_call | solution.py:157
  714.3 3.7 copy.154
  718.0 2.1 collective-permute-start.11
  720.7 3.2 fusion.73
  724.0 2.4 convert_reduce_fusion.1
  729.5 3.2 fusion.16.refs_0_
  732.7 3.8 pack_grads.1.refs_0_
  740.3 2.2 stack_reshape.7
  744.4 2.9 convert_add_fusion.2.refs_2_
  747.2 6.9 reduce-scatter.8.cloned.1.call-done
  757.2 122.2 %reduce_chunks.1 = (f32[160,384]{1,0:T(8,128)}, f32[768,384]{1,0:T(8,128)}, bf16[16,2,48,384]{3,2,1,0:T(8,128)(2,1)}) custom-call(bf16[16,160,384]{2,1,0:T(8,128)(2,1)} %get-tuple-element.245.refs_0_, bf16[16,768,384]{2,1,0:T(8,128)(2,1)} %get-tuple-element.246.refs_1_, bf16[16,48,384]{2,1,0:T(8,128)(2,1)} %bitcast.325, ...), custom_call_target="tpu_custom_call" | custom-call | flops 1024 | bytes 1024 | tf_op jit(solution)/shard_map/reduce_chunks/pallas_call | solution.py:1043
  880.6 8.0 finish.1
  892.6 4.2 multiply_subtract_fusion.1
  896.8 2.3 multiply_subtract_fusion
  (383 shorter events, 114.4 us)
Async XLA Ops:
  7.2 4.0 copy-start.43
  7.2 100.3 %all-gather.5.cloned.1.call-start = ((), (), s32[]{:S(2)}) async-start(), calls=%async_computation.4 | async-start | bytes 12115968 | tf_op jit(solution)/shard_map/all_gather | solution.py:1358
  8.6 31.6 %copy-start.17 = (f32[8,48,768]{2,1,0:T(8,128)S(1)}, f32[8,48,768]{2,1,0:T(8,128)}, u32[]{:S(2)}) copy-start(f32[8,48,768]{2,1,0:T(8,128)} %refs_6_.1) | copy-start | bytes 3538948
  11.1 29.1 %copy-start.20 = (f32[2,48,3072]{2,1,0:T(8,128)S(1)}, f32[2,48,3072]{2,1,0:T(8,128)}, u32[]{:S(2)}) copy-start(f32[2,48,3072]{2,1,0:T(8,128)} %param.48) | copy-start | bytes 3538948
  11.2 208.1 %all-gather.7.cloned.1.call-start = ((), (), s32[]{:S(2)}) async-start(), calls=%async_computation.5 | async-start | bytes 15040512 | tf_op jit(solution)/shard_map/all_gather | solution.py:1358
  42.8 252.4 %all-gather.9.cloned.1.call-start = ((), (), s32[]{:S(2)}) async-start(), calls=%async_computation.6 | async-start | bytes 5013504 | tf_op jit(solution)/shard_map/all_gather | solution.py:1358
  42.9 135.1 %copy-start.75 = (pred[768]{0:T(1024)(128)(4,1)}, pred[768]{0:T(1024)(128)(4,1)S(1)}, u32[]{:S(2)}) copy-start(pred[768]{0:T(1024)(128)(4,1)S(1)} %broadcast_in_dim.63) | copy-start | bytes 2308
  42.9 135.1 %copy-start.77 = (pred[768]{0:T(1024)(128)(4,1)}, pred[768]{0:T(1024)(128)(4,1)S(1)}, u32[]{:S(2)}) copy-start(pred[768]{0:T(1024)(128)(4,1)S(1)} %get-tuple-element.400) | copy-start | bytes 2308
  42.9 135.1 %copy-start.79 = (pred[768]{0:T(1024)(128)(4,1)}, pred[768]{0:T(1024)(128)(4,1)S(1)}, u32[]{:S(2)}) copy-start(pred[768]{0:T(1024)(128)(4,1)S(1)} %get-tuple-element.401) | copy-start | bytes 2308
  42.9 135.1 %copy-start.67 = (s32[768]{0:T(1024)}, s32[768]{0:T(1024)S(1)}, u32[]{:S(2)}) copy-start(s32[768]{0:T(1024)S(1)} %get-tuple-element.398) | copy-start | bytes 9220
  42.9 135.1 %copy-start.69 = (s32[768]{0:T(1024)}, s32[768]{0:T(1024)S(1)}, u32[]{:S(2)}) copy-start(s32[768]{0:T(1024)S(1)} %get-tuple-element.399) | copy-start | bytes 9220
  43.0 135.1 %copy-start.71 = (s32[768]{0:T(1024)}, s32[768]{0:T(1024)S(1)}, u32[]{:S(2)}) copy-start(s32[768]{0:T(1024)S(1)} %get-tuple-element.396) | copy-start | bytes 9220
  43.0 135.1 %copy-start.73 = (s32[768]{0:T(1024)}, s32[768]{0:T(1024)S(1)}, u32[]{:S(2)}) copy-start(s32[768]{0:T(1024)S(1)} %get-tuple-element.397) | copy-start | bytes 9220
  44.0 66.0 %copy-start.52 = (f32[2,384]{1,0:T(2,128)}, f32[2,384]{1,0:T(2,128)S(1)}, u32[]{:S(2)}) copy-start(f32[2,384]{1,0:T(2,128)S(1)} %broadcast_multiply_fusion.4) | copy-start | bytes 9220
  44.4 65.9 %copy-start.54 = (f32[2,384]{1,0:T(2,128)}, f32[2,384]{1,0:T(2,128)S(1)}, u32[]{:S(2)}) copy-start(f32[2,384]{1,0:T(2,128)S(1)} %add_rsqrt_fusion.3) | copy-start | bytes 9220
  111.2 7.9 collective-permute-start
  114.6 8.7 collective-permute-start.1
  116.4 65.8 %copy-start.48 = (f32[768]{0:T(1024)}, f32[768]{0:T(1024)S(1)}, u32[]{:S(2)}) copy-start(f32[768]{0:T(1024)S(1)} %get-tuple-element.361) | copy-start | bytes 9220
  184.7 171.6 %all-gather.11.cloned.1.call-start = ((), (), s32[]{:S(2)}) async-start(), calls=%async_computation.7 | async-start | bytes 10027008 | tf_op jit(solution)/shard_map/all_gather | solution.py:1358
  184.7 41.1 %collective-permute-start.2 = (bf16[768,768]{1,0:T(8,128)(2,1)}, bf16[768,768]{1,0:T(8,128)(2,1)S(1)}, u32[]{:S(2)}, u32[]{:S(2)}) collective-permute-start(bf16[768,768]{1,0:T(8,128)(2,1)} %get-tuple-element.152.x_ref.refs_0_), channel_id=1, source_target_pairs={{0,16},{16,0},{1,17},{17,1},{2,18},{18,2},{3,19},{19,3},{4,20},{20... | collective-permute-start | bytes 3538952 | tf_op jit(solution)/shard_map/ppermute | solution.py:1110
  250.4 431.1 %reduce-scatter.4.cloned.1.call-start = ((), (), s32[]{:S(2)}) async-start(), calls=%async_computation.8 | async-start | bytes 10027008 | tf_op jit(solution)/shard_map/reduce_scatter | solution.py:1382
  251.1 3.6 collective-permute-start.4
  256.0 34.3 %copy-start.39 = (pred[1536,320]{1,0:T(32,128)(4,1)}, pred[1536,320]{1,0:T(32,128)(4,1)S(1)}, u32[]{:S(2)}) copy-start(pred[1536,320]{1,0:T(32,128)(4,1)S(1)} %get-tuple-element.404) | copy-start | bytes 1474564
  256.0 34.3 %copy-start.41 = (pred[1536,320]{1,0:T(32,128)(4,1)}, pred[1536,320]{1,0:T(32,128)(4,1)S(1)}, u32[]{:S(2)}) copy-start(pred[1536,320]{1,0:T(32,128)(4,1)S(1)} %get-tuple-element.405) | copy-start | bytes 1474564
  287.8 27.8 %collective-permute-start.3 = (bf16[768,768]{1,0:T(8,128)(2,1)}, bf16[768,768]{1,0:T(8,128)(2,1)}, u32[]{:S(2)}, u32[]{:S(2)}) collective-permute-start(bf16[768,768]{1,0:T(8,128)(2,1)} %get-tuple-element.157.x_ref.refs_0_), channel_id=1, source_target_pairs={{0,16},{16,0},{1,17},{17,1},{2,18},{18,2},{3,19},{19,3},{4,20},{20... | collective-permute-start | bytes 3538952 | tf_op jit(solution)/shard_map/ppermute | solution.py:1110
  415.5 298.8 %reduce-scatter.6.cloned.1.call-start = ((), (), s32[]{:S(2)}) async-start(), calls=%async_computation.9 | async-start | bytes 15040512 | tf_op jit(solution)/shard_map/reduce_scatter | solution.py:1382
  455.1 28.3 %collective-permute-start.5 = (bf16[768,768]{1,0:T(8,128)(2,1)}, bf16[768,768]{1,0:T(8,128)(2,1)S(1)}, u32[]{:S(2)}, u32[]{:S(2)}) collective-permute-start(bf16[768,768]{1,0:T(8,128)(2,1)} %get-tuple-element.192), channel_id=1, source_target_pairs={{0,16},{16,0},{1,17},{17,1},{2,18},{18,2},{3,19},{19,3},{4,20},{20... | collective-permute-start | bytes 3538952 | tf_op jit(solution)/shard_map/ppermute | solution.py:1115
  520.5 4.4 copy-start.55
  520.5 5.0 copy-start.53
  520.5 5.6 copy-start.62
  520.5 6.2 copy-start.63
  520.5 55.7 %all-to-all-start = ((bf16[16,3,48,384]{3,2,1,0:T(8,128)(2,1)}), bf16[16,3,48,384]{3,2,1,0:T(8,128)(2,1)S(1)}, u32[]{:S(2)}, u32[]{:S(2)}) async-start(bf16[16,3,48,384]{3,2,1,0:T(8,128)(2,1)} %bitcast.52), calls=%async_computation | async-start | bytes 3538944 | tf_op jit(solution)/shard_map/all_to_all | solution.py:1386
  524.3 229.8 %reduce-scatter.8.cloned.1.call-start = ((), (), s32[]{:S(2)}) async-start(), calls=%async_computation.10 | async-start | bytes 5013504 | tf_op jit(solution)/shard_map/reduce_scatter | solution.py:1382
  531.6 7.9 copy-start
  541.3 5.8 copy-start.45
  541.3 6.1 copy-start.44
  588.5 6.8 copy-start.57
  588.5 7.4 copy-start.35
  588.5 13.1 %copy-start.7 = (bf16[16,3,48,384]{3,2,1,0:T(8,128)(2,1)S(1)}, bf16[16,3,48,384]{3,2,1,0:T(8,128)(2,1)}, u32[]{:S(2)}) copy-start(bf16[16,3,48,384]{3,2,1,0:T(8,128)(2,1)} %get-tuple-element.234) | copy-start | bytes 5308420
  588.5 28.4 %collective-permute-start.6 = (bf16[768,768]{1,0:T(8,128)(2,1)}, bf16[768,768]{1,0:T(8,128)(2,1)S(1)}, u32[]{:S(2)}, u32[]{:S(2)}) collective-permute-start(bf16[768,768]{1,0:T(8,128)(2,1)} %get-tuple-element.221), channel_id=1, source_target_pairs={{0,16},{16,0},{1,17},{17,1},{2,18},{18,2},{3,19},{19,3},{4,20},{20... | collective-permute-start | bytes 3538952 | tf_op jit(solution)/shard_map/ppermute | solution.py:1115
  603.0 74.1 %collective-permute-start.10 = (bf16[3,768,384]{2,1,0:T(8,128)(2,1)}, bf16[3,768,384]{2,1,0:T(8,128)(2,1)}, u32[]{:S(2)}, u32[]{:S(2)}) collective-permute-start(bf16[3,768,384]{2,1,0:T(8,128)(2,1)} %bitcast.71), channel_id=1, source_target_pairs={{0,1},{1,0},{2,3},{3,2},{4,5},{5,4},{6,7},{7,6},{8,9},{9,8},{10,11... | collective-permute-start | bytes 5308424 | tf_op jit(solution)/shard_map/ppermute | solution.py:1477
  617.9 4.6 copy-start.30
  624.5 12.2 %copy-start.68 = (s32[768]{0:T(1024)S(1)}, s32[768]{0:T(1024)}, u32[]{:S(2)}) copy-start(s32[768]{0:T(1024)} %copy-done.67) | copy-start | bytes 9220
  624.5 12.2 %copy-start.70 = (s32[768]{0:T(1024)S(1)}, s32[768]{0:T(1024)}, u32[]{:S(2)}) copy-start(s32[768]{0:T(1024)} %copy-done.69) | copy-start | bytes 9220
  624.5 12.2 %copy-start.72 = (s32[768]{0:T(1024)S(1)}, s32[768]{0:T(1024)}, u32[]{:S(2)}) copy-start(s32[768]{0:T(1024)} %copy-done.71) | copy-start | bytes 9220
  624.5 12.2 %copy-start.74 = (s32[768]{0:T(1024)S(1)}, s32[768]{0:T(1024)}, u32[]{:S(2)}) copy-start(s32[768]{0:T(1024)} %copy-done.73) | copy-start | bytes 9220
  624.5 12.2 %copy-start.78 = (pred[768]{0:T(1024)(128)(4,1)S(1)}, pred[768]{0:T(1024)(128)(4,1)}, u32[]{:S(2)}) copy-start(pred[768]{0:T(1024)(128)(4,1)} %copy-done.77) | copy-start | bytes 2308
  624.5 12.2 %copy-start.80 = (pred[768]{0:T(1024)(128)(4,1)S(1)}, pred[768]{0:T(1024)(128)(4,1)}, u32[]{:S(2)}) copy-start(pred[768]{0:T(1024)(128)(4,1)} %copy-done.79) | copy-start | bytes 2308
  625.2 7.3 collective-permute-start.7
  628.6 8.0 collective-permute-start.8
  681.5 31.6 %collective-permute-start.9 = (bf16[384,768]{1,0:T(8,128)(2,1)}, bf16[384,768]{1,0:T(8,128)(2,1)S(1)}, u32[]{:S(2)}, u32[]{:S(2)}) collective-permute-start(bf16[384,768]{1,0:T(8,128)(2,1)} %get-tuple-element.232), channel_id=1, source_target_pairs={{0,16},{16,0},{1,17},{17,1},{2,18},{18,2},{3,19},{19,3},{4,20},{20... | collective-permute-start | bytes 1769480 | tf_op jit(solution)/shard_map/ppermute | solution.py:1121
  681.5 31.6 %copy-start.31 = (bf16[384,768]{1,0:T(8,128)(2,1)S(1)}, bf16[384,768]{1,0:T(8,128)(2,1)}, u32[]{:S(2)}) copy-start(bf16[384,768]{1,0:T(8,128)(2,1)} %get-tuple-element.232) | copy-start | bytes 1769476
  718.0 26.3 %collective-permute-start.11 = (bf16[576,768]{1,0:T(8,128)(2,1)}, bf16[576,768]{1,0:T(8,128)(2,1)}, u32[]{:S(2)}, u32[]{:S(2)}) collective-permute-start(bf16[576,768]{1,0:T(8,128)(2,1)} %get-tuple-element.244), channel_id=1, source_target_pairs={{0,16},{16,0},{1,17},{17,1},{2,18},{18,2},{3,19},{19,3},{4,20},{20... | collective-permute-start | bytes 2654216 | tf_op jit(solution)/shard_map/ppermute | solution.py:1121
  723.9 3.7 copy-start.14
  723.9 3.6 copy-start.28
  723.9 3.6 copy-start.59
  732.7 5.5 copy-start.9
  738.2 4.3 copy-start.3
  880.6 12.0 %copy-start.33 = (f32[1,48,3072]{2,1,0:T(8,128)S(1)}, f32[1,48,3072]{2,1,0:T(8,128)}, u32[]{:S(2)}) copy-start(f32[1,48,3072]{2,1,0:T(8,128)} %stack_reshape.7) | copy-start | bytes 1769476
  880.6 12.0 %copy-start.21 = (f32[2,48,3072]{2,1,0:T(8,128)S(1)}, f32[2,48,3072]{2,1,0:T(8,128)}, u32[]{:S(2)}) copy-start(f32[2,48,3072]{2,1,0:T(8,128)} %param.48) | copy-start | bytes 3538948
  892.6 4.2 copy-start.23
  892.6 4.2 copy-start.32
  892.6 4.2 copy-start.37
  892.6 4.2 copy-start.38
  (38 other events, 76.1 us)
Sparse Core Ops, SparseCore 0:
  11.3 96.2 all-gather.4
  110.4 108.8 all-gather.6
  222.1 51.3 all-gather.8
  276.2 79.9 all-gather.10
  415.6 109.4 reduce-scatter.3
  529.7 145.3 reduce-scatter.5
  679.5 74.6 reduce-scatter.7
